TPU v7x, 32 devices: a whole 2x2x4 slice. The times are simulated.
32 devices in a mesh: cores: 8 (over y, x, core), face: 4 (over z).
Axes of the slice: x: 2, y: 2, z: 4, core: 2. Of those that a mesh axis runs over, the one named last changes fastest.
Arguments:
- fields: bfloat16 [2, 16, 16, 128, 256], P(None, 'cores', 'face'), may hold values from -6 to 6
- pore_mask: int32 [16, 16, 128], P('cores', 'face'), may hold values 0 or 1
- conv_kernel: bfloat16 [54, 32], replicated, may hold values from -0.875 to 0.875
- conv_bias: float32 [32], replicated, may hold values from -3 to 3
- read_weight: float32 [32], replicated, may hold values from -1 to 1
- obs_cells: int32 [2048], P(('cores', 'face')), may hold values from 0 to 1023
- obs_values: float32 [2048], P(('cores', 'face')), may hold values from 0 to 1
- obs_sigma: float32 [2048], P(('cores', 'face')), may hold values from 0.3 to 3
Outputs:
- analysis: bfloat16 [3, 16, 16, 128, 256], P(None, 'cores', 'face')
Inputs may be any that keep to these rules, and one draw needn't show every extreme that they name: obs_cells holds the index (z * 4 + x) * 128 + y of a cell in the block of the device that holds the observation.
All inputs are finite; a program needn't handle non-finite values. No bound on the sum of `pore_mask` on one device may be relied on, other than what follows from the above.
Results may differ from a plain program's by a relative error of at most 0.0091.
Values may be sent and summed in bfloat16 or wider, within the bound.
No kernel may reach another device: no remote copies, remote signals or barrier semaphores. Data moves between devices by JAX's collectives and lax.ppermute only.
A program may use at most 64 MiB of HBM per device.

v0:
```python
import math

import jax
import jax.numpy as jnp
from jax import lax
from jax.sharding import PartitionSpec as P


def with_halo(cells, sides, width, closed):
    for axis, dim in sides:
        count = lax.axis_size(axis)
        ends = count if closed else count - 1
        head = lax.slice_in_dim(cells, 0, width, axis=dim)
        tail = lax.slice_in_dim(cells, cells.shape[dim] - width, cells.shape[dim], axis=dim)
        cells = jnp.concatenate(
            [
                lax.ppermute(tail, axis, [(i, (i + 1) % count) for i in range(ends)]),
                cells,
                lax.ppermute(head, axis, [((i + 1) % count, i) for i in range(ends)]),
            ],
            axis=dim,
        )
    return cells


def ensemble_terms(predicted, obs_values, obs_sigma):
    members = predicted.shape[1]
    root_count = math.sqrt(members - 1)
    center = jnp.mean(predicted, axis=1)
    spread = predicted - center[:, None]
    inverse_sigma = 1.0 / obs_sigma
    scaled = spread * (inverse_sigma / root_count)[:, None]
    innovation = (obs_values - center) * inverse_sigma
    gram_part = jnp.einsum("om,on->mn", scaled, scaled, precision=lax.Precision.HIGHEST)
    coeff_part = (
        jnp.einsum("om,o->m", scaled, innovation, precision=lax.Precision.HIGHEST) / root_count
    )
    return (gram_part, coeff_part)


def finish_mixing(gram_sum, coeff_sum):
    members = gram_sum.shape[0]
    identity = jnp.eye(members, dtype=jnp.float32)
    lower_factor = jnp.linalg.cholesky(gram_sum + identity)
    transform = jax.scipy.linalg.solve_triangular(lower_factor, identity, lower=True, trans="T")
    mean_weights = jax.scipy.linalg.cho_solve((lower_factor, True), coeff_sum)
    return (transform + mean_weights[:, None]).astype(jnp.bfloat16)


def padded_fields(fields):
    extended = with_halo(fields, (("cores", 1),), 1, True)
    complete = with_halo(extended, (("face", 2),), 1, False)
    return jnp.pad(complete, ((0, 0), (0, 0), (0, 0), (1, 1), (0, 0)))


def shards(
    fields, pore_mask, conv_kernel, conv_bias, read_weight, obs_cells, obs_values, obs_sigma
):
    plane_list = fields.shape[1]
    column_list = fields.shape[2]
    lanes = fields.shape[3]
    members = fields.shape[4]
    padded = padded_fields(fields)
    mask_float = pore_mask.astype(jnp.float32)
    zero_index = jnp.int32(0)

    def prior_row(current_row):
        plane_index = current_row // column_list
        column_index = current_row % column_list
        window = lax.dynamic_slice(
            padded,
            (zero_index, plane_index, column_index, zero_index, zero_index),
            (2, 3, 3, lanes + 2, members),
        )
        stencil_taps = jnp.stack(
            [window[:, :, :, offset : offset + lanes, :] for offset in range(3)], axis=3
        ).reshape(54, lanes * members)
        hidden = jnp.einsum(
            "kc,kn->cn", conv_kernel, stencil_taps, preferred_element_type=jnp.float32
        )
        hidden = jax.nn.silu(hidden + conv_bias[:, None])
        logits_sat = jnp.einsum("c,cn->n", read_weight, hidden, precision=lax.Precision.HIGHEST)
        row_mask = lax.dynamic_slice(
            mask_float, (plane_index, column_index, zero_index), (1, 1, lanes)
        ).reshape(lanes, 1)
        return (jax.nn.sigmoid(logits_sat).reshape(lanes, members) * row_mask).astype(jnp.bfloat16)

    finished_rows = lax.map(prior_row, jnp.arange(plane_list * column_list, dtype=jnp.int32))
    saturation = finished_rows.reshape(plane_list, column_list, lanes, members)
    predicted = jnp.take(
        finished_rows.reshape(plane_list * column_list * lanes, members), obs_cells, axis=0
    ).astype(jnp.float32)
    gram_part, coeff_part = ensemble_terms(predicted, obs_values, obs_sigma)
    gram_sum, coeff_sum = lax.psum((gram_part, coeff_part), ("cores", "face"))
    mixing = finish_mixing(gram_sum, coeff_sum)
    state = jnp.concatenate([fields, saturation[None]], axis=0)
    state_float = state.astype(jnp.float32)
    state_mean = jnp.mean(state_float, axis=-1, keepdims=True)
    anomalies = (state_float - state_mean).astype(jnp.bfloat16)
    moved = jnp.dot(anomalies.reshape(-1, members), mixing, preferred_element_type=jnp.float32)
    return (state_mean + moved.reshape(state.shape)).astype(jnp.bfloat16)


def solution(mesh):
    return jax.shard_map(
        shards,
        mesh=mesh,
        in_specs=(
            P(None, "cores", "face", None, None),
            P("cores", "face", None),
            P(),
            P(),
            P(),
            P(("cores", "face")),
            P(("cores", "face")),
            P(("cores", "face")),
        ),
        out_specs=P(None, "cores", "face", None, None),
        check_vma=False,
    )
```

profile of v0, /device:TPU:0, one launch (start us, length us, event | category | flops | bytes accessed | tf_op | source)
XLA Modules:
  0.0 370.6 jit_solution(12509376263341740722)
XLA Ops:
  8.4 2.9 collective-permute-start.1
  13.3 7.8 %collective-permute-done = bf16[2,1,4,128,256]{4,3,2,1,0:T(8,128)(2,1)S(1)} collective-permute-done((bf16[2,1,4,128,256]{4,3,2,1,0:T(8,128)(2,1)S(1)}, bf16[2,1,4,128,256]{4,3,2,1,0:T(8,128)(2,1)S(1)}, u32[]{:S(2)}, u32[]{:S(2)}) %collective-permute-start) | collective-permute-done | bytes 524320 | tf_op jit(solution)/shard_map/ppermute | solution.py:17
  22.8 3.6 collective-permute-start.2
  29.6 8.5 %collective-permute-done.2 = bf16[2,4,1,128,256]{4,3,2,1,0:T(8,128)(2,1)S(1)} collective-permute-done((bf16[2,4,1,128,256]{4,3,2,1,0:T(8,128)(2,1)S(1)}, bf16[2,4,1,128,256]{4,3,2,1,0:T(8,128)(2,1)S(1)}, u32[]{:S(2)}, u32[]{:S(2)}) %collective-permute-start.2) | collective-permute-done | bytes 524320 | tf_op jit(solution)/shard_map/ppermute | solution.py:17
  38.1 4.7 %collective-permute-done.3 = bf16[2,4,1,128,256]{4,3,2,1,0:T(8,128)(2,1)S(1)} collective-permute-done((bf16[2,4,1,128,256]{4,3,2,1,0:T(8,128)(2,1)S(1)}, bf16[2,4,1,128,256]{4,3,2,1,0:T(8,128)(2,1)S(1)}, u32[]{:S(2)}, u32[]{:S(2)}) %collective-permute-start.3) | collective-permute-done | bytes 524320 | tf_op jit(solution)/shard_map/ppermute | solution.py:19
  45.0 120.3 %while.13 = (s32[]{:T(128)}, bf16[8,128,256]{2,1,0:T(8,128)(2,1)}, s32[8]{0:T(128)}, bf16[2,4,6,130,256]{4,3,2,1,0:T(8,128)(2,1)S(1)}, bf16[54,32]{0,1:T(8,128)(...) while((s32[]{:T(128)}, bf16[8,128,256]{2,1,0:T(8,128)(2,1)}, ...), condition=%wide.region_1.2_spmd, body=%wide.region_0.1_spmd.sunk | while | flops 134774816 | bytes 48568464 | solution.py:88
  50.9 2.3 copy.20
  53.9 3.8 %fusion.85 = f32[1,32768]{1,0:T(1,128)S(1)} fusion(f32[32,32768]{1,0:T(8,128)S(1)} %fusion.84, f32[32]{0:T(128)} %get-tuple-element.285), kind=kOutput, calls=%fused_computation.3.clone.1 | convolution fusion | flops 16777216 | bytes 4325504 | tf_op jit(solution)/shard_map/while/body/eval_jaxpr/c,cn->n/dot_general | solution.py:82
  65.9 2.3 copy.20
  68.9 3.8 %fusion.85 = f32[1,32768]{1,0:T(1,128)S(1)} fusion(f32[32,32768]{1,0:T(8,128)S(1)} %fusion.84, f32[32]{0:T(128)} %get-tuple-element.285), kind=kOutput, calls=%fused_computation.3.clone.1 | convolution fusion | flops 16777216 | bytes 4325504 | tf_op jit(solution)/shard_map/while/body/eval_jaxpr/c,cn->n/dot_general | solution.py:82
  81.0 2.3 copy.20
  83.9 3.8 %fusion.85 = f32[1,32768]{1,0:T(1,128)S(1)} fusion(f32[32,32768]{1,0:T(8,128)S(1)} %fusion.84, f32[32]{0:T(128)} %get-tuple-element.285), kind=kOutput, calls=%fused_computation.3.clone.1 | convolution fusion | flops 16777216 | bytes 4325504 | tf_op jit(solution)/shard_map/while/body/eval_jaxpr/c,cn->n/dot_general | solution.py:82
  96.0 2.3 copy.20
  99.0 3.8 %fusion.85 = f32[1,32768]{1,0:T(1,128)S(1)} fusion(f32[32,32768]{1,0:T(8,128)S(1)} %fusion.84, f32[32]{0:T(128)} %get-tuple-element.285), kind=kOutput, calls=%fused_computation.3.clone.1 | convolution fusion | flops 16777216 | bytes 4325504 | tf_op jit(solution)/shard_map/while/body/eval_jaxpr/c,cn->n/dot_general | solution.py:82
  111.0 2.3 copy.20
  114.0 3.8 %fusion.85 = f32[1,32768]{1,0:T(1,128)S(1)} fusion(f32[32,32768]{1,0:T(8,128)S(1)} %fusion.84, f32[32]{0:T(128)} %get-tuple-element.285), kind=kOutput, calls=%fused_computation.3.clone.1 | convolution fusion | flops 16777216 | bytes 4325504 | tf_op jit(solution)/shard_map/while/body/eval_jaxpr/c,cn->n/dot_general | solution.py:82
  126.1 2.3 copy.20
  129.1 3.8 %fusion.85 = f32[1,32768]{1,0:T(1,128)S(1)} fusion(f32[32,32768]{1,0:T(8,128)S(1)} %fusion.84, f32[32]{0:T(128)} %get-tuple-element.285), kind=kOutput, calls=%fused_computation.3.clone.1 | convolution fusion | flops 16777216 | bytes 4325504 | tf_op jit(solution)/shard_map/while/body/eval_jaxpr/c,cn->n/dot_general | solution.py:82
  141.1 2.3 copy.20
  144.1 3.8 %fusion.85 = f32[1,32768]{1,0:T(1,128)S(1)} fusion(f32[32,32768]{1,0:T(8,128)S(1)} %fusion.84, f32[32]{0:T(128)} %get-tuple-element.285), kind=kOutput, calls=%fused_computation.3.clone.1 | convolution fusion | flops 16777216 | bytes 4325504 | tf_op jit(solution)/shard_map/while/body/eval_jaxpr/c,cn->n/dot_general | solution.py:82
  156.1 2.3 copy.20
  159.1 3.8 %fusion.85 = f32[1,32768]{1,0:T(1,128)S(1)} fusion(f32[32,32768]{1,0:T(8,128)S(1)} %fusion.84, f32[32]{0:T(128)} %get-tuple-element.285), kind=kOutput, calls=%fused_computation.3.clone.1 | convolution fusion | flops 16777216 | bytes 4325504 | tf_op jit(solution)/shard_map/while/body/eval_jaxpr/c,cn->n/dot_general | solution.py:82
  171.6 40.0 %psum.15 = f32[256]{0:T(256)S(1)} all-reduce(f32[256]{0:T(256)S(1)} %broadcast_multiply_fusion.1), channel_id=1, replica_groups=mesh['cores'=8,'face'=4] {'cores','face'}, use_global_device_ids=true, to_apply=%region_9.10 | all-reduce | flops 256 | bytes 2048 | tf_op jit(solution)/shard_map/psum | solution.py:94
  213.6 81.9 %all-reduce.4.cloned.1.call-done = f32[256,256]{0,1:T(8,128)} async-done(((f32[256,256]{0,1:T(8,128)}), f32[256,256]{0,1:T(8,128)}) %all-reduce.4.cloned.1.call-update) | async-done | bytes 262160 | tf_op jit(solution)/shard_map/psum | solution.py:94
  297.6 11.7 %cholesky.50 = f32[128,128]{1,0:T(8,128)S(1)} custom-call(f32[128,128]{1,0:T(8,128)S(1)} %cholesky.118), custom_call_target="Cholesky" | custom-call | tf_op jit(solution)/shard_map/jit(cholesky)/cholesky | solution.py:44
  309.3 9.8 %custom-call.21 = f32[1,128,128]{1,2,0:T(8,128)S(1)} custom-call(f32[1,128,128]{2,1,0:T(8,128)S(1)} %get-tuple-element.154), custom_call_target="InvertDiagBlocksLowerTriangular" | custom-call | tf_op jit(solution)/shard_map/jit(cholesky)/cholesky | solution.py:44
  319.6 11.7 %cholesky.105 = f32[128,128]{1,0:T(8,128)S(1)} custom-call(f32[128,128]{1,0:T(8,128)S(1)} %convolution_subtract_fusion.1), custom_call_target="Cholesky" | custom-call | tf_op jit(solution)/shard_map/jit(cholesky)/cholesky | solution.py:44
  334.1 5.1 %while.14 = (s32[]{:T(128)}, f32[256,256]{1,0:T(8,128)S(1)}, s32[2,2]{1,0:T(2,128)S(1)}, f32[2,128,128]{2,1,0:T(8,128)}, s32[]{:T(128)}) while((s32[]{:T(128)}, f32[256,256]{1,0:T(8,128)S(1)}, s32[2,2]{1,0:T(2,128)S(1)}, f32[2,128,128]{2,1,0:T(8,128)}, s32[]{:T(128)}) %tuple.53), condition=%wide.while_cond, body=%wide.while_body.sunk | while | flops 2 | bytes 132705 | solution.py:45
  334.7 1.9 bitcast_dynamic-update-slice_fusion.2
  337.2 1.9 bitcast_dynamic-update-slice_fusion.2
  339.1 20.5 %custom-call.22 = f32[2,128,128]{1,2,0:T(8,128)S(1)} custom-call(f32[2,128,128]{2,1,0:T(8,128)} %get-tuple-element.117), custom_call_target="InvertDiagBlocksLowerTriangular" | custom-call | tf_op jit(solution)/shard_map/jit(_solve_triangular)/triangular_solve | solution.py:45
  361.8 2.0 add_convert_fusion
  (152 shorter events, 80.0 us)
Async XLA Ops:
  6.5 14.6 %copy-start = (bf16[2,2,4,128,256]{4,3,2,1,0:T(8,128)(2,1)S(1)}, bf16[2,2,4,128,256]{4,3,2,1,0:T(8,128)(2,1)}, u32[]{:S(2)}) copy-start(bf16[2,2,4,128,256]{4,3,2,1,0:T(8,128)(2,1)} %param.10) | copy-start | bytes 3145732
  6.5 288.9 %all-reduce.4.cloned.1.call-start = ((), (), s32[]{:S(2)}) async-start(), calls=%async_computation | async-start | bytes 524288 | tf_op jit(solution)/shard_map/psum | solution.py:94
  7.9 21.1 %copy-start.6 = (s32[64]{0:T(128)S(1)}, s32[64]{0:T(128)}, u32[]{:S(2)}) copy-start(s32[64]{0:T(128)} %param.15) | copy-start | bytes 772
  7.9 13.2 %collective-permute-start = (bf16[2,1,4,128,256]{4,3,2,1,0:T(8,128)(2,1)S(1)}, bf16[2,1,4,128,256]{4,3,2,1,0:T(8,128)(2,1)S(1)}, u32[]{:S(2)}, u32[]{:S(2)}) collective-permute-start(bf16[2,1,4,128,256]{4,3,2,1,0:T(8,128)(2,1)S(1)} %get-tuple-element.150), channel_id=1, source_target_pairs={{0,4},{4,8},{8,12},{12,16},{16,20},{20,24},{24,28},{28,0},{1,5},{5... | collective-permute-start | bytes 1572872 | tf_op jit(solution)/shard_map/ppermute | solution.py:17
  8.4 14.2 %collective-permute-start.1 = (bf16[2,1,4,128,256]{4,3,2,1,0:T(8,128)(2,1)S(1)}, bf16[2,1,4,128,256]{4,3,2,1,0:T(8,128)(2,1)S(1)}, u32[]{:S(2)}, u32[]{:S(2)}) collective-permute-start(bf16[2,1,4,128,256]{4,3,2,1,0:T(8,128)(2,1)S(1)} %get-tuple-element.149), channel_id=1, source_target_pairs={{4,0},{8,4},{12,8},{16,12},{20,16},{24,20},{28,24},{0,28},{5,1},{9... | collective-permute-start | bytes 1572872 | tf_op jit(solution)/shard_map/ppermute | solution.py:19
  22.8 15.3 %collective-permute-start.2 = (bf16[2,4,1,128,256]{4,3,2,1,0:T(8,128)(2,1)S(1)}, bf16[2,4,1,128,256]{4,3,2,1,0:T(8,128)(2,1)S(1)}, u32[]{:S(2)}, u32[]{:S(2)}) collective-permute-start(bf16[2,4,1,128,256]{4,3,2,1,0:T(8,128)(2,1)S(1)} %get-tuple-element.147), channel_id=1, source_target_pairs={{0,1},{1,2},{2,3},{4,5},{5,6},{6,7},{8,9},{9,10},{10,11},{12,13},{... | collective-permute-start | bytes 1572872 | tf_op jit(solution)/shard_map/ppermute | solution.py:17
  26.4 16.4 %collective-permute-start.3 = (bf16[2,4,1,128,256]{4,3,2,1,0:T(8,128)(2,1)S(1)}, bf16[2,4,1,128,256]{4,3,2,1,0:T(8,128)(2,1)S(1)}, u32[]{:S(2)}, u32[]{:S(2)}) collective-permute-start(bf16[2,4,1,128,256]{4,3,2,1,0:T(8,128)(2,1)S(1)} %get-tuple-element.148), channel_id=1, source_target_pairs={{1,0},{2,1},{3,2},{5,4},{6,5},{7,6},{9,8},{10,9},{11,10},{13,12},{... | collective-permute-start | bytes 1572872 | tf_op jit(solution)/shard_map/ppermute | solution.py:19
  28.3 16.7 %copy-start.4 = (bf16[54,32]{0,1:T(8,128)(2,1)S(1)}, bf16[54,32]{0,1:T(8,128)(2,1)}, u32[]{:S(2)}) copy-start(bf16[54,32]{0,1:T(8,128)(2,1)} %param.12) | copy-start | bytes 10372
  28.3 16.7 %copy-start.5 = (f32[32]{0:T(128)S(1)}, f32[32]{0:T(128)}, u32[]{:S(2)}) copy-start(f32[32]{0:T(128)} %param.13) | copy-start | bytes 388
  165.3 168.7 %copy-start.7 = (s32[2]{0:T(128)S(1)}, s32[2]{0:T(128)}, u32[]{:S(2)}) copy-start(s32[2]{0:T(128)} %iota_multiply_fusion) | copy-start | bytes 28
  211.6 149.5 %copy-start.3 = (f32[256,256]{0,1:T(8,128)S(1)}, f32[256,256]{0,1:T(8,128)}, u32[]{:S(2)}) copy-start(f32[256,256]{0,1:T(8,128)} %fusion.32) | copy-start | bytes 786436
  213.5 148.2 %copy-start.1 = (bf16[2,2,4,128,256]{4,3,2,1,0:T(8,128)(2,1)S(1)}, bf16[2,2,4,128,256]{4,3,2,1,0:T(8,128)(2,1)}, u32[]{:S(2)}) copy-start(bf16[2,2,4,128,256]{4,3,2,1,0:T(8,128)(2,1)} %param.10) | copy-start | bytes 3145732
  213.5 148.2 %copy-start.2 = (bf16[8,128,256]{2,1,0:T(8,128)(2,1)S(1)}, bf16[8,128,256]{2,1,0:T(8,128)(2,1)}, u32[]{:S(2)}) copy-start(bf16[8,128,256]{2,1,0:T(8,128)(2,1)} %get-tuple-element.109) | copy-start | bytes 1572868
Sparse Core Ops, SparseCore 0:
  170.8 124.6 all-reduce.3
where the time goes:
time: 372 us; the launch traced here: 371 us
  waiting for transfers between devices  104 us (28%)
  other arithmetic  80.9 us (22%)
  local copies, waits for them, and re-layouts  60.7 us (16%)
  matrix products  43 us (12%)
  blocking collectives  40 us (11%)
  loops' own time  18.4 us (5%)
  between operations  14.9 us (4%)
  starting transfers between devices  8.38 us (2%)
    psum x1, waiting for transfers between devices, shards(): gram_sum, coeff_sum = lax.psum((gram_part, coeff_part), ('cores', 'face'))  81.9 us
    psum x1, blocking collectives, shards(): gram_sum, coeff_sum = lax.psum((gram_part, coeff_part), ('cores', 'face'))  40 us
    another operation x7, other arithmetic, finish_mixing(): lower_factor = jnp.linalg.cholesky(gram_sum + identity)  34.6 us
    dot_general x8, matrix products, prior_row(): jnp.einsum('c,cn->n', read_weight, hidden, precision=lax.Precision.HIGHEST)  30.1 us
    while x16, local copies, waits for them, and re-layouts  22.4 us
    another operation x3, other arithmetic, finish_mixing(): jax.scipy.linalg.solve_triangular(lower_factor, identity, lower=True, tra...  21.1 us
    another operation x1, loops' own time, shards(): lax.map(prior_row, jnp.arange(plane_list * column_list, dtype=jnp.int32))  18.4 us
    ppermute x2, waiting for transfers between devices, with_halo(): lax.ppermute(tail, axis, [(i, (i + 1) % count) for i in range(ends)])  16.3 us
  transfers between devices with their start and end apart: 5, of which 5 were waited for; matrix products, arithmetic and copies ran while one was open for 2% of the time, Pallas kernels for 0%

commit v1 on v0

v1 whole, which is shorter than its diff:
```python
import functools
import math

import jax
import jax.numpy as jnp
import numpy as np
from jax import lax
from jax.experimental import pallas as pl
from jax.experimental.pallas import tpu as pltpu
from jax.sharding import PartitionSpec as P

HIGHEST = lax.Precision.HIGHEST
PAY_ROWS = 16
GATHER_DEVICES = 64
BLOCK = 64
VMEM_BYTES = 48 * 1024 * 1024


def plane_places(planes, columns):
    own = [(f, z + 1, x + 1) for f in range(2) for z in range(planes) for x in range(columns)]
    low = [(f, 0, x + 1) for f in range(2) for x in range(columns)]
    high = [(f, planes + 1, x + 1) for f in range(2) for x in range(columns)]
    left = [(f, z + 1, 0) for f in range(2) for z in range(planes)]
    right = [(f, z + 1, columns + 1) for f in range(2) for z in range(planes)]
    corner_left = [(f, z, 0) for f in range(2) for z in (0, planes + 1)]
    corner_right = [(f, z, columns + 1) for f in range(2) for z in (0, planes + 1)]
    return own + low + high + left + right + corner_left + corner_right


def tap_selector(planes, columns):
    places = plane_places(planes, columns)
    chosen = np.zeros((54, planes * columns, 3 * len(places)), np.float32)
    for z in range(planes):
        for x in range(columns):
            for n, (f, zz, xx) in enumerate(places):
                a, b = zz - z, xx - x
                if 0 <= a <= 2 and 0 <= b <= 2:
                    for c in range(3):
                        chosen[27 * f + 9 * a + 3 * b + c, z * columns + x, c * len(places) + n] = 1.0
    return chosen


def swap_matrix(outer, inner):
    matrix = np.zeros((outer * inner, outer * inner), np.float32)
    for i in range(outer):
        for j in range(inner):
            matrix[j * outer + i, i * inner + j] = 1.0
    return matrix


def three_pieces(value):
    first = lax.reduce_precision(value, 8, 7)
    second = lax.reduce_precision(value - first, 8, 7)
    third = lax.reduce_precision(value - first - second, 8, 7)
    return first, second, third


def surrogate_kernel(
    own, low, high, left, right, corner_left, corner_right, weights, swap_in, swap_out, mask,
    sigma, values, read_half, cells, sat_out, pay_out, packed, sat_rows, sat_float, pred
):
    lanes, members = own.shape[1], own.shape[2]
    count = packed.shape[1]
    rows = mask.shape[0]
    channels = read_half.shape[0]
    packed[0] = jnp.zeros((count, members), jnp.bfloat16)
    packed[lanes + 1] = jnp.zeros((count, members), jnp.bfloat16)

    def pack(step, carry):
        at = pl.multiple_of(step * 16, 16)
        groups = ((own,), (low, high), (left, right, corner_left, corner_right))
        for g, refs in enumerate(groups):
            parts = [ref[:, pl.ds(at, 16), :] for ref in refs]
            block = parts[0] if len(parts) == 1 else jnp.concatenate(parts, axis=0)
            moved = jnp.dot(
                swap_in[...], block.reshape(256, members), preferred_element_type=jnp.float32
            )
            packed[pl.ds(at + 1, 16), 16 * g : 16 * g + 16, :] = (
                moved.astype(jnp.bfloat16).reshape(16, 16, members)
            )
        return carry

    lax.fori_loop(0, lanes // 16, pack, 0)

    row_index = lax.broadcasted_iota(jnp.int32, (16, members), 0)
    ones = jnp.where(row_index < 3, 1.0, 0.0).astype(jnp.bfloat16)
    lane_index = lax.broadcasted_iota(jnp.int32, (rows, lanes), 1)

    def two_rows(step, carry):
        found = []
        for k in range(2):
            y = step * 2 + k
            taps = jnp.concatenate(
                [packed[pl.ds(y, 3)].reshape(3 * count, members), ones], axis=0
            )
            half = jnp.dot(weights[...], taps, preferred_element_type=jnp.float32)
            total = jnp.zeros((rows, members), jnp.float32)
            for c in range(channels):
                part = half[rows * c : rows * c + rows]
                total = total + read_half[c] * (part * (1.0 + jnp.tanh(part)))
            here = jnp.sum(jnp.where(lane_index == y, mask[...], 0.0), axis=1, keepdims=True)
            found.append(here * (0.5 + 0.5 * jnp.tanh(total)))
        both = jnp.concatenate(found, axis=0).astype(jnp.bfloat16)
        at = pl.multiple_of(step * 2 * rows, 2 * rows)
        sat_rows[pl.ds(at, 2 * rows), :] = both
        sat_float[pl.ds(at, 2 * rows), :] = both.astype(jnp.float32)
        return carry

    lax.fori_loop(0, lanes // 2, two_rows, 0)

    span = 256 // rows
    for b in range(lanes // span):
        moved = jnp.dot(
            swap_out[...], sat_rows[256 * b : 256 * b + 256, :], preferred_element_type=jnp.float32
        )
        sat_out[:, span * b : span * b + span, :] = moved.astype(jnp.bfloat16).reshape(
            rows, span, members
        )

    for o in range(cells.shape[0]):
        cell = cells[o]
        row = (cell % lanes) * rows + cell // lanes
        pred[o : o + 1, :] = sat_float[pl.ds(row, 1), :]

    root_count = math.sqrt(members - 1)
    predicted = pred[...]
    center = jnp.mean(predicted, axis=1, keepdims=True)
    inverse_sigma = 1.0 / sigma[...]
    scaled = (predicted - center) * (inverse_sigma / root_count)
    innovation = (values[...] - center) * inverse_sigma
    coeff = jnp.sum(scaled * innovation, axis=0, keepdims=True) / root_count
    first = coeff.astype(jnp.bfloat16).astype(jnp.float32)
    second = (coeff - first).astype(jnp.bfloat16).astype(jnp.float32)
    third = coeff - first - second
    index = lax.broadcasted_iota(jnp.int32, (PAY_ROWS, members), 0)
    tail = jnp.where(index == 0, first, jnp.where(index == 1, second, jnp.where(index == 2, third, 0.0)))
    observed = cells.shape[0]
    pay_out[0:observed, :] = scaled.astype(jnp.bfloat16)
    pay_out[observed : observed + PAY_ROWS, :] = tail.astype(jnp.bfloat16)


def transposed_dot(a, b, precision):
    return lax.dot_general(
        a, b, (((0,), (0,)), ((), ())), preferred_element_type=jnp.float32, precision=precision
    )


def inverse_factor_block(block):
    lane = lax.broadcasted_iota(jnp.int32, (8, 2 * BLOCK), 1)
    sub = lax.broadcasted_iota(jnp.int32, (8, 2 * BLOCK), 0)
    parts = []
    for i in range(BLOCK // 8):
        unit = jnp.where(lane == sub + (BLOCK + 8 * i), 1.0, 0.0)
        known = jnp.concatenate(
            [block[8 * i : 8 * i + 8, :], jnp.zeros((8, BLOCK), jnp.float32)], axis=1
        )
        parts.append(known + unit)
    pivots = [jnp.ones((8, 2 * BLOCK), jnp.float32) for _ in parts]
    for j in range(BLOCK):
        top, inner = j // 8, j % 8
        row = jnp.broadcast_to(parts[top][inner : inner + 1, :], (8, 2 * BLOCK))
        pivot = jnp.broadcast_to(row[:, j : j + 1], (8, 2 * BLOCK))
        pivots[top] = jnp.where(sub == inner, pivot, pivots[top])
        row = row * (1.0 / pivot)
        for i in range(top, BLOCK // 8):
            column = jnp.broadcast_to(parts[i][:, j : j + 1], (8, 2 * BLOCK))
            if i == top:
                column = jnp.where(sub > inner, column, 0.0)
            parts[i] = parts[i] - column * row
    return jnp.concatenate(
        [(part * lax.rsqrt(pivot))[:, BLOCK:] for part, pivot in zip(parts, pivots)], axis=0
    )


def update_kernel(gathered, *refs):
    if gathered:
        pay, fields, sat, out, joint, mixing = refs
    else:
        gram, coeff_in, fields, sat, out, joint, mixing = refs
    members = fields.shape[1]
    sub = lax.broadcasted_iota(jnp.int32, (members, members), 0)
    lane = lax.broadcasted_iota(jnp.int32, (members, members), 1)
    identity = jnp.where(sub == lane, 1.0, 0.0)
    if gathered:
        devices, observed = pay.shape[0], pay.shape[1] - PAY_ROWS
        group = max(1, 256 // observed)
        total = identity
        for d in range(0, devices, group):
            block = pay[d : d + group, 0:observed, :].reshape(-1, members)
            total = total + transposed_dot(block, block, None)
        coeff = jnp.zeros((PAY_ROWS, members), jnp.float32)
        for d in range(devices):
            coeff = coeff + pay[d, observed:, :].astype(jnp.float32)
        coeff = jnp.sum(coeff, axis=0, keepdims=True)
    else:
        total = identity + gram[...]
        coeff = coeff_in[...]
    joint[:, 0:members] = total
    joint[:, members:] = identity
    for k in range(members // BLOCK):
        at = k * BLOCK
        inverse = inverse_factor_block(joint[at : at + BLOCK, at : at + BLOCK])
        rows = jnp.dot(
            inverse, joint[at : at + BLOCK, :], precision=HIGHEST, preferred_element_type=jnp.float32
        )
        joint[at : at + BLOCK, :] = rows
        if at + BLOCK < members:
            joint[at + BLOCK :, :] = joint[at + BLOCK :, :] - transposed_dot(
                rows[:, at + BLOCK : members], rows, HIGHEST
            )
    inverse = joint[:, members:]
    wide = jnp.broadcast_to(coeff, (8, members))
    half = lax.dot_general(
        wide, inverse, (((1,), (1,)), ((), ())), preferred_element_type=jnp.float32, precision=HIGHEST
    )
    weight = jnp.dot(half, inverse, preferred_element_type=jnp.float32, precision=HIGHEST)
    mixing[...] = jnp.transpose(inverse + weight[0:1, :]).astype(jnp.bfloat16)

    def blend(source, target, base):
        span = 256

        def step(s, carry):
            at = pl.multiple_of(s * span, span)
            state = source[pl.ds(at, span), :].astype(jnp.float32)
            mean = jnp.mean(state, axis=1, keepdims=True)
            anomalies = (state - mean).astype(jnp.bfloat16)
            moved = jnp.dot(anomalies, mixing[...], preferred_element_type=jnp.float32)
            target[pl.ds(base + at, span), :] = (mean + moved).astype(jnp.bfloat16)
            return carry

        lax.fori_loop(0, source.shape[0] // span, step, 0)

    blend(fields, out, 0)
    blend(sat, out, fields.shape[0])


def shift(value, axis, by, closed):
    count = lax.axis_size(axis)
    if by > 0:
        pairs = [(i, (i + 1) % count) for i in range(count if closed else count - 1)]
    else:
        pairs = [((i + 1) % count, i) for i in range(count if closed else count - 1)]
    return lax.ppermute(value, axis, pairs)


def gather_rows(block, steps):
    for axis, bit in steps:
        count = lax.axis_size(axis)
        other = lax.ppermute(block, axis, [(i, i ^ bit) for i in range(count)])
        block = jnp.concatenate([block, other], axis=0)
    return block


def bits_of(axis, count):
    bits = []
    while (1 << len(bits)) < count:
        bits.append((axis, 1 << len(bits)))
    return bits


def vmem():
    return pl.BlockSpec(memory_space=pltpu.VMEM)


def smem():
    return pl.BlockSpec(memory_space=pltpu.SMEM)


def shards(
    fields, pore_mask, conv_kernel, conv_bias, read_weight, obs_cells, obs_values, obs_sigma
):
    _, planes, columns, lanes, members = fields.shape
    channels = conv_kernel.shape[1]
    rows = planes * columns
    observed = obs_cells.shape[0]

    low = shift(fields[:, -1:], "cores", 1, True)
    high = shift(fields[:, :1], "cores", -1, True)
    left = shift(fields[:, :, -1:], "face", 1, False)
    right = shift(fields[:, :, :1], "face", -1, False)
    corner_left = shift(
        jnp.concatenate([low[:, :, -1:], high[:, :, -1:]], axis=1), "face", 1, False
    )
    corner_right = shift(
        jnp.concatenate([low[:, :, :1], high[:, :, :1]], axis=1), "face", -1, False
    )

    selector = tap_selector(planes, columns)
    count = selector.shape[2] // 3
    taps = jnp.dot(
        jnp.transpose(conv_kernel),
        jnp.asarray(selector.reshape(54, -1), jnp.bfloat16),
        preferred_element_type=jnp.float32,
    ).reshape(channels, rows, 3 * count)
    bias = jnp.stack(three_pieces(0.5 * conv_bias), axis=1)
    bias = jnp.broadcast_to(bias[:, None, :], (channels, rows, 3))
    weights = (
        jnp.concatenate(
            [0.5 * taps, bias, jnp.zeros((channels, rows, 13), jnp.float32)], axis=2
        )
        .reshape(channels * rows, 3 * count + 16)
        .astype(jnp.bfloat16)
    )
    flat = lambda a: a.reshape(-1, lanes, members)
    sat, pay = pl.pallas_call(
        surrogate_kernel,
        out_shape=(
            jax.ShapeDtypeStruct((rows, lanes, members), jnp.bfloat16),
            jax.ShapeDtypeStruct((observed + PAY_ROWS, members), jnp.bfloat16),
        ),
        in_specs=[vmem()] * 13 + [smem()] * 2,
        out_specs=(vmem(), vmem()),
        scratch_shapes=[
            pltpu.VMEM((lanes + 2, count, members), jnp.bfloat16),
            pltpu.VMEM((rows * lanes, members), jnp.bfloat16),
            pltpu.VMEM((rows * lanes, members), jnp.float32),
            pltpu.VMEM((observed, members), jnp.float32),
        ],
        compiler_params=pltpu.CompilerParams(vmem_limit_bytes=VMEM_BYTES),
        name="surrogate",
    )(
        flat(fields), flat(low), flat(high), flat(left), flat(right), flat(corner_left),
        flat(corner_right), weights,
        jnp.asarray(swap_matrix(16, 16), jnp.bfloat16),
        jnp.asarray(swap_matrix(256 // rows, rows), jnp.bfloat16),
        pore_mask.reshape(rows, lanes).astype(jnp.float32),
        obs_sigma.reshape(observed, 1), obs_values.reshape(observed, 1),
        0.5 * read_weight, obs_cells,
    )

    core_count, face_count = lax.axis_size("cores"), lax.axis_size("face")
    devices = core_count * face_count
    gathered = devices <= GATHER_DEVICES and devices & (devices - 1) == 0
    if gathered:
        steps = bits_of("face", face_count)[::-1] + bits_of("cores", core_count)[1:]
        steps = steps + bits_of("cores", core_count)[:1]
        terms = (gather_rows(pay[None], steps),)
    else:
        part = pay[:observed]
        gram = lax.dot_general(
            part, part, (((0,), (0,)), ((), ())), preferred_element_type=jnp.float32
        )
        coeff = jnp.sum(pay[observed:].astype(jnp.float32), axis=0, keepdims=True)
        terms = lax.psum((gram, coeff), ("cores", "face"))
    out = pl.pallas_call(
        functools.partial(update_kernel, gathered),
        out_shape=jax.ShapeDtypeStruct((3 * rows * lanes, members), jnp.bfloat16),
        in_specs=[vmem()] * (len(terms) + 2),
        out_specs=vmem(),
        scratch_shapes=[
            pltpu.VMEM((members, 2 * members), jnp.float32),
            pltpu.VMEM((members, members), jnp.bfloat16),
        ],
        compiler_params=pltpu.CompilerParams(vmem_limit_bytes=VMEM_BYTES),
        name="update",
    )(*terms, fields.reshape(-1, members), sat.reshape(-1, members))
    return out.reshape(3, planes, columns, lanes, members)


def solution(mesh):
    return jax.shard_map(
        shards,
        mesh=mesh,
        in_specs=(
            P(None, "cores", "face", None, None),
            P("cores", "face", None),
            P(),
            P(),
            P(),
            P(("cores", "face")),
            P(("cores", "face")),
            P(("cores", "face")),
        ),
        out_specs=P(None, "cores", "face", None, None),
        check_vma=False,
    )
```

time: 372 us -> 120 us (0.32)
  other arithmetic: 80.9 us -> 2.59 us
  waiting for transfers between devices: 104 us -> 26.7 us
  Pallas kernels: 0 us -> 62.9 us
  local copies, waits for them, and re-layouts: 60.7 us -> 5.12 us
  matrix products: 43 us -> 0.15 us
  blocking collectives: 40 us -> 0 us
  loops' own time: 18.4 us -> 0 us
  between operations: 14.9 us -> 0.21 us
  starting transfers between devices: 8.38 us -> 22.4 us
    psum x1 -> x0, waiting for transfers between devices: 81.9 us -> none  [shards(): gram_sum, coeff_sum = lax.psum((gram_part, coeff_part), ('cores', 'face'))]
    pallas_call x0 -> x2, Pallas kernels: none -> 62.9 us  [the longest x1 41.4 us: shards(): pl.pallas_call(functools.partial(update_kernel, gathered), out_shape=jax....]
    another operation x19 -> x2, other arithmetic: 59.2 us -> 0.02 us  [the longest x7 34.6 us: finish_mixing(): lower_factor = jnp.linalg.cholesky(gram_sum + identity)]
    dot_general x19 -> x1, matrix products: 40.4 us -> 0.15 us  [shards(): jnp.dot(jnp.transpose(conv_kernel), jnp.asarray(selector.reshape(54, -1),...]
    psum x1 -> x0, blocking collectives: 40 us -> none  [shards(): gram_sum, coeff_sum = lax.psum((gram_part, coeff_part), ('cores', 'face'))]
    while x16 -> x0, local copies, waits for them, and re-layouts: 22.4 us -> none
    another operation x2 -> x0, loops' own time: 18.4 us -> none  [the longest x1 18.4 us: shards(): lax.map(prior_row, jnp.arange(plane_list * column_list, dtype=jnp.int32))]
    another operation x25 -> x1, local copies, waits for them, and re-layouts: 17.3 us -> 0.1 us  [the longest x16 12.1 us: prior_row(): jnp.stack([window[:, :, :, offset:offset + lanes, :] for offset in range(...]
  transfers between devices with their start and end apart: 5 -> 11, of which waited for: 5 -> 8; matrix products, arithmetic and copies ran while one was open for 2% -> 5% of each run, Pallas kernels for 0% -> 0%
where the time goes in v1:
time: 120 us
  Pallas kernels  62.9 us (52%)
  waiting for transfers between devices  26.7 us (22%)
  starting transfers between devices  22.4 us (19%)
  local copies, waits for them, and re-layouts  5.12 us (4%)
  other arithmetic  2.59 us (2%)
    pallas_call x1, Pallas kernels, shards(): pl.pallas_call(functools.partial(update_kernel, gathered), out_shape=jax....  41.4 us
    pallas_call x1, Pallas kernels, shards(): pl.pallas_call(surrogate_kernel, out_shape=(jax.ShapeDtypeStruct((rows, l...  21.4 us
    ppermute x5, waiting for transfers between devices, gather_rows(): other = lax.ppermute(block, axis, [(i, i ^ bit) for i in range(count)])  15.6 us
    ppermute x6, starting transfers between devices, shift(): return lax.ppermute(value, axis, pairs)  13.8 us
    ppermute x6, waiting for transfers between devices, shift(): return lax.ppermute(value, axis, pairs)  11 us
    ppermute x5, starting transfers between devices, gather_rows(): other = lax.ppermute(block, axis, [(i, i ^ bit) for i in range(count)])  8.67 us
  transfers between devices with their start and end apart: 11, of which 8 were waited for; matrix products, arithmetic and copies ran while one was open for 5% of the time, Pallas kernels for 0%

profile of v1, /device:TPU:0, one launch (start us, length us, event | category | flops | bytes accessed | tf_op | source)
XLA Modules:
  0.0 120.1 jit_solution(3355222717769654706)
XLA Ops:
  0.0 2.2 %fusion.5 = (bf16[2,1,4,128,256]{4,3,2,1,0:T(8,128)(2,1)}, bf16[2,1,4,128,256]{4,3,2,1,0:T(8,128)(2,1)S(1)}) fusion(bf16[2,2,4,128,256]{4,3,2,1,0:T(8,128)(2,1)} %param.11), kind=kLoop, calls=%fused_computation.30 | loop fusion | bytes 2097152 | tf_op jit(solution)/shard_map/slice | solution.py:278
  2.2 0.5 collective-permute-start
  2.7 2.9 %collective-permute-start.1 = (bf16[2,1,4,128,256]{4,3,2,1,0:T(8,128)(2,1)}, bf16[2,1,4,128,256]{4,3,2,1,0:T(8,128)(2,1)S(1)}, u32[]{:S(2)}, u32[]{:S(2)}) collective-permute-start(bf16[2,1,4,128,256]{4,3,2,1,0:T(8,128)(2,1)} %get-tuple-element.11), channel_id=1, source_target_pairs={{4,0},{8,4},{12,8},{16,12},{20,16},{24,20},{28,24},{0,28},{5,1},{9... | collective-permute-start | bytes 1572872 | tf_op jit(solution)/shard_map/ppermute | solution.py:243
  5.5 0.8 fusion.4
  6.4 4.4 %collective-permute-start.2 = (bf16[2,2,1,128,256]{4,3,2,1,0:T(8,128)(2,1)}, bf16[2,2,1,128,256]{4,3,2,1,0:T(8,128)(2,1)S(1)}, u32[]{:S(2)}, u32[]{:S(2)}) collective-permute-start(bf16[2,2,1,128,256]{4,3,2,1,0:T(8,128)(2,1)} %get-tuple-element.10), channel_id=1, source_target_pairs={{0,1},{1,2},{2,3},{4,5},{5,6},{6,7},{8,9},{9,10},{10,11},{12,13},{... | collective-permute-start | bytes 786440 | tf_op jit(solution)/shard_map/ppermute | solution.py:243
  10.8 1.3 %collective-permute-start.3 = (bf16[2,2,1,128,256]{4,3,2,1,0:T(8,128)(2,1)}, bf16[2,2,1,128,256]{4,3,2,1,0:T(8,128)(2,1)S(1)}, u32[]{:S(2)}, u32[]{:S(2)}) collective-permute-start(bf16[2,2,1,128,256]{4,3,2,1,0:T(8,128)(2,1)} %get-tuple-element.9), channel_id=1, source_target_pairs={{1,0},{2,1},{3,2},{5,4},{6,5},{7,6},{9,8},{10,9},{11,10},{13,12},{... | collective-permute-start | bytes 786440 | tf_op jit(solution)/shard_map/ppermute | solution.py:243
  12.1 0.1 copy.15
  12.2 0.6 broadcast_bitcast_fusion
  12.9 0.1 fusion.1
  13.0 3.9 %collective-permute-done.1 = bf16[2,1,4,128,256]{4,3,2,1,0:T(8,128)(2,1)S(1)} collective-permute-done((bf16[2,1,4,128,256]{4,3,2,1,0:T(8,128)(2,1)}, bf16[2,1,4,128,256]{4,3,2,1,0:T(8,128)(2,1)S(1)}, u32[]{:S(2)}, u32[]{:S(2)}) %collective-permute-start.1) | collective-permute-done | bytes 524320 | tf_op jit(solution)/shard_map/ppermute | solution.py:243
  17.0 0.7 pad_maximum_fusion.1
  17.8 3.5 %collective-permute-start.4 = (bf16[2,2,1,128,256]{4,3,2,1,0:T(8,128)(2,1)}, bf16[2,2,1,128,256]{4,3,2,1,0:T(8,128)(2,1)S(1)}, u32[]{:S(2)}, u32[]{:S(2)}) collective-permute-start(bf16[2,2,1,128,256]{4,3,2,1,0:T(8,128)(2,1)} %pad_maximum_fusion.1), channel_id=1, source_target_pairs={{0,1},{1,2},{2,3},{4,5},{5,6},{6,7},{8,9},{9,10},{10,11},{12,13},{... | collective-permute-start | bytes 786440 | tf_op jit(solution)/shard_map/ppermute | solution.py:243
  21.3 0.7 pad_maximum_fusion.2
  22.0 1.3 %collective-permute-start.5 = (bf16[2,2,1,128,256]{4,3,2,1,0:T(8,128)(2,1)}, bf16[2,2,1,128,256]{4,3,2,1,0:T(8,128)(2,1)S(1)}, u32[]{:S(2)}, u32[]{:S(2)}) collective-permute-start(bf16[2,2,1,128,256]{4,3,2,1,0:T(8,128)(2,1)} %pad_maximum_fusion.2), channel_id=1, source_target_pairs={{1,0},{2,1},{3,2},{5,4},{6,5},{7,6},{9,8},{10,9},{11,10},{13,12},{... | collective-permute-start | bytes 786440 | tf_op jit(solution)/shard_map/ppermute | solution.py:243
  23.3 0.9 mul.18
  24.2 0.1 copy.16.sigma
  24.3 0.1 copy.17.values
  24.4 0.1 pad.11.clone
  24.5 1.0 maximum_maximum_fusion.weights
  25.5 1.7 %collective-permute-done.4 = bf16[2,2,1,128,256]{4,3,2,1,0:T(8,128)(2,1)S(1)} collective-permute-done((bf16[2,2,1,128,256]{4,3,2,1,0:T(8,128)(2,1)}, bf16[2,2,1,128,256]{4,3,2,1,0:T(8,128)(2,1)S(1)}, u32[]{:S(2)}, u32[]{:S(2)}) %collective-permute-start.4) | collective-permute-done | bytes 262176 | tf_op jit(solution)/shard_map/ppermute | solution.py:243
  27.3 5.3 %collective-permute-done.5 = bf16[2,2,1,128,256]{4,3,2,1,0:T(8,128)(2,1)S(1)} collective-permute-done((bf16[2,2,1,128,256]{4,3,2,1,0:T(8,128)(2,1)}, bf16[2,2,1,128,256]{4,3,2,1,0:T(8,128)(2,1)S(1)}, u32[]{:S(2)}, u32[]{:S(2)}) %collective-permute-start.5) | collective-permute-done | bytes 262176 | tf_op jit(solution)/shard_map/ppermute | solution.py:243
  32.6 21.4 %surrogate.1 = (bf16[8,128,256]{2,1,0:T(8,128)(2,1)S(1)}, bf16[80,256]{1,0:T(8,128)(2,1)S(1)}) custom-call(bf16[16,128,256]{2,1,0:T(8,128)(2,1)S(1)} %bitcast.28, bf16[8,128,256]{2,1,0:T(8,128)(2,1)S(1)} %bitcast.30, bf16[8,128,256]{2,1,0:T(8,128)(2,1)S(1)} %bitcast.31, bf16[4,128,256]{2,1,0:T(8,128)(2,1)S(1)} %bitcast.37, ...), custom_call_target="tpu_custom_call" | custom-call | tf_op jit(solution)/shard_map/surrogate/pallas_call | solution.py:305
  54.1 3.0 %collective-permute-start.6 = (bf16[1,80,256]{2,1,0:T(8,128)(2,1)S(1)}, bf16[1,80,256]{2,1,0:T(8,128)(2,1)S(1)}, u32[]{:S(2)}, u32[]{:S(2)}) collective-permute-start(bf16[1,80,256]{2,1,0:T(8,128)(2,1)S(1)} %bitcast.32), channel_id=1, source_target_pairs={{0,2},{1,3},{2,0},{3,1},{4,6},{5,7},{6,4},{7,5},{8,10},{9,11},{10,... | collective-permute-start | bytes 122888 | tf_op jit(solution)/shard_map/ppermute | solution.py:249
  57.0 2.0 %collective-permute-done.6 = bf16[1,80,256]{2,1,0:T(8,128)(2,1)S(1)} collective-permute-done((bf16[1,80,256]{2,1,0:T(8,128)(2,1)S(1)}, bf16[1,80,256]{2,1,0:T(8,128)(2,1)S(1)}, u32[]{:S(2)}, u32[]{:S(2)}) %collective-permute-start.6) | collective-permute-done | bytes 40992 | tf_op jit(solution)/shard_map/ppermute | solution.py:249
  59.0 1.6 %collective-permute-start.7 = (bf16[2,80,256]{2,1,0:T(8,128)(2,1)S(1)}, bf16[2,80,256]{2,1,0:T(8,128)(2,1)S(1)}, u32[]{:S(2)}, u32[]{:S(2)}) collective-permute-start(bf16[2,80,256]{2,1,0:T(8,128)(2,1)S(1)} %pad_maximum_fusion.4), channel_id=1, source_target_pairs={{0,1},{1,0},{2,3},{3,2},{4,5},{5,4},{6,7},{7,6},{8,9},{9,8},{10,11... | collective-permute-start | bytes 245768 | tf_op jit(solution)/shard_map/ppermute | solution.py:249
  60.7 2.9 %collective-permute-done.7 = bf16[2,80,256]{2,1,0:T(8,128)(2,1)S(1)} collective-permute-done((bf16[2,80,256]{2,1,0:T(8,128)(2,1)S(1)}, bf16[2,80,256]{2,1,0:T(8,128)(2,1)S(1)}, u32[]{:S(2)}, u32[]{:S(2)}) %collective-permute-start.7) | collective-permute-done | bytes 81952 | tf_op jit(solution)/shard_map/ppermute | solution.py:249
  63.6 2.3 %collective-permute-start.8 = (bf16[4,80,256]{2,1,0:T(8,128)(2,1)S(1)}, bf16[4,80,256]{2,1,0:T(8,128)(2,1)S(1)}, u32[]{:S(2)}, u32[]{:S(2)}) collective-permute-start(bf16[4,80,256]{2,1,0:T(8,128)(2,1)S(1)} %pad_maximum_fusion.3), channel_id=1, source_target_pairs={{0,8},{4,12},{8,0},{12,4},{16,24},{20,28},{24,16},{28,20},{1,9},{5... | collective-permute-start | bytes 491528 | tf_op jit(solution)/shard_map/ppermute | solution.py:249
  65.9 3.3 %collective-permute-done.8 = bf16[4,80,256]{2,1,0:T(8,128)(2,1)S(1)} collective-permute-done((bf16[4,80,256]{2,1,0:T(8,128)(2,1)S(1)}, bf16[4,80,256]{2,1,0:T(8,128)(2,1)S(1)}, u32[]{:S(2)}, u32[]{:S(2)}) %collective-permute-start.8) | collective-permute-done | bytes 163872 | tf_op jit(solution)/shard_map/ppermute | solution.py:249
  69.2 1.7 %collective-permute-start.9 = (bf16[8,80,256]{2,1,0:T(8,128)(2,1)S(1)}, bf16[8,80,256]{2,1,0:T(8,128)(2,1)S(1)}, u32[]{:S(2)}, u32[]{:S(2)}) collective-permute-start(bf16[8,80,256]{2,1,0:T(8,128)(2,1)S(1)} %pad_maximum_fusion), channel_id=1, source_target_pairs={{0,16},{4,20},{8,24},{12,28},{16,0},{20,4},{24,8},{28,12},{1,17},{... | collective-permute-start | bytes 983048 | tf_op jit(solution)/shard_map/ppermute | solution.py:249
  71.0 5.4 %collective-permute-done.9 = bf16[8,80,256]{2,1,0:T(8,128)(2,1)S(1)} collective-permute-done((bf16[8,80,256]{2,1,0:T(8,128)(2,1)S(1)}, bf16[8,80,256]{2,1,0:T(8,128)(2,1)S(1)}, u32[]{:S(2)}, u32[]{:S(2)}) %collective-permute-start.9) | collective-permute-done | bytes 327712 | tf_op jit(solution)/shard_map/ppermute | solution.py:249
  76.5 2.1 %collective-permute-done.10 = bf16[16,80,256]{2,1,0:T(8,128)(2,1)S(1)} collective-permute-done((bf16[16,80,256]{2,1,0:T(8,128)(2,1)S(1)}, bf16[16,80,256]{2,1,0:T(8,128)(2,1)S(1)}, u32[]{:S(2)}, u32[]{:S(2)}) %collective-permute-start.10) | collective-permute-done | bytes 655392 | tf_op jit(solution)/shard_map/ppermute | solution.py:249
  78.6 41.4 %update.1 = bf16[3072,256]{1,0:T(8,128)(2,1)} custom-call(bf16[32,80,256]{2,1,0:T(8,128)(2,1)S(1)} %constant_dynamic-update-slice_fusion.5.refs_0_, bf16[2048,256]{1,0:T(8,128)(2,1)S(1)} %bitcast.29, bf16[1024,256]{1,0:T(8,128)(2,1)S(1)} %bitcast.36), custom_call_target="tpu_custom_call" | custom-call | tf_op jit(solution)/shard_map/update/pallas_call | solution.py:345
  (42 shorter events, 0.4 us)
Async XLA Ops:
  0.0 12.9 %copy-start = (bf16[54,32]{0,1:T(8,128)(2,1)S(1)}, bf16[54,32]{0,1:T(8,128)(2,1)}, u32[]{:S(2)}) copy-start(bf16[54,32]{0,1:T(8,128)(2,1)} %param.13) | copy-start | bytes 10372
  0.0 12.9 %copy-start.5 = (bf16[54,1152]{1,0:T(8,128)(2,1)S(1)}, bf16[54,1152]{1,0:T(8,128)(2,1)}, u32[]{:S(2)}) copy-start(bf16[54,1152]{1,0:T(8,128)(2,1)} %constant.12.clone) | copy-start | bytes 373252
  0.0 5.5 %copy-start.1 = (bf16[2,2,4,128,256]{4,3,2,1,0:T(8,128)(2,1)S(1)}, bf16[2,2,4,128,256]{4,3,2,1,0:T(8,128)(2,1)}, u32[]{:S(2)}) copy-start(bf16[2,2,4,128,256]{4,3,2,1,0:T(8,128)(2,1)} %param.11) | copy-start | bytes 3145732
  0.0 12.1 %copy-start.9 = (f32[32]{0:T(128)S(1)}, f32[32]{0:T(128)}, u32[]{:S(2)}) copy-start(f32[32]{0:T(128)} %param.14) | copy-start | bytes 388
  2.2 14.8 %collective-permute-start = (bf16[2,1,4,128,256]{4,3,2,1,0:T(8,128)(2,1)S(1)}, bf16[2,1,4,128,256]{4,3,2,1,0:T(8,128)(2,1)S(1)}, u32[]{:S(2)}, u32[]{:S(2)}) collective-permute-start(bf16[2,1,4,128,256]{4,3,2,1,0:T(8,128)(2,1)S(1)} %get-tuple-element.12), channel_id=1, source_target_pairs={{0,4},{4,8},{8,12},{12,16},{16,20},{20,24},{24,28},{28,0},{1,5},{5... | collective-permute-start | bytes 1572872 | tf_op jit(solution)/shard_map/ppermute | solution.py:243
  2.7 14.3 %collective-permute-start.1 = (bf16[2,1,4,128,256]{4,3,2,1,0:T(8,128)(2,1)}, bf16[2,1,4,128,256]{4,3,2,1,0:T(8,128)(2,1)S(1)}, u32[]{:S(2)}, u32[]{:S(2)}) collective-permute-start(bf16[2,1,4,128,256]{4,3,2,1,0:T(8,128)(2,1)} %get-tuple-element.11), channel_id=1, source_target_pairs={{4,0},{8,4},{12,8},{16,12},{20,16},{24,20},{28,24},{0,28},{5,1},{9... | collective-permute-start | bytes 1572872 | tf_op jit(solution)/shard_map/ppermute | solution.py:243
  6.4 16.9 %copy-start.10 = (f32[32]{0:T(128)S(1)}, f32[32]{0:T(128)}, u32[]{:S(2)}) copy-start(f32[32]{0:T(128)} %param.15) | copy-start | bytes 388
  6.4 17.8 %copy-start.6 = (s32[2,4,128]{2,1,0:T(4,128)S(1)}, s32[2,4,128]{2,1,0:T(4,128)}, u32[]{:S(2)}) copy-start(s32[2,4,128]{2,1,0:T(4,128)} %param.12) | copy-start | bytes 12292
  6.4 19.1 %collective-permute-start.2 = (bf16[2,2,1,128,256]{4,3,2,1,0:T(8,128)(2,1)}, bf16[2,2,1,128,256]{4,3,2,1,0:T(8,128)(2,1)S(1)}, u32[]{:S(2)}, u32[]{:S(2)}) collective-permute-start(bf16[2,2,1,128,256]{4,3,2,1,0:T(8,128)(2,1)} %get-tuple-element.10), channel_id=1, source_target_pairs={{0,1},{1,2},{2,3},{4,5},{5,6},{6,7},{8,9},{9,10},{10,11},{12,13},{... | collective-permute-start | bytes 786440 | tf_op jit(solution)/shard_map/ppermute | solution.py:243
  10.8 14.7 %collective-permute-start.3 = (bf16[2,2,1,128,256]{4,3,2,1,0:T(8,128)(2,1)}, bf16[2,2,1,128,256]{4,3,2,1,0:T(8,128)(2,1)S(1)}, u32[]{:S(2)}, u32[]{:S(2)}) collective-permute-start(bf16[2,2,1,128,256]{4,3,2,1,0:T(8,128)(2,1)} %get-tuple-element.9), channel_id=1, source_target_pairs={{1,0},{2,1},{3,2},{5,4},{6,5},{7,6},{9,8},{10,9},{11,10},{13,12},{... | collective-permute-start | bytes 786440 | tf_op jit(solution)/shard_map/ppermute | solution.py:243
  12.1 12.1 %copy-start.7 = (f32[64]{0:T(128)S(1)}, f32[64]{0:T(128)}, u32[]{:S(2)}) copy-start(f32[64]{0:T(128)} %param.18) | copy-start | bytes 772
  12.2 12.1 %copy-start.8 = (f32[64]{0:T(128)S(1)}, f32[64]{0:T(128)}, u32[]{:S(2)}) copy-start(f32[64]{0:T(128)} %param.17) | copy-start | bytes 772
  13.0 19.6 %copy-start.2 = (bf16[256,256]{1,0:T(8,128)(2,1)S(1)}, bf16[256,256]{1,0:T(8,128)(2,1)}, u32[]{:S(2)}) copy-start(bf16[256,256]{1,0:T(8,128)(2,1)} %constant.13.clone.swap_in) | copy-start | bytes 393220
  13.0 19.6 %copy-start.3 = (bf16[256,256]{1,0:T(8,128)(2,1)S(1)}, bf16[256,256]{1,0:T(8,128)(2,1)}, u32[]{:S(2)}) copy-start(bf16[256,256]{1,0:T(8,128)(2,1)} %constant.14.clone.swap_out) | copy-start | bytes 393220
  13.0 19.6 %copy-start.4 = (s32[64]{0:T(128)S(1)}, s32[64]{0:T(128)}, u32[]{:S(2)}) copy-start(s32[64]{0:T(128)} %cells.1) | copy-start | bytes 772
  17.8 9.5 %collective-permute-start.4 = (bf16[2,2,1,128,256]{4,3,2,1,0:T(8,128)(2,1)}, bf16[2,2,1,128,256]{4,3,2,1,0:T(8,128)(2,1)S(1)}, u32[]{:S(2)}, u32[]{:S(2)}) collective-permute-start(bf16[2,2,1,128,256]{4,3,2,1,0:T(8,128)(2,1)} %pad_maximum_fusion.1), channel_id=1, source_target_pairs={{0,1},{1,2},{2,3},{4,5},{5,6},{6,7},{8,9},{9,10},{10,11},{12,13},{... | collective-permute-start | bytes 786440 | tf_op jit(solution)/shard_map/ppermute | solution.py:243
  22.0 10.6 %collective-permute-start.5 = (bf16[2,2,1,128,256]{4,3,2,1,0:T(8,128)(2,1)}, bf16[2,2,1,128,256]{4,3,2,1,0:T(8,128)(2,1)S(1)}, u32[]{:S(2)}, u32[]{:S(2)}) collective-permute-start(bf16[2,2,1,128,256]{4,3,2,1,0:T(8,128)(2,1)} %pad_maximum_fusion.2), channel_id=1, source_target_pairs={{1,0},{2,1},{3,2},{5,4},{6,5},{7,6},{9,8},{10,9},{11,10},{13,12},{... | collective-permute-start | bytes 786440 | tf_op jit(solution)/shard_map/ppermute | solution.py:243
  54.1 5.0 %collective-permute-start.6 = (bf16[1,80,256]{2,1,0:T(8,128)(2,1)S(1)}, bf16[1,80,256]{2,1,0:T(8,128)(2,1)S(1)}, u32[]{:S(2)}, u32[]{:S(2)}) collective-permute-start(bf16[1,80,256]{2,1,0:T(8,128)(2,1)S(1)} %bitcast.32), channel_id=1, source_target_pairs={{0,2},{1,3},{2,0},{3,1},{4,6},{5,7},{6,4},{7,5},{8,10},{9,11},{10,... | collective-permute-start | bytes 122888 | tf_op jit(solution)/shard_map/ppermute | solution.py:249
  59.0 4.5 %collective-permute-start.7 = (bf16[2,80,256]{2,1,0:T(8,128)(2,1)S(1)}, bf16[2,80,256]{2,1,0:T(8,128)(2,1)S(1)}, u32[]{:S(2)}, u32[]{:S(2)}) collective-permute-start(bf16[2,80,256]{2,1,0:T(8,128)(2,1)S(1)} %pad_maximum_fusion.4), channel_id=1, source_target_pairs={{0,1},{1,0},{2,3},{3,2},{4,5},{5,4},{6,7},{7,6},{8,9},{9,8},{10,11... | collective-permute-start | bytes 245768 | tf_op jit(solution)/shard_map/ppermute | solution.py:249
  63.6 5.6 %collective-permute-start.8 = (bf16[4,80,256]{2,1,0:T(8,128)(2,1)S(1)}, bf16[4,80,256]{2,1,0:T(8,128)(2,1)S(1)}, u32[]{:S(2)}, u32[]{:S(2)}) collective-permute-start(bf16[4,80,256]{2,1,0:T(8,128)(2,1)S(1)} %pad_maximum_fusion.3), channel_id=1, source_target_pairs={{0,8},{4,12},{8,0},{12,4},{16,24},{20,28},{24,16},{28,20},{1,9},{5... | collective-permute-start | bytes 491528 | tf_op jit(solution)/shard_map/ppermute | solution.py:249
  69.2 7.1 %collective-permute-start.9 = (bf16[8,80,256]{2,1,0:T(8,128)(2,1)S(1)}, bf16[8,80,256]{2,1,0:T(8,128)(2,1)S(1)}, u32[]{:S(2)}, u32[]{:S(2)}) collective-permute-start(bf16[8,80,256]{2,1,0:T(8,128)(2,1)S(1)} %pad_maximum_fusion), channel_id=1, source_target_pairs={{0,16},{4,20},{8,24},{12,28},{16,0},{20,4},{24,8},{28,12},{1,17},{... | collective-permute-start | bytes 983048 | tf_op jit(solution)/shard_map/ppermute | solution.py:249
  76.4 2.2 %collective-permute-start.10 = (bf16[16,80,256]{2,1,0:T(8,128)(2,1)S(1)}, bf16[16,80,256]{2,1,0:T(8,128)(2,1)S(1)}, u32[]{:S(2)}, u32[]{:S(2)}) collective-permute-start(bf16[16,80,256]{2,1,0:T(8,128)(2,1)S(1)} %get-tuple-element.17), channel_id=1, source_target_pairs={{0,4},{4,0},{8,12},{12,8},{16,20},{20,16},{24,28},{28,24},{1,5},{5... | collective-permute-start | bytes 1966088 | tf_op jit(solution)/shard_map/ppermute | solution.py:249

commit v2 on v1

--- a/solution.py
+++ b/solution.py
@@ -13,7 +13,8 @@
 PAY_ROWS = 16
 GATHER_DEVICES = 64
 BLOCK = 64
-VMEM_BYTES = 48 * 1024 * 1024
+PIECES = 4
+VMEM_BYTES = 32 * 1024 * 1024
 
 
 def plane_places(planes, columns):
@@ -55,14 +56,18 @@
     return first, second, third
 
 
-def surrogate_kernel(
-    own, low, high, left, right, corner_left, corner_right, weights, swap_in, swap_out, mask,
-    sigma, values, read_half, cells, sat_out, pay_out, packed, sat_rows, sat_float, pred
+def ones_rows(members):
+    row_index = lax.broadcasted_iota(jnp.int32, (16, members), 0)
+    return jnp.where(row_index < 3, 1.0, 0.0).astype(jnp.bfloat16)
+
+
+def observe_kernel(
+    own, low, high, left, right, corner_left, corner_right, by_row, swap_in, read_column,
+    sigma, values, cells, mask, packed, pay_out, pred
 ):
     lanes, members = own.shape[1], own.shape[2]
     count = packed.shape[1]
-    rows = mask.shape[0]
-    channels = read_half.shape[0]
+    observed = cells.shape[0]
     packed[0] = jnp.zeros((count, members), jnp.bfloat16)
     packed[lanes + 1] = jnp.zeros((count, members), jnp.bfloat16)
 
@@ -81,46 +86,24 @@
         return carry
 
     lax.fori_loop(0, lanes // 16, pack, 0)
-
-    row_index = lax.broadcasted_iota(jnp.int32, (16, members), 0)
-    ones = jnp.where(row_index < 3, 1.0, 0.0).astype(jnp.bfloat16)
-    lane_index = lax.broadcasted_iota(jnp.int32, (rows, lanes), 1)
-
-    def two_rows(step, carry):
-        found = []
-        for k in range(2):
-            y = step * 2 + k
+    ones = ones_rows(members)
+    read = jnp.broadcast_to(read_column[...], (read_column.shape[0], members))
+
+    def some_cells(step, carry):
+        for k in range(4):
+            o = step * 4 + k
+            cell = cells[o]
+            row, y = cell // lanes, cell % lanes
             taps = jnp.concatenate(
                 [packed[pl.ds(y, 3)].reshape(3 * count, members), ones], axis=0
             )
-            half = jnp.dot(weights[...], taps, preferred_element_type=jnp.float32)
-            total = jnp.zeros((rows, members), jnp.float32)
-            for c in range(channels):
-                part = half[rows * c : rows * c + rows]
-                total = total + read_half[c] * (part * (1.0 + jnp.tanh(part)))
-            here = jnp.sum(jnp.where(lane_index == y, mask[...], 0.0), axis=1, keepdims=True)
-            found.append(here * (0.5 + 0.5 * jnp.tanh(total)))
-        both = jnp.concatenate(found, axis=0).astype(jnp.bfloat16)
-        at = pl.multiple_of(step * 2 * rows, 2 * rows)
-        sat_rows[pl.ds(at, 2 * rows), :] = both
-        sat_float[pl.ds(at, 2 * rows), :] = both.astype(jnp.float32)
+            half = jnp.dot(by_row[row], taps, preferred_element_type=jnp.float32)
+            total = jnp.sum(read * (half * (1.0 + jnp.tanh(half))), axis=0, keepdims=True)
+            found = (0.5 + 0.5 * jnp.tanh(total)) * mask[row, y].astype(jnp.float32)
+            pred[pl.ds(o, 1), :] = found.astype(jnp.bfloat16).astype(jnp.float32)
         return carry
 
-    lax.fori_loop(0, lanes // 2, two_rows, 0)
-
-    span = 256 // rows
-    for b in range(lanes // span):
-        moved = jnp.dot(
-            swap_out[...], sat_rows[256 * b : 256 * b + 256, :], preferred_element_type=jnp.float32
-        )
-        sat_out[:, span * b : span * b + span, :] = moved.astype(jnp.bfloat16).reshape(
-            rows, span, members
-        )
-
-    for o in range(cells.shape[0]):
-        cell = cells[o]
-        row = (cell % lanes) * rows + cell // lanes
-        pred[o : o + 1, :] = sat_float[pl.ds(row, 1), :]
+    lax.fori_loop(0, observed // 4, some_cells, 0)
 
     root_count = math.sqrt(members - 1)
     predicted = pred[...]
@@ -134,9 +117,38 @@
     third = coeff - first - second
     index = lax.broadcasted_iota(jnp.int32, (PAY_ROWS, members), 0)
     tail = jnp.where(index == 0, first, jnp.where(index == 1, second, jnp.where(index == 2, third, 0.0)))
-    observed = cells.shape[0]
     pay_out[0:observed, :] = scaled.astype(jnp.bfloat16)
     pay_out[observed : observed + PAY_ROWS, :] = tail.astype(jnp.bfloat16)
+
+
+def saturate_kernel(start, packed, weights, swap_out, mask, read_half, sat_out, sat_rows):
+    rows, span, members = sat_out.shape
+    count = packed.shape[1]
+    channels = read_half.shape[0]
+    ones = ones_rows(members)
+    lane_index = lax.broadcasted_iota(jnp.int32, mask.shape, 1)
+
+    def two_rows(step, carry):
+        found = []
+        for k in range(2):
+            y = start + step * 2 + k
+            taps = jnp.concatenate(
+                [packed[pl.ds(y, 3)].reshape(3 * count, members), ones], axis=0
+            )
+            half = jnp.dot(weights[...], taps, preferred_element_type=jnp.float32)
+            total = jnp.zeros((rows, members), jnp.float32)
+            for c in range(channels):
+                part = half[rows * c : rows * c + rows]
+                total = total + read_half[c] * (part * (1.0 + jnp.tanh(part)))
+            here = jnp.sum(jnp.where(lane_index == y, mask[...], 0.0), axis=1, keepdims=True)
+            found.append(here * (0.5 + 0.5 * jnp.tanh(total)))
+        at = pl.multiple_of(step * 2 * rows, 2 * rows)
+        sat_rows[pl.ds(at, 2 * rows), :] = jnp.concatenate(found, axis=0).astype(jnp.bfloat16)
+        return carry
+
+    lax.fori_loop(0, span // 2, two_rows, 0)
+    moved = jnp.dot(swap_out[...], sat_rows[...], preferred_element_type=jnp.float32)
+    sat_out[...] = moved.astype(jnp.bfloat16).reshape(rows, span, members)
 
 
 def transposed_dot(a, b, precision):
@@ -145,39 +157,81 @@
     )
 
 
+def spread_row(part, p):
+    return jnp.broadcast_to(part[p : p + 1, :], part.shape)
+
+
+def spread_lane(part, q):
+    return jnp.broadcast_to(part[:, q : q + 1], part.shape)
+
+
+def inverse_root(value):
+    guess = lax.rsqrt(value)
+    return guess * (1.5 - (0.5 * value) * (guess * guess))
+
+
 def inverse_factor_block(block):
     lane = lax.broadcasted_iota(jnp.int32, (8, 2 * BLOCK), 1)
     sub = lax.broadcasted_iota(jnp.int32, (8, 2 * BLOCK), 0)
+    groups = BLOCK // 8
     parts = []
-    for i in range(BLOCK // 8):
+    for i in range(groups):
         unit = jnp.where(lane == sub + (BLOCK + 8 * i), 1.0, 0.0)
         known = jnp.concatenate(
             [block[8 * i : 8 * i + 8, :], jnp.zeros((8, BLOCK), jnp.float32)], axis=1
         )
         parts.append(known + unit)
-    pivots = [jnp.ones((8, 2 * BLOCK), jnp.float32) for _ in parts]
-    for j in range(BLOCK):
-        top, inner = j // 8, j % 8
-        row = jnp.broadcast_to(parts[top][inner : inner + 1, :], (8, 2 * BLOCK))
-        pivot = jnp.broadcast_to(row[:, j : j + 1], (8, 2 * BLOCK))
-        pivots[top] = jnp.where(sub == inner, pivot, pivots[top])
-        row = row * (1.0 / pivot)
-        for i in range(top, BLOCK // 8):
-            column = jnp.broadcast_to(parts[i][:, j : j + 1], (8, 2 * BLOCK))
-            if i == top:
-                column = jnp.where(sub > inner, column, 0.0)
-            parts[i] = parts[i] - column * row
-    return jnp.concatenate(
-        [(part * lax.rsqrt(pivot))[:, BLOCK:] for part, pivot in zip(parts, pivots)], axis=0
-    )
+    done = []
+    for j in range(groups):
+        corner = [spread_lane(parts[j], 8 * j + q) for q in range(8)]
+        entry = {(p, q): spread_row(corner[q], p) for q in range(8) for p in range(q, 8)}
+        line = [spread_row(parts[j], p) for p in range(8)]
+        near = j + 1 < groups
+        if near:
+            beside = [spread_lane(parts[j + 1], 8 * j + q) for q in range(8)]
+        factor, scale = {}, []
+        for q in range(8):
+            root = inverse_root(entry[q, q])
+            scale.append(root)
+            line[q] = line[q] * root
+            for p in range(q + 1, 8):
+                factor[p, q] = entry[p, q] * root
+            for t in range(q + 1, 8):
+                for p in range(t, 8):
+                    entry[p, t] = entry[p, t] - factor[p, q] * factor[t, q]
+            for p in range(q + 1, 8):
+                line[p] = line[p] - factor[p, q] * line[q]
+            if near:
+                lead = beside[q] * root
+                for t in range(q + 1, 8):
+                    beside[t] = beside[t] - lead * factor[t, q]
+                parts[j + 1] = parts[j + 1] - lead * line[q]
+        if j + 2 < groups:
+            weighted = [None] * 8
+            for q in range(7, -1, -1):
+                rest = line[q]
+                for p in range(q + 1, 8):
+                    rest = rest - factor[p, q] * weighted[p]
+                weighted[q] = rest * scale[q]
+            for i in range(j + 2, groups):
+                change = spread_lane(parts[i], 8 * j) * weighted[0]
+                for q in range(1, 8):
+                    change = change + spread_lane(parts[i], 8 * j + q) * weighted[q]
+                parts[i] = parts[i] - change
+        merged = line[0]
+        for q in range(1, 8):
+            merged = jnp.where(sub == q, line[q], merged)
+        done.append(merged[:, BLOCK:])
+    return jnp.concatenate(done, axis=0)
 
 
 def update_kernel(gathered, *refs):
     if gathered:
-        pay, fields, sat, out, joint, mixing = refs
+        pay, refs = refs[0], refs[1:]
     else:
-        gram, coeff_in, fields, sat, out, joint, mixing = refs
-    members = fields.shape[1]
+        gram, coeff_in, refs = refs[0], refs[1], refs[2:]
+    fields, sats, (out, joint, mixing) = refs[0], refs[1:-3], refs[-3:]
+    members = fields.shape[2]
     sub = lax.broadcasted_iota(jnp.int32, (members, members), 0)
     lane = lax.broadcasted_iota(jnp.int32, (members, members), 1)
     identity = jnp.where(sub == lane, 1.0, 0.0)
@@ -216,22 +270,27 @@
     weight = jnp.dot(half, inverse, preferred_element_type=jnp.float32, precision=HIGHEST)
     mixing[...] = jnp.transpose(inverse + weight[0:1, :]).astype(jnp.bfloat16)
 
-    def blend(source, target, base):
-        span = 256
-
-        def step(s, carry):
-            at = pl.multiple_of(s * span, span)
-            state = source[pl.ds(at, span), :].astype(jnp.float32)
-            mean = jnp.mean(state, axis=1, keepdims=True)
-            anomalies = (state - mean).astype(jnp.bfloat16)
-            moved = jnp.dot(anomalies, mixing[...], preferred_element_type=jnp.float32)
-            target[pl.ds(base + at, span), :] = (mean + moved).astype(jnp.bfloat16)
-            return carry
-
-        lax.fori_loop(0, source.shape[0] // span, step, 0)
-
-    blend(fields, out, 0)
-    blend(sat, out, fields.shape[0])
+    def blend(state):
+        state = state.astype(jnp.float32)
+        mean = jnp.mean(state, axis=1, keepdims=True)
+        anomalies = (state - mean).astype(jnp.bfloat16)
+        moved = jnp.dot(anomalies, mixing[...], preferred_element_type=jnp.float32)
+        return (mean + moved).astype(jnp.bfloat16)
+
+    field_rows, lanes = fields.shape[0], fields.shape[1]
+
+    def step(n, carry):
+        at = pl.multiple_of(2 * n, 2)
+        block = fields[pl.ds(at, 2)].reshape(2 * lanes, members)
+        out[pl.ds(at, 2)] = blend(block).reshape(2, lanes, members)
+        return carry
+
+    lax.fori_loop(0, field_rows // 2, step, 0)
+    for n, sat in enumerate(sats):
+        rows, span = sat.shape[0], sat.shape[1]
+        out[field_rows:, n * span : (n + 1) * span, :] = blend(
+            sat[...].reshape(rows * span, members)
+        ).reshape(rows, span, members)
 
 
 def shift(value, axis, by, closed):
@@ -243,12 +302,20 @@
     return lax.ppermute(value, axis, pairs)
 
 
-def gather_rows(block, steps):
-    for axis, bit in steps:
+def gather_rows(block, steps, packed, saturate):
+    pieces = []
+    for n, (axis, bit) in enumerate(steps):
         count = lax.axis_size(axis)
+        if n < PIECES:
+            block, packed = lax.optimization_barrier((block, packed))
         other = lax.ppermute(block, axis, [(i, i ^ bit) for i in range(count)])
+        if n < PIECES:
+            piece = saturate(n, packed)
         block = jnp.concatenate([block, other], axis=0)
-    return block
+        if n < PIECES:
+            block, piece = lax.optimization_barrier((block, piece))
+            pieces.append(piece)
+    return block, pieces + [saturate(n, packed) for n in range(len(pieces), PIECES)]
 
 
 def bits_of(axis, count):
@@ -294,39 +361,51 @@
     ).reshape(channels, rows, 3 * count)
     bias = jnp.stack(three_pieces(0.5 * conv_bias), axis=1)
     bias = jnp.broadcast_to(bias[:, None, :], (channels, rows, 3))
-    weights = (
-        jnp.concatenate(
-            [0.5 * taps, bias, jnp.zeros((channels, rows, 13), jnp.float32)], axis=2
-        )
-        .reshape(channels * rows, 3 * count + 16)
-        .astype(jnp.bfloat16)
-    )
+    weights = jnp.concatenate(
+        [0.5 * taps, bias, jnp.zeros((channels, rows, 13), jnp.float32)], axis=2
+    ).astype(jnp.bfloat16)
+    by_row = jnp.transpose(weights, (1, 0, 2))
+    weights = weights.reshape(channels * rows, 3 * count + 16)
     flat = lambda a: a.reshape(-1, lanes, members)
-    sat, pay = pl.pallas_call(
-        surrogate_kernel,
+    span = lanes // PIECES
+    mask = pore_mask.reshape(rows, lanes)
+    mask_float = mask.astype(jnp.float32)
+    read_half = 0.5 * read_weight
+    swap_in = jnp.asarray(swap_matrix(16, 16), jnp.bfloat16)
+    swap_out = jnp.asarray(swap_matrix(span, rows), jnp.bfloat16)
+    params = pltpu.CompilerParams(vmem_limit_bytes=VMEM_BYTES)
+    packed, pay = pl.pallas_call(
+        observe_kernel,
         out_shape=(
-            jax.ShapeDtypeStruct((rows, lanes, members), jnp.bfloat16),
+            jax.ShapeDtypeStruct((lanes + 2, count, members), jnp.bfloat16),
             jax.ShapeDtypeStruct((observed + PAY_ROWS, members), jnp.bfloat16),
         ),
-        in_specs=[vmem()] * 13 + [smem()] * 2,
+        in_specs=[vmem()] * 12 + [smem()] * 2,
         out_specs=(vmem(), vmem()),
-        scratch_shapes=[
-            pltpu.VMEM((lanes + 2, count, members), jnp.bfloat16),
-            pltpu.VMEM((rows * lanes, members), jnp.bfloat16),
-            pltpu.VMEM((rows * lanes, members), jnp.float32),
-            pltpu.VMEM((observed, members), jnp.float32),
-        ],
-        compiler_params=pltpu.CompilerParams(vmem_limit_bytes=VMEM_BYTES),
-        name="surrogate",
+        scratch_shapes=[pltpu.VMEM((observed, members), jnp.float32)],
+        compiler_params=params,
+        name="observe",
     )(
         flat(fields), flat(low), flat(high), flat(left), flat(right), flat(corner_left),
-        flat(corner_right), weights,
-        jnp.asarray(swap_matrix(16, 16), jnp.bfloat16),
-        jnp.asarray(swap_matrix(256 // rows, rows), jnp.bfloat16),
-        pore_mask.reshape(rows, lanes).astype(jnp.float32),
-        obs_sigma.reshape(observed, 1), obs_values.reshape(observed, 1),
-        0.5 * read_weight, obs_cells,
-    )
+        flat(corner_right), by_row, swap_in, read_half[:, None],
+        obs_sigma[:, None], obs_values[:, None], obs_cells, mask,
+    )
+
+    def saturate(n, packed):
+        return pl.pallas_call(
+            functools.partial(saturate_kernel, n * span),
+            out_shape=jax.ShapeDtypeStruct((rows, span, members), jnp.bfloat16),
+            in_specs=[vmem()] * 4 + [smem()],
+            out_specs=vmem(),
+            scratch_shapes=[pltpu.VMEM((rows * span, members), jnp.bfloat16)],
+            compiler_params=params,
+            cost_estimate=pl.CostEstimate(
+                flops=2 * 256 * 256 * span * members,
+                bytes_accessed=4 * 1024 * 1024,
+                transcendentals=channels * rows * span * members,
+            ),
+            name="saturate",
+        )(packed, weights, swap_out, mask_float, read_half)
 
     core_count, face_count = lax.axis_size("cores"), lax.axis_size("face")
     devices = core_count * face_count
@@ -334,7 +413,8 @@
     if gathered:
         steps = bits_of("face", face_count)[::-1] + bits_of("cores", core_count)[1:]
         steps = steps + bits_of("cores", core_count)[:1]
-        terms = (gather_rows(pay[None], steps),)
+        block, pieces = gather_rows(pay[None], steps, packed, saturate)
+        terms = (block,)
     else:
         part = pay[:observed]
         gram = lax.dot_general(
@@ -342,18 +422,19 @@
         )
         coeff = jnp.sum(pay[observed:].astype(jnp.float32), axis=0, keepdims=True)
         terms = lax.psum((gram, coeff), ("cores", "face"))
+        pieces = [saturate(n, packed) for n in range(PIECES)]
     out = pl.pallas_call(
         functools.partial(update_kernel, gathered),
-        out_shape=jax.ShapeDtypeStruct((3 * rows * lanes, members), jnp.bfloat16),
-        in_specs=[vmem()] * (len(terms) + 2),
+        out_shape=jax.ShapeDtypeStruct((3 * rows, lanes, members), jnp.bfloat16),
+        in_specs=[vmem()] * (len(terms) + 1 + PIECES),
         out_specs=vmem(),
         scratch_shapes=[
             pltpu.VMEM((members, 2 * members), jnp.float32),
             pltpu.VMEM((members, members), jnp.bfloat16),
         ],
-        compiler_params=pltpu.CompilerParams(vmem_limit_bytes=VMEM_BYTES),
+        compiler_params=params,
         name="update",
-    )(*terms, fields.reshape(-1, members), sat.reshape(-1, members))
+    )(*terms, flat(fields), *pieces)
     return out.reshape(3, planes, columns, lanes, members)
 
 

time: 120 us -> 87.6 us (0.73)
  Pallas kernels: 62.9 us -> 43.1 us
  waiting for transfers between devices: 26.7 us -> 16.3 us
  starting transfers between devices: 22.4 us -> 19.1 us
    pallas_call x1, Pallas kernels: 41.4 us -> 16.2 us  [shards(): pl.pallas_call(functools.partial(update_kernel, gathered), out_shape=jax....]
    ppermute x5, waiting for transfers between devices: 15.6 us -> 5.47 us  [gather_rows(): other = lax.ppermute(block, axis, [(i, i ^ bit) for i in range(count)])]
    pallas_call x1 -> x5, Pallas kernels: 21.4 us -> 26.9 us  [the longest x4 20.4 us: saturate(): pl.pallas_call(functools.partial(saturate_kernel, n * span), out_shape=ja...]
    ppermute x5, starting transfers between devices: 8.67 us -> 5.43 us  [gather_rows(): other = lax.ppermute(block, axis, [(i, i ^ bit) for i in range(count)])]
  transfers between devices with their start and end apart: 11 -> 11, of which waited for: 8 -> 6; matrix products, arithmetic and copies ran while one was open for 5% -> 7% of each run, Pallas kernels for 0% -> 23%
where the time goes in v2:
time: 87.6 us; the launch traced here: 87.4 us
  Pallas kernels  43.1 us (49%)
  starting transfers between devices  19.1 us (22%)
  waiting for transfers between devices  16.3 us (19%)
  local copies, waits for them, and re-layouts  5.52 us (6%)
  other arithmetic  2.87 us (3%)
    pallas_call x4, Pallas kernels, saturate(): pl.pallas_call(functools.partial(saturate_kernel, n * span), out_shape=ja...  20.4 us
    pallas_call x1, Pallas kernels, shards(): pl.pallas_call(functools.partial(update_kernel, gathered), out_shape=jax....  16.2 us
    ppermute x6, starting transfers between devices, shift(): return lax.ppermute(value, axis, pairs)  13.6 us
    ppermute x6, waiting for transfers between devices, shift(): return lax.ppermute(value, axis, pairs)  10.8 us
    pallas_call x1, Pallas kernels, shards(): pl.pallas_call(observe_kernel, out_shape=(jax.ShapeDtypeStruct((lanes + 2...  6.51 us
    ppermute x5, waiting for transfers between devices, gather_rows(): other = lax.ppermute(block, axis, [(i, i ^ bit) for i in range(count)])  5.47 us
    ppermute x5, starting transfers between devices, gather_rows(): other = lax.ppermute(block, axis, [(i, i ^ bit) for i in range(count)])  5.43 us
    slice x1, local copies, waits for them, and re-layouts, shards(): high = shift(fields[:, :1], 'cores', -1, True)  2.38 us
  transfers between devices with their start and end apart: 11, of which 6 were waited for; matrix products, arithmetic and copies ran while one was open for 7% of the time, Pallas kernels for 23%

profile of v2, /device:TPU:0, one launch (start us, length us, event | category | flops | bytes accessed | tf_op | source)
XLA Modules:
  0.0 87.4 jit_solution(15919023938070031462)
XLA Ops:
  0.0 2.4 %fusion.6 = (bf16[2,1,4,128,256]{4,3,2,1,0:T(8,128)(2,1)}, bf16[2,1,4,128,256]{4,3,2,1,0:T(8,128)(2,1)}) fusion(bf16[2,2,4,128,256]{4,3,2,1,0:T(8,128)(2,1)} %param.11), kind=kLoop, calls=%fused_computation.23 | loop fusion | bytes 2097152 | tf_op jit(solution)/shard_map/slice | solution.py:345
  2.4 0.5 collective-permute-start
  2.9 2.9 %collective-permute-start.1 = (bf16[2,1,4,128,256]{4,3,2,1,0:T(8,128)(2,1)}, bf16[2,1,4,128,256]{4,3,2,1,0:T(8,128)(2,1)S(1)}, u32[]{:S(2)}, u32[]{:S(2)}) collective-permute-start(bf16[2,1,4,128,256]{4,3,2,1,0:T(8,128)(2,1)} %get-tuple-element.43), channel_id=1, source_target_pairs={{4,0},{8,4},{12,8},{16,12},{20,16},{24,20},{28,24},{0,28},{5,1},{9... | collective-permute-start | bytes 1572872 | tf_op jit(solution)/shard_map/ppermute | solution.py:302
  5.7 0.9 fusion.5
  6.6 4.2 %collective-permute-start.2 = (bf16[2,2,1,128,256]{4,3,2,1,0:T(8,128)(2,1)}, bf16[2,2,1,128,256]{4,3,2,1,0:T(8,128)(2,1)S(1)}, u32[]{:S(2)}, u32[]{:S(2)}) collective-permute-start(bf16[2,2,1,128,256]{4,3,2,1,0:T(8,128)(2,1)} %get-tuple-element.42), channel_id=1, source_target_pairs={{0,1},{1,2},{2,3},{4,5},{5,6},{6,7},{8,9},{9,10},{10,11},{12,13},{... | collective-permute-start | bytes 786440 | tf_op jit(solution)/shard_map/ppermute | solution.py:302
  10.8 1.3 %collective-permute-start.3 = (bf16[2,2,1,128,256]{4,3,2,1,0:T(8,128)(2,1)}, bf16[2,2,1,128,256]{4,3,2,1,0:T(8,128)(2,1)S(1)}, u32[]{:S(2)}, u32[]{:S(2)}) collective-permute-start(bf16[2,2,1,128,256]{4,3,2,1,0:T(8,128)(2,1)} %get-tuple-element.41), channel_id=1, source_target_pairs={{1,0},{2,1},{3,2},{5,4},{6,5},{7,6},{9,8},{10,9},{11,10},{13,12},{... | collective-permute-start | bytes 786440 | tf_op jit(solution)/shard_map/ppermute | solution.py:302
  12.2 0.1 fusion.1
  12.3 0.1 copy.17
  12.5 0.6 broadcast_bitcast_fusion
  13.1 0.2 mul.21
  13.6 2.1 %collective-permute-done = bf16[2,1,4,128,256]{4,3,2,1,0:T(8,128)(2,1)S(1)} collective-permute-done((bf16[2,1,4,128,256]{4,3,2,1,0:T(8,128)(2,1)}, bf16[2,1,4,128,256]{4,3,2,1,0:T(8,128)(2,1)S(1)}, u32[]{:S(2)}, u32[]{:S(2)}) %collective-permute-start) | collective-permute-done | bytes 524320 | tf_op jit(solution)/shard_map/ppermute | solution.py:302
  15.8 1.6 %collective-permute-done.1 = bf16[2,1,4,128,256]{4,3,2,1,0:T(8,128)(2,1)S(1)} collective-permute-done((bf16[2,1,4,128,256]{4,3,2,1,0:T(8,128)(2,1)}, bf16[2,1,4,128,256]{4,3,2,1,0:T(8,128)(2,1)S(1)}, u32[]{:S(2)}, u32[]{:S(2)}) %collective-permute-start.1) | collective-permute-done | bytes 524320 | tf_op jit(solution)/shard_map/ppermute | solution.py:302
  17.4 0.7 pad_maximum_fusion.3
  18.1 3.5 %collective-permute-start.4 = (bf16[2,2,1,128,256]{4,3,2,1,0:T(8,128)(2,1)}, bf16[2,2,1,128,256]{4,3,2,1,0:T(8,128)(2,1)S(1)}, u32[]{:S(2)}, u32[]{:S(2)}) collective-permute-start(bf16[2,2,1,128,256]{4,3,2,1,0:T(8,128)(2,1)} %pad_maximum_fusion.3), channel_id=1, source_target_pairs={{0,1},{1,2},{2,3},{4,5},{5,6},{6,7},{8,9},{9,10},{10,11},{12,13},{... | collective-permute-start | bytes 786440 | tf_op jit(solution)/shard_map/ppermute | solution.py:302
  21.6 0.7 pad_maximum_fusion.4
  22.4 1.3 %collective-permute-start.5 = (bf16[2,2,1,128,256]{4,3,2,1,0:T(8,128)(2,1)}, bf16[2,2,1,128,256]{4,3,2,1,0:T(8,128)(2,1)S(1)}, u32[]{:S(2)}, u32[]{:S(2)}) collective-permute-start(bf16[2,2,1,128,256]{4,3,2,1,0:T(8,128)(2,1)} %pad_maximum_fusion.4), channel_id=1, source_target_pairs={{1,0},{2,1},{3,2},{5,4},{6,5},{7,6},{9,8},{10,9},{11,10},{13,12},{... | collective-permute-start | bytes 786440 | tf_op jit(solution)/shard_map/ppermute | solution.py:302
  23.7 0.9 mul.24
  24.8 1.0 %maximum_maximum_fusion.weights = bf16[256,160]{1,0:T(8,128)(2,1)S(1)} fusion(bf16[256,3]{1,0:T(8,128)(2,1)} %broadcast_bitcast_fusion, bf16[256,144]{1,0:T(8,128)(2,1)} %mul.24, bf16[160]{0:T(256)(128)(2,1)S(1)} %pad.15.clone), kind=kLoop, calls=%fused_computation.10 | loop fusion | flops 245760 | bytes 157504 | tf_op jit(solution)/shard_map/concatenate | solution.py:364
  25.9 1.7 %collective-permute-done.4 = bf16[2,2,1,128,256]{4,3,2,1,0:T(8,128)(2,1)S(1)} collective-permute-done((bf16[2,2,1,128,256]{4,3,2,1,0:T(8,128)(2,1)}, bf16[2,2,1,128,256]{4,3,2,1,0:T(8,128)(2,1)S(1)}, u32[]{:S(2)}, u32[]{:S(2)}) %collective-permute-start.4) | collective-permute-done | bytes 262176 | tf_op jit(solution)/shard_map/ppermute | solution.py:302
  27.6 5.3 %collective-permute-done.5 = bf16[2,2,1,128,256]{4,3,2,1,0:T(8,128)(2,1)S(1)} collective-permute-done((bf16[2,2,1,128,256]{4,3,2,1,0:T(8,128)(2,1)}, bf16[2,2,1,128,256]{4,3,2,1,0:T(8,128)(2,1)S(1)}, u32[]{:S(2)}, u32[]{:S(2)}) %collective-permute-start.5) | collective-permute-done | bytes 262176 | tf_op jit(solution)/shard_map/ppermute | solution.py:302
  33.0 6.5 %observe.1 = (bf16[130,48,256]{2,1,0:T(8,128)(2,1)S(1)}, bf16[80,256]{1,0:T(8,128)(2,1)S(1)}) custom-call(bf16[16,128,256]{2,1,0:T(8,128)(2,1)S(1)} %bitcast.28, bf16[8,128,256]{2,1,0:T(8,128)(2,1)S(1)} %bitcast.30, bf16[8,128,256]{2,1,0:T(8,128)(2,1)S(1)} %bitcast.31, bf16[4,128,256]{2,1,0:T(8,128)(2,1)S(1)} %bitcast.32, bf16[4,128,256]{2,1,0:T(8,128)(2,1)S(1)} %bitcast.33, ...), custom_call_target="tpu_custom_call" | custom-call | tf_op jit(solution)/shard_map/observe/pallas_call | solution.py:377
  39.5 3.0 %collective-permute-start.6 = (bf16[1,80,256]{2,1,0:T(8,128)(2,1)S(1)}, bf16[1,80,256]{2,1,0:T(8,128)(2,1)S(1)}, u32[]{:S(2)}, u32[]{:S(2)}) collective-permute-start(bf16[1,80,256]{2,1,0:T(8,128)(2,1)S(1)} %bitcast.36), channel_id=1, source_target_pairs={{0,2},{1,3},{2,0},{3,1},{4,6},{5,7},{6,4},{7,5},{8,10},{9,11},{10,... | collective-permute-start | bytes 122888 | tf_op jit(solution)/shard_map/ppermute | solution.py:311
  42.5 5.1 %saturate.4.refs_2_ = bf16[8,32,256]{2,1,0:T(8,128)(2,1)S(1)} custom-call(bf16[130,48,256]{2,1,0:T(8,128)(2,1)S(1)} %get-tuple-element.35.packed, bf16[256,160]{1,0:T(8,128)(2,1)S(1)} %maximum_maximum_fusion.weights, bf16[256,256]{1,0:T(8,128)(2,1)S(1)} %copy-done.5, f32[8,128]{1,0:T(8,128)S(1)} %convert_element_type.5.mask, f32[32]{0:T(128)S(1)} %get-tuple-element.49.read_half), custom_call_target="tpu_custom_call" | custom-call | flops 1073741824 | bytes 4194304 | tf_op jit(solution)/shard_map/saturate/pallas_call | solution.py:395
  47.7 5.1 %saturate.5.refs_3_ = bf16[8,32,256]{2,1,0:T(8,128)(2,1)S(1)} custom-call(bf16[130,48,256]{2,1,0:T(8,128)(2,1)S(1)} %get-tuple-element.35.packed, bf16[256,160]{1,0:T(8,128)(2,1)S(1)} %maximum_maximum_fusion.weights, bf16[256,256]{1,0:T(8,128)(2,1)S(1)} %copy-done.5, f32[8,128]{1,0:T(8,128)S(1)} %convert_element_type.5.mask, f32[32]{0:T(128)S(1)} %get-tuple-element.49.read_half), custom_call_target="tpu_custom_call" | custom-call | flops 1073741824 | bytes 4194304 | tf_op jit(solution)/shard_map/saturate/pallas_call | solution.py:395
  52.8 1.6 %collective-permute-start.8 = (bf16[4,80,256]{2,1,0:T(8,128)(2,1)S(1)}, bf16[4,80,256]{2,1,0:T(8,128)(2,1)S(1)}, u32[]{:S(2)}, u32[]{:S(2)}) collective-permute-start(bf16[4,80,256]{2,1,0:T(8,128)(2,1)S(1)} %pad_maximum_fusion.5), channel_id=1, source_target_pairs={{0,8},{4,12},{8,0},{12,4},{16,24},{20,28},{24,16},{28,20},{1,9},{5... | collective-permute-start | bytes 491528 | tf_op jit(solution)/shard_map/ppermute | solution.py:311
  54.4 5.1 %saturate.6.refs_4_ = bf16[8,32,256]{2,1,0:T(8,128)(2,1)S(1)} custom-call(bf16[130,48,256]{2,1,0:T(8,128)(2,1)S(1)} %get-tuple-element.35.packed, bf16[256,160]{1,0:T(8,128)(2,1)S(1)} %maximum_maximum_fusion.weights, bf16[256,256]{1,0:T(8,128)(2,1)S(1)} %copy-done.5, f32[8,128]{1,0:T(8,128)S(1)} %convert_element_type.5.mask, f32[32]{0:T(128)S(1)} %get-tuple-element.49.read_half), custom_call_target="tpu_custom_call" | custom-call | flops 1073741824 | bytes 4194304 | tf_op jit(solution)/shard_map/saturate/pallas_call | solution.py:395
  59.6 0.8 collective-permute-start.9
  60.3 5.1 %saturate.7.refs_5_ = bf16[8,32,256]{2,1,0:T(8,128)(2,1)S(1)} custom-call(bf16[130,48,256]{2,1,0:T(8,128)(2,1)S(1)} %get-tuple-element.35.packed, bf16[256,160]{1,0:T(8,128)(2,1)S(1)} %maximum_maximum_fusion.weights, bf16[256,256]{1,0:T(8,128)(2,1)S(1)} %copy-done.5, f32[8,128]{1,0:T(8,128)S(1)} %convert_element_type.5.mask, f32[32]{0:T(128)S(1)} %get-tuple-element.49.read_half), custom_call_target="tpu_custom_call" | custom-call | flops 1073741824 | bytes 4194304 | tf_op jit(solution)/shard_map/saturate/pallas_call | solution.py:395
  65.5 3.4 %collective-permute-done.9 = bf16[8,80,256]{2,1,0:T(8,128)(2,1)S(1)} collective-permute-done((bf16[8,80,256]{2,1,0:T(8,128)(2,1)S(1)}, bf16[8,80,256]{2,1,0:T(8,128)(2,1)S(1)}, u32[]{:S(2)}, u32[]{:S(2)}) %collective-permute-start.9) | collective-permute-done | bytes 327712 | tf_op jit(solution)/shard_map/ppermute | solution.py:311
  69.0 2.1 %collective-permute-done.10 = bf16[16,80,256]{2,1,0:T(8,128)(2,1)S(1)} collective-permute-done((bf16[16,80,256]{2,1,0:T(8,128)(2,1)S(1)}, bf16[16,80,256]{2,1,0:T(8,128)(2,1)S(1)}, u32[]{:S(2)}, u32[]{:S(2)}) %collective-permute-start.10) | collective-permute-done | bytes 655392 | tf_op jit(solution)/shard_map/ppermute | solution.py:311
  71.1 0.1 pad_maximum_fusion.refs_0_
  71.2 16.2 %update.1 = bf16[24,128,256]{2,1,0:T(8,128)(2,1)} custom-call(bf16[32,80,256]{2,1,0:T(8,128)(2,1)S(1)} %pad_maximum_fusion.refs_0_, bf16[16,128,256]{2,1,0:T(8,128)(2,1)S(1)} %bitcast.29, bf16[8,32,256]{2,1,0:T(8,128)(2,1)S(1)} %saturate.4.refs_2_, bf16[8,32,256]{2,1,0:T(8,128)(2,1)S(1)} %saturate.5.refs_3_, bf16[8,32,256]{2,1,0:T(8,128)(2,1)S(1)} %saturate.6.refs_4_, ...), custom_call_target="tpu_custom_call" | custom-call | tf_op jit(solution)/shard_map/update/pallas_call | solution.py:426
  (47 shorter events, 0.9 us)
Async XLA Ops:
  0.0 12.2 %copy-start = (bf16[54,32]{0,1:T(8,128)(2,1)S(1)}, bf16[54,32]{0,1:T(8,128)(2,1)}, u32[]{:S(2)}) copy-start(bf16[54,32]{0,1:T(8,128)(2,1)} %param.13) | copy-start | bytes 10372
  0.0 12.2 %copy-start.6 = (bf16[54,1152]{1,0:T(8,128)(2,1)S(1)}, bf16[54,1152]{1,0:T(8,128)(2,1)}, u32[]{:S(2)}) copy-start(bf16[54,1152]{1,0:T(8,128)(2,1)} %constant.12.clone) | copy-start | bytes 373252
  0.0 5.7 %copy-start.1 = (bf16[2,2,4,128,256]{4,3,2,1,0:T(8,128)(2,1)S(1)}, bf16[2,2,4,128,256]{4,3,2,1,0:T(8,128)(2,1)}, u32[]{:S(2)}) copy-start(bf16[2,2,4,128,256]{4,3,2,1,0:T(8,128)(2,1)} %param.11) | copy-start | bytes 3145732
  0.0 12.1 %copy-start.9 = (f32[32]{0:T(128)S(1)}, f32[32]{0:T(128)}, u32[]{:S(2)}) copy-start(f32[32]{0:T(128)} %param.14) | copy-start | bytes 388
  2.4 13.4 %collective-permute-start = (bf16[2,1,4,128,256]{4,3,2,1,0:T(8,128)(2,1)}, bf16[2,1,4,128,256]{4,3,2,1,0:T(8,128)(2,1)S(1)}, u32[]{:S(2)}, u32[]{:S(2)}) collective-permute-start(bf16[2,1,4,128,256]{4,3,2,1,0:T(8,128)(2,1)} %get-tuple-element.44), channel_id=1, source_target_pairs={{0,4},{4,8},{8,12},{12,16},{16,20},{20,24},{24,28},{28,0},{1,5},{5... | collective-permute-start | bytes 1572872 | tf_op jit(solution)/shard_map/ppermute | solution.py:302
  2.9 14.5 %collective-permute-start.1 = (bf16[2,1,4,128,256]{4,3,2,1,0:T(8,128)(2,1)}, bf16[2,1,4,128,256]{4,3,2,1,0:T(8,128)(2,1)S(1)}, u32[]{:S(2)}, u32[]{:S(2)}) collective-permute-start(bf16[2,1,4,128,256]{4,3,2,1,0:T(8,128)(2,1)} %get-tuple-element.43), channel_id=1, source_target_pairs={{4,0},{8,4},{12,8},{16,12},{20,16},{24,20},{28,24},{0,28},{5,1},{9... | collective-permute-start | bytes 1572872 | tf_op jit(solution)/shard_map/ppermute | solution.py:302
  6.6 19.3 %collective-permute-start.2 = (bf16[2,2,1,128,256]{4,3,2,1,0:T(8,128)(2,1)}, bf16[2,2,1,128,256]{4,3,2,1,0:T(8,128)(2,1)S(1)}, u32[]{:S(2)}, u32[]{:S(2)}) collective-permute-start(bf16[2,2,1,128,256]{4,3,2,1,0:T(8,128)(2,1)} %get-tuple-element.42), channel_id=1, source_target_pairs={{0,1},{1,2},{2,3},{4,5},{5,6},{6,7},{8,9},{9,10},{10,11},{12,13},{... | collective-permute-start | bytes 786440 | tf_op jit(solution)/shard_map/ppermute | solution.py:302
  10.8 15.1 %collective-permute-start.3 = (bf16[2,2,1,128,256]{4,3,2,1,0:T(8,128)(2,1)}, bf16[2,2,1,128,256]{4,3,2,1,0:T(8,128)(2,1)S(1)}, u32[]{:S(2)}, u32[]{:S(2)}) collective-permute-start(bf16[2,2,1,128,256]{4,3,2,1,0:T(8,128)(2,1)} %get-tuple-element.41), channel_id=1, source_target_pairs={{1,0},{2,1},{3,2},{5,4},{6,5},{7,6},{9,8},{10,9},{11,10},{13,12},{... | collective-permute-start | bytes 786440 | tf_op jit(solution)/shard_map/ppermute | solution.py:302
  13.3 10.3 %copy-start.10 = (f32[32]{0:T(128)S(1)}, f32[32]{0:T(128)}, u32[]{:S(2)}) copy-start(f32[32]{0:T(128)} %param.15) | copy-start | bytes 388
  13.4 11.2 %copy-start.7 = (f32[64]{0:T(128)S(1)}, f32[64]{0:T(128)}, u32[]{:S(2)}) copy-start(f32[64]{0:T(128)} %param.18) | copy-start | bytes 772
  13.5 11.3 %copy-start.8 = (f32[64]{0:T(128)S(1)}, f32[64]{0:T(128)}, u32[]{:S(2)}) copy-start(f32[64]{0:T(128)} %param.17) | copy-start | bytes 772
  13.5 11.4 %copy-start.3 = (s32[2,4,128]{2,1,0:T(4,128)S(1)}, s32[2,4,128]{2,1,0:T(4,128)}, u32[]{:S(2)}) copy-start(s32[2,4,128]{2,1,0:T(4,128)} %param.12) | copy-start | bytes 12292
  13.6 19.4 %copy-start.2 = (bf16[256,256]{1,0:T(8,128)(2,1)S(1)}, bf16[256,256]{1,0:T(8,128)(2,1)}, u32[]{:S(2)}) copy-start(bf16[256,256]{1,0:T(8,128)(2,1)} %constant.13.clone.swap_in) | copy-start | bytes 393220
  13.6 19.4 %copy-start.4 = (s32[64]{0:T(128)S(1)}, s32[64]{0:T(128)}, u32[]{:S(2)}) copy-start(s32[64]{0:T(128)} %cells.1) | copy-start | bytes 772
  18.1 9.5 %collective-permute-start.4 = (bf16[2,2,1,128,256]{4,3,2,1,0:T(8,128)(2,1)}, bf16[2,2,1,128,256]{4,3,2,1,0:T(8,128)(2,1)S(1)}, u32[]{:S(2)}, u32[]{:S(2)}) collective-permute-start(bf16[2,2,1,128,256]{4,3,2,1,0:T(8,128)(2,1)} %pad_maximum_fusion.3), channel_id=1, source_target_pairs={{0,1},{1,2},{2,3},{4,5},{5,6},{6,7},{8,9},{9,10},{10,11},{12,13},{... | collective-permute-start | bytes 786440 | tf_op jit(solution)/shard_map/ppermute | solution.py:302
  22.4 10.6 %collective-permute-start.5 = (bf16[2,2,1,128,256]{4,3,2,1,0:T(8,128)(2,1)}, bf16[2,2,1,128,256]{4,3,2,1,0:T(8,128)(2,1)S(1)}, u32[]{:S(2)}, u32[]{:S(2)}) collective-permute-start(bf16[2,2,1,128,256]{4,3,2,1,0:T(8,128)(2,1)} %pad_maximum_fusion.4), channel_id=1, source_target_pairs={{1,0},{2,1},{3,2},{5,4},{6,5},{7,6},{9,8},{10,9},{11,10},{13,12},{... | collective-permute-start | bytes 786440 | tf_op jit(solution)/shard_map/ppermute | solution.py:302
  33.0 9.5 %copy-start.5 = (bf16[256,256]{1,0:T(8,128)(2,1)S(1)}, bf16[256,256]{1,0:T(8,128)(2,1)}, u32[]{:S(2)}) copy-start(bf16[256,256]{1,0:T(8,128)(2,1)} %constant.14.clone.swap_out) | copy-start | bytes 393220
  39.5 8.1 %collective-permute-start.6 = (bf16[1,80,256]{2,1,0:T(8,128)(2,1)S(1)}, bf16[1,80,256]{2,1,0:T(8,128)(2,1)S(1)}, u32[]{:S(2)}, u32[]{:S(2)}) collective-permute-start(bf16[1,80,256]{2,1,0:T(8,128)(2,1)S(1)} %bitcast.36), channel_id=1, source_target_pairs={{0,2},{1,3},{2,0},{3,1},{4,6},{5,7},{6,4},{7,5},{8,10},{9,11},{10,... | collective-permute-start | bytes 122888 | tf_op jit(solution)/shard_map/ppermute | solution.py:311
  47.6 5.2 %collective-permute-start.7 = (bf16[2,80,256]{2,1,0:T(8,128)(2,1)S(1)}, bf16[2,80,256]{2,1,0:T(8,128)(2,1)S(1)}, u32[]{:S(2)}, u32[]{:S(2)}) collective-permute-start(bf16[2,80,256]{2,1,0:T(8,128)(2,1)S(1)} %pad_maximum_fusion.6), channel_id=1, source_target_pairs={{0,1},{1,0},{2,3},{3,2},{4,5},{5,4},{6,7},{7,6},{8,9},{9,8},{10,11... | collective-permute-start | bytes 245768 | tf_op jit(solution)/shard_map/ppermute | solution.py:311
  52.8 6.7 %collective-permute-start.8 = (bf16[4,80,256]{2,1,0:T(8,128)(2,1)S(1)}, bf16[4,80,256]{2,1,0:T(8,128)(2,1)S(1)}, u32[]{:S(2)}, u32[]{:S(2)}) collective-permute-start(bf16[4,80,256]{2,1,0:T(8,128)(2,1)S(1)} %pad_maximum_fusion.5), channel_id=1, source_target_pairs={{0,8},{4,12},{8,0},{12,4},{16,24},{20,28},{24,16},{28,20},{1,9},{5... | collective-permute-start | bytes 491528 | tf_op jit(solution)/shard_map/ppermute | solution.py:311
  59.6 9.2 %collective-permute-start.9 = (bf16[8,80,256]{2,1,0:T(8,128)(2,1)S(1)}, bf16[8,80,256]{2,1,0:T(8,128)(2,1)S(1)}, u32[]{:S(2)}, u32[]{:S(2)}) collective-permute-start(bf16[8,80,256]{2,1,0:T(8,128)(2,1)S(1)} %pad_maximum_fusion.2), channel_id=1, source_target_pairs={{0,16},{4,20},{8,24},{12,28},{16,0},{20,4},{24,8},{28,12},{1,17},{... | collective-permute-start | bytes 983048 | tf_op jit(solution)/shard_map/ppermute | solution.py:311
  68.9 2.2 %collective-permute-start.10 = (bf16[16,80,256]{2,1,0:T(8,128)(2,1)S(1)}, bf16[16,80,256]{2,1,0:T(8,128)(2,1)S(1)}, u32[]{:S(2)}, u32[]{:S(2)}) collective-permute-start(bf16[16,80,256]{2,1,0:T(8,128)(2,1)S(1)} %pad_maximum_fusion.1), channel_id=1, source_target_pairs={{0,4},{4,0},{8,12},{12,8},{16,20},{20,16},{24,28},{28,24},{1,5},{5... | collective-permute-start | bytes 1966088 | tf_op jit(solution)/shard_map/ppermute | solution.py:311

commit v3 on v2

--- a/solution.py
+++ b/solution.py
@@ -23,9 +23,9 @@
     high = [(f, planes + 1, x + 1) for f in range(2) for x in range(columns)]
     left = [(f, z + 1, 0) for f in range(2) for z in range(planes)]
     right = [(f, z + 1, columns + 1) for f in range(2) for z in range(planes)]
-    corner_left = [(f, z, 0) for f in range(2) for z in (0, planes + 1)]
-    corner_right = [(f, z, columns + 1) for f in range(2) for z in (0, planes + 1)]
-    return own + low + high + left + right + corner_left + corner_right
+    corner_low = [(f, 0, x) for f in range(2) for x in (0, columns + 1)]
+    corner_high = [(f, planes + 1, x) for f in range(2) for x in (0, columns + 1)]
+    return own + low + high + left + right + corner_low + corner_high
 
 
 def tap_selector(planes, columns):
@@ -62,7 +62,7 @@
 
 
 def observe_kernel(
-    own, low, high, left, right, corner_left, corner_right, by_row, swap_in, read_column,
+    own, low, high, left, right, corner_low, corner_high, by_row, swap_in, read_column,
     sigma, values, cells, mask, packed, pay_out, pred
 ):
     lanes, members = own.shape[1], own.shape[2]
@@ -73,7 +73,7 @@
 
     def pack(step, carry):
         at = pl.multiple_of(step * 16, 16)
-        groups = ((own,), (low, high), (left, right, corner_left, corner_right))
+        groups = ((own,), (low, high), (left, right, corner_low, corner_high))
         for g, refs in enumerate(groups):
             parts = [ref[:, pl.ds(at, 16), :] for ref in refs]
             block = parts[0] if len(parts) == 1 else jnp.concatenate(parts, axis=0)
@@ -302,29 +302,6 @@
     return lax.ppermute(value, axis, pairs)
 
 
-def gather_rows(block, steps, packed, saturate):
-    pieces = []
-    for n, (axis, bit) in enumerate(steps):
-        count = lax.axis_size(axis)
-        if n < PIECES:
-            block, packed = lax.optimization_barrier((block, packed))
-        other = lax.ppermute(block, axis, [(i, i ^ bit) for i in range(count)])
-        if n < PIECES:
-            piece = saturate(n, packed)
-        block = jnp.concatenate([block, other], axis=0)
-        if n < PIECES:
-            block, piece = lax.optimization_barrier((block, piece))
-            pieces.append(piece)
-    return block, pieces + [saturate(n, packed) for n in range(len(pieces), PIECES)]
-
-
-def bits_of(axis, count):
-    bits = []
-    while (1 << len(bits)) < count:
-        bits.append((axis, 1 << len(bits)))
-    return bits
-
-
 def vmem():
     return pl.BlockSpec(memory_space=pltpu.VMEM)
 
@@ -341,15 +318,15 @@
     rows = planes * columns
     observed = obs_cells.shape[0]
 
+    left = shift(fields[:, :, -1:], "face", 1, False)
+    right = shift(fields[:, :, :1], "face", -1, False)
     low = shift(fields[:, -1:], "cores", 1, True)
     high = shift(fields[:, :1], "cores", -1, True)
-    left = shift(fields[:, :, -1:], "face", 1, False)
-    right = shift(fields[:, :, :1], "face", -1, False)
-    corner_left = shift(
-        jnp.concatenate([low[:, :, -1:], high[:, :, -1:]], axis=1), "face", 1, False
-    )
-    corner_right = shift(
-        jnp.concatenate([low[:, :, :1], high[:, :, :1]], axis=1), "face", -1, False
+    corner_low = shift(
+        jnp.concatenate([left[:, -1:], right[:, -1:]], axis=2), "cores", 1, True
+    )
+    corner_high = shift(
+        jnp.concatenate([left[:, :1], right[:, :1]], axis=2), "cores", -1, True
     )
 
     selector = tap_selector(planes, columns)
@@ -386,8 +363,8 @@
         compiler_params=params,
         name="observe",
     )(
-        flat(fields), flat(low), flat(high), flat(left), flat(right), flat(corner_left),
-        flat(corner_right), by_row, swap_in, read_half[:, None],
+        flat(fields), flat(low), flat(high), flat(left), flat(right), flat(corner_low),
+        flat(corner_high), by_row, swap_in, read_half[:, None],
         obs_sigma[:, None], obs_values[:, None], obs_cells, mask,
     )
 
@@ -411,10 +388,7 @@
     devices = core_count * face_count
     gathered = devices <= GATHER_DEVICES and devices & (devices - 1) == 0
     if gathered:
-        steps = bits_of("face", face_count)[::-1] + bits_of("cores", core_count)[1:]
-        steps = steps + bits_of("cores", core_count)[:1]
-        block, pieces = gather_rows(pay[None], steps, packed, saturate)
-        terms = (block,)
+        terms = (lax.all_gather(pay, ("cores", "face"), axis=0),)
     else:
         part = pay[:observed]
         gram = lax.dot_general(
@@ -422,7 +396,7 @@
         )
         coeff = jnp.sum(pay[observed:].astype(jnp.float32), axis=0, keepdims=True)
         terms = lax.psum((gram, coeff), ("cores", "face"))
-        pieces = [saturate(n, packed) for n in range(PIECES)]
+    pieces = [saturate(n, packed) for n in range(PIECES)]
     out = pl.pallas_call(
         functools.partial(update_kernel, gathered),
         out_shape=jax.ShapeDtypeStruct((3 * rows, lanes, members), jnp.bfloat16),

time: 87.6 us -> 125 us (1.43)
  waiting for transfers between devices: 16.3 us -> 43.2 us
  between operations: 0.32 us -> 13.6 us
  starting transfers between devices: 19.1 us -> 11.6 us
  local copies, waits for them, and re-layouts: 5.52 us -> 9.65 us
    all_gather x0 -> x1, waiting for transfers between devices: none -> 33.5 us  [shards(): terms = (lax.all_gather(pay, ('cores', 'face'), axis=0),)]
    ppermute x5 -> x0, waiting for transfers between devices: 5.47 us -> none  [gather_rows(): other = lax.ppermute(block, axis, [(i, i ^ bit) for i in range(count)])]
    ppermute x5 -> x0, starting transfers between devices: 5.43 us -> none  [gather_rows(): other = lax.ppermute(block, axis, [(i, i ^ bit) for i in range(count)])]
    unnamed x22 -> x30, local copies, waits for them, and re-layouts: 0.06 us -> 4.91 us
    ppermute x6, starting transfers between devices: 13.6 us -> 11.5 us  [shift(): return lax.ppermute(value, axis, pairs)]
    slice x1, local copies, waits for them, and re-layouts: 2.38 us -> 1.09 us  [shards(): high = shift(fields[:, :1], 'cores', -1, True)]
  transfers between devices with their start and end apart: 11 -> 7, of which waited for: 6 -> 5; matrix products, arithmetic and copies ran while one was open for 7% -> 5% of each run, Pallas kernels for 23% -> 17%
where the time goes in v3:
time: 125 us
  Pallas kernels  44 us (35%)
  waiting for transfers between devices  43.2 us (35%)
  between operations  13.6 us (11%)
  starting transfers between devices  11.6 us (9%)
  local copies, waits for them, and re-layouts  9.65 us (8%)
  other arithmetic  2.61 us (2%)
    all_gather x1, waiting for transfers between devices, shards(): terms = (lax.all_gather(pay, ('cores', 'face'), axis=0),)  33.5 us
    pallas_call x4, Pallas kernels, saturate(): pl.pallas_call(functools.partial(saturate_kernel, n * span), out_shape=ja...  20.7 us
    pallas_call x1, Pallas kernels, shards(): pl.pallas_call(functools.partial(update_kernel, gathered), out_shape=jax....  16.2 us
    ppermute x6, starting transfers between devices, shift(): return lax.ppermute(value, axis, pairs)  11.5 us
    ppermute x6, waiting for transfers between devices, shift(): return lax.ppermute(value, axis, pairs)  9.71 us
    pallas_call x1, Pallas kernels, shards(): pl.pallas_call(observe_kernel, out_shape=(jax.ShapeDtypeStruct((lanes + 2...  7.13 us
    unnamed x30, local copies, waits for them, and re-layouts  4.91 us
  transfers between devices with their start and end apart: 7, of which 5 were waited for; matrix products, arithmetic and copies ran while one was open for 5% of the time, Pallas kernels for 17%

profile of v3, /device:TPU:0, one launch (start us, length us, event | category | flops | bytes accessed | tf_op | source)
XLA Modules:
  0.0 124.8 jit_solution(7225459825648050129)
XLA Ops:
  6.6 1.2 fusion.5
  7.8 4.9 %collective-permute-start.2 = (bf16[2,2,1,128,256]{4,3,2,1,0:T(8,128)(2,1)S(1)}, bf16[2,2,1,128,256]{4,3,2,1,0:T(8,128)(2,1)S(1)}, u32[]{:S(2)}, u32[]{:S(2)}) collective-permute-start(bf16[2,2,1,128,256]{4,3,2,1,0:T(8,128)(2,1)S(1)} %get-tuple-element.10), channel_id=1, source_target_pairs={{0,1},{1,2},{2,3},{4,5},{5,6},{6,7},{8,9},{9,10},{10,11},{12,13},{... | collective-permute-start | bytes 786440 | tf_op jit(solution)/shard_map/ppermute | solution.py:302
  12.7 1.3 %collective-permute-start.3 = (bf16[2,2,1,128,256]{4,3,2,1,0:T(8,128)(2,1)S(1)}, bf16[2,2,1,128,256]{4,3,2,1,0:T(8,128)(2,1)S(1)}, u32[]{:S(2)}, u32[]{:S(2)}) collective-permute-start(bf16[2,2,1,128,256]{4,3,2,1,0:T(8,128)(2,1)S(1)} %get-tuple-element.9), channel_id=1, source_target_pairs={{1,0},{2,1},{3,2},{5,4},{6,5},{7,6},{9,8},{10,9},{11,10},{13,12},{... | collective-permute-start | bytes 786440 | tf_op jit(solution)/shard_map/ppermute | solution.py:302
  14.0 1.1 fusion.6
  15.1 2.6 %collective-permute-start.1 = (bf16[2,1,4,128,256]{4,3,2,1,0:T(8,128)(2,1)}, bf16[2,1,4,128,256]{4,3,2,1,0:T(8,128)(2,1)S(1)}, u32[]{:S(2)}, u32[]{:S(2)}) collective-permute-start(bf16[2,1,4,128,256]{4,3,2,1,0:T(8,128)(2,1)} %get-tuple-element.11), channel_id=1, source_target_pairs={{4,0},{8,4},{12,8},{16,12},{20,16},{24,20},{28,24},{0,28},{5,1},{9... | collective-permute-start | bytes 1572872 | tf_op jit(solution)/shard_map/ppermute | solution.py:302
  17.8 0.1 fusion.1
  18.0 0.2 collective-permute-done.2
  18.3 4.1 %collective-permute-done.3 = bf16[2,2,1,128,256]{4,3,2,1,0:T(8,128)(2,1)S(1)} collective-permute-done((bf16[2,2,1,128,256]{4,3,2,1,0:T(8,128)(2,1)S(1)}, bf16[2,2,1,128,256]{4,3,2,1,0:T(8,128)(2,1)S(1)}, u32[]{:S(2)}, u32[]{:S(2)}) %collective-permute-start.3) | collective-permute-done | bytes 262176 | tf_op jit(solution)/shard_map/ppermute | solution.py:302
  22.4 0.7 pad_maximum_fusion
  23.1 0.7 pad_maximum_fusion.1
  23.9 2.6 %collective-permute-start.5 = (bf16[2,1,2,128,256]{4,3,2,1,0:T(8,128)(2,1)}, bf16[2,1,2,128,256]{4,3,2,1,0:T(8,128)(2,1)S(1)}, u32[]{:S(2)}, u32[]{:S(2)}) collective-permute-start(bf16[2,1,2,128,256]{4,3,2,1,0:T(8,128)(2,1)} %pad_maximum_fusion.1), channel_id=1, source_target_pairs={{4,0},{8,4},{12,8},{16,12},{20,16},{24,20},{28,24},{0,28},{5,1},{9... | collective-permute-start | bytes 786440 | tf_op jit(solution)/shard_map/ppermute | solution.py:302
  26.5 0.1 copy.17
  26.6 0.2 mul.21
  26.9 0.7 copy.18
  27.5 0.1 copy.19.read_column
  27.6 0.1 copy.20.sigma
  27.7 0.1 copy.21.values
  27.9 1.0 maximum_bitcast_fusion.by_row
  28.9 5.2 %collective-permute-done.4 = bf16[2,1,2,128,256]{4,3,2,1,0:T(8,128)(2,1)S(1)} collective-permute-done((bf16[2,1,2,128,256]{4,3,2,1,0:T(8,128)(2,1)}, bf16[2,1,2,128,256]{4,3,2,1,0:T(8,128)(2,1)S(1)}, u32[]{:S(2)}, u32[]{:S(2)}) %collective-permute-start.4) | collective-permute-done | bytes 262176 | tf_op jit(solution)/shard_map/ppermute | solution.py:302
  34.2 0.1 collective-permute-done.5
  34.3 7.1 %observe.1 = (bf16[130,48,256]{2,1,0:T(8,128)(2,1)S(1)}, bf16[80,256]{1,0:T(8,128)(2,1)}) custom-call(bf16[16,128,256]{2,1,0:T(8,128)(2,1)S(1)} %bitcast.28, bf16[8,128,256]{2,1,0:T(8,128)(2,1)S(1)} %bitcast.33, bf16[8,128,256]{2,1,0:T(8,128)(2,1)S(1)} %bitcast.34, bf16[4,128,256]{2,1,0:T(8,128)(2,1)S(1)} %bitcast.31, bf16[4,128,256]{2,1,0:T(8,128)(2,1)S(1)} %bitcast.32, ...), custom_call_target="tpu_custom_call" | custom-call | tf_op jit(solution)/shard_map/observe/pallas_call | solution.py:354
  41.5 1.6 %copy-done.6 = bf16[130,48,256]{2,1,0:T(8,128)(2,1)} copy-done((bf16[130,48,256]{2,1,0:T(8,128)(2,1)}, bf16[130,48,256]{2,1,0:T(8,128)(2,1)S(1)}, u32[]{:S(2)}) %copy-start.6) | copy-done | bytes 3194904
  43.1 1.1 mul.24
  44.2 0.1 maximum_maximum_fusion.weights
  44.4 1.9 %copy-done.7 = bf16[130,48,256]{2,1,0:T(8,128)(2,1)S(1)} copy-done((bf16[130,48,256]{2,1,0:T(8,128)(2,1)S(1)}, bf16[130,48,256]{2,1,0:T(8,128)(2,1)}, u32[]{:S(2)}) %copy-start.7) | copy-done | bytes 3194904
  46.3 5.2 %saturate.5.refs_3_ = bf16[8,32,256]{2,1,0:T(8,128)(2,1)S(1)} custom-call(bf16[130,48,256]{2,1,0:T(8,128)(2,1)S(1)} %copy-done.7, bf16[256,160]{1,0:T(8,128)(2,1)S(1)} %maximum_maximum_fusion.weights, bf16[256,256]{1,0:T(8,128)(2,1)S(1)} %copy-done.8, f32[8,128]{1,0:T(8,128)S(1)} %convert_element_type.5.mask, f32[32]{0:T(128)S(1)} %get-tuple-element.17.read_half), custom_call_target="tpu_custom_call" | custom-call | flops 1073741824 | bytes 4194304 | tf_op jit(solution)/shard_map/saturate/pallas_call | solution.py:372
  51.4 5.2 %saturate.6.refs_4_ = bf16[8,32,256]{2,1,0:T(8,128)(2,1)S(1)} custom-call(bf16[130,48,256]{2,1,0:T(8,128)(2,1)S(1)} %copy-done.7, bf16[256,160]{1,0:T(8,128)(2,1)S(1)} %maximum_maximum_fusion.weights, bf16[256,256]{1,0:T(8,128)(2,1)S(1)} %copy-done.8, f32[8,128]{1,0:T(8,128)S(1)} %convert_element_type.5.mask, f32[32]{0:T(128)S(1)} %get-tuple-element.17.read_half), custom_call_target="tpu_custom_call" | custom-call | flops 1073741824 | bytes 4194304 | tf_op jit(solution)/shard_map/saturate/pallas_call | solution.py:372
  56.6 5.2 %saturate.7.refs_5_ = bf16[8,32,256]{2,1,0:T(8,128)(2,1)S(1)} custom-call(bf16[130,48,256]{2,1,0:T(8,128)(2,1)S(1)} %copy-done.7, bf16[256,160]{1,0:T(8,128)(2,1)S(1)} %maximum_maximum_fusion.weights, bf16[256,256]{1,0:T(8,128)(2,1)S(1)} %copy-done.8, f32[8,128]{1,0:T(8,128)S(1)} %convert_element_type.5.mask, f32[32]{0:T(128)S(1)} %get-tuple-element.17.read_half), custom_call_target="tpu_custom_call" | custom-call | flops 1073741824 | bytes 4194304 | tf_op jit(solution)/shard_map/saturate/pallas_call | solution.py:372
  61.8 5.2 %saturate.4.refs_2_ = bf16[8,32,256]{2,1,0:T(8,128)(2,1)S(1)} custom-call(bf16[130,48,256]{2,1,0:T(8,128)(2,1)S(1)} %copy-done.7, bf16[256,160]{1,0:T(8,128)(2,1)S(1)} %maximum_maximum_fusion.weights, bf16[256,256]{1,0:T(8,128)(2,1)S(1)} %copy-done.8, f32[8,128]{1,0:T(8,128)S(1)} %convert_element_type.5.mask, f32[32]{0:T(128)S(1)} %get-tuple-element.17.read_half), custom_call_target="tpu_custom_call" | custom-call | flops 1073741824 | bytes 4194304 | tf_op jit(solution)/shard_map/saturate/pallas_call | solution.py:372
  67.0 33.5 %all-gather.3.cloned.1.call-done = bf16[2560,256]{1,0:T(8,128)(2,1)} async-done(((bf16[80,256]{1,0:T(8,128)(2,1)}), bf16[2560,256]{1,0:T(8,128)(2,1)}) %all-gather.3.cloned.1.call-update) | async-done | bytes 1310736 | tf_op jit(solution)/shard_map/all_gather | solution.py:391
  100.4 1.3 %copy-done.2 = bf16[2560,256]{1,0:T(8,128)(2,1)S(1)} copy-done((bf16[2560,256]{1,0:T(8,128)(2,1)S(1)}, bf16[2560,256]{1,0:T(8,128)(2,1)}, u32[]{:S(2)}) %copy-start.2) | copy-done | bytes 1310744
  101.7 16.2 %update.1 = bf16[24,128,256]{2,1,0:T(8,128)(2,1)} custom-call(bf16[32,80,256]{2,1,0:T(8,128)(2,1)S(1)} %bitcast.30, bf16[16,128,256]{2,1,0:T(8,128)(2,1)S(1)} %bitcast.29, bf16[8,32,256]{2,1,0:T(8,128)(2,1)S(1)} %saturate.4.refs_2_, bf16[8,32,256]{2,1,0:T(8,128)(2,1)S(1)} %saturate.5.refs_3_, bf16[8,32,256]{2,1,0:T(8,128)(2,1)S(1)} %saturate.6.refs_4_, ...), custom_call_target="tpu_custom_call" | custom-call | tf_op jit(solution)/shard_map/update/pallas_call | solution.py:400
  (43 shorter events, 0.3 us)
Async XLA Ops:
  6.5 11.2 %copy-start = (bf16[54,32]{0,1:T(8,128)(2,1)S(1)}, bf16[54,32]{0,1:T(8,128)(2,1)}, u32[]{:S(2)}) copy-start(bf16[54,32]{0,1:T(8,128)(2,1)} %param.13) | copy-start | bytes 10372
  6.5 7.5 %copy-start.1 = (bf16[2,2,4,128,256]{4,3,2,1,0:T(8,128)(2,1)S(1)}, bf16[2,2,4,128,256]{4,3,2,1,0:T(8,128)(2,1)}, u32[]{:S(2)}) copy-start(bf16[2,2,4,128,256]{4,3,2,1,0:T(8,128)(2,1)} %param.11) | copy-start | bytes 3145732
  6.5 11.2 %copy-start.10 = (bf16[54,1152]{1,0:T(8,128)(2,1)S(1)}, bf16[54,1152]{1,0:T(8,128)(2,1)}, u32[]{:S(2)}) copy-start(bf16[54,1152]{1,0:T(8,128)(2,1)} %constant.12.clone) | copy-start | bytes 373252
  6.5 11.4 %copy-start.13 = (f32[32]{0:T(128)S(1)}, f32[32]{0:T(128)}, u32[]{:S(2)}) copy-start(f32[32]{0:T(128)} %param.14) | copy-start | bytes 388
  6.5 11.4 %copy-start.14 = (f32[32]{0:T(128)S(1)}, f32[32]{0:T(128)}, u32[]{:S(2)}) copy-start(f32[32]{0:T(128)} %param.15) | copy-start | bytes 388
  6.5 93.9 %all-gather.3.cloned.1.call-start = ((), (), s32[]{:S(2)}) async-start(), calls=%async_computation | async-start | bytes 1351680 | tf_op jit(solution)/shard_map/all_gather | solution.py:391
  7.8 10.5 %collective-permute-start.2 = (bf16[2,2,1,128,256]{4,3,2,1,0:T(8,128)(2,1)S(1)}, bf16[2,2,1,128,256]{4,3,2,1,0:T(8,128)(2,1)S(1)}, u32[]{:S(2)}, u32[]{:S(2)}) collective-permute-start(bf16[2,2,1,128,256]{4,3,2,1,0:T(8,128)(2,1)S(1)} %get-tuple-element.10), channel_id=1, source_target_pairs={{0,1},{1,2},{2,3},{4,5},{5,6},{6,7},{8,9},{9,10},{10,11},{12,13},{... | collective-permute-start | bytes 786440 | tf_op jit(solution)/shard_map/ppermute | solution.py:302
  12.7 9.7 %collective-permute-start.3 = (bf16[2,2,1,128,256]{4,3,2,1,0:T(8,128)(2,1)S(1)}, bf16[2,2,1,128,256]{4,3,2,1,0:T(8,128)(2,1)S(1)}, u32[]{:S(2)}, u32[]{:S(2)}) collective-permute-start(bf16[2,2,1,128,256]{4,3,2,1,0:T(8,128)(2,1)S(1)} %get-tuple-element.9), channel_id=1, source_target_pairs={{1,0},{2,1},{3,2},{5,4},{6,5},{7,6},{9,8},{10,9},{11,10},{13,12},{... | collective-permute-start | bytes 786440 | tf_op jit(solution)/shard_map/ppermute | solution.py:302
  15.1 12.5 %copy-start.11 = (f32[64]{0:T(128)S(1)}, f32[64]{0:T(128)}, u32[]{:S(2)}) copy-start(f32[64]{0:T(128)} %param.18) | copy-start | bytes 772
  15.1 12.6 %copy-start.12 = (f32[64]{0:T(128)S(1)}, f32[64]{0:T(128)}, u32[]{:S(2)}) copy-start(f32[64]{0:T(128)} %param.17) | copy-start | bytes 772
  15.1 19.2 %collective-permute-start = (bf16[2,1,4,128,256]{4,3,2,1,0:T(8,128)(2,1)}, bf16[2,1,4,128,256]{4,3,2,1,0:T(8,128)(2,1)S(1)}, u32[]{:S(2)}, u32[]{:S(2)}) collective-permute-start(bf16[2,1,4,128,256]{4,3,2,1,0:T(8,128)(2,1)} %get-tuple-element.12), channel_id=1, source_target_pairs={{0,4},{4,8},{8,12},{12,16},{16,20},{20,24},{24,28},{28,0},{1,5},{5... | collective-permute-start | bytes 1572872 | tf_op jit(solution)/shard_map/ppermute | solution.py:302
  15.1 19.2 %collective-permute-start.1 = (bf16[2,1,4,128,256]{4,3,2,1,0:T(8,128)(2,1)}, bf16[2,1,4,128,256]{4,3,2,1,0:T(8,128)(2,1)S(1)}, u32[]{:S(2)}, u32[]{:S(2)}) collective-permute-start(bf16[2,1,4,128,256]{4,3,2,1,0:T(8,128)(2,1)} %get-tuple-element.11), channel_id=1, source_target_pairs={{4,0},{8,4},{12,8},{16,12},{20,16},{24,20},{28,24},{0,28},{5,1},{9... | collective-permute-start | bytes 1572872 | tf_op jit(solution)/shard_map/ppermute | solution.py:302
  17.9 9.6 %copy-start.9 = (bf16[32,1152]{1,0:T(8,128)(2,1)}, bf16[32,1152]{1,0:T(8,128)(2,1)S(1)}, u32[]{:S(2)}) copy-start(bf16[32,1152]{1,0:T(8,128)(2,1)S(1)} %fusion.1) | copy-start | bytes 221188
  17.9 16.4 %copy-start.3 = (bf16[256,256]{1,0:T(8,128)(2,1)S(1)}, bf16[256,256]{1,0:T(8,128)(2,1)}, u32[]{:S(2)}) copy-start(bf16[256,256]{1,0:T(8,128)(2,1)} %constant.13.clone.swap_in) | copy-start | bytes 393220
  17.9 16.4 %copy-start.4 = (s32[2,4,128]{2,1,0:T(4,128)S(1)}, s32[2,4,128]{2,1,0:T(4,128)}, u32[]{:S(2)}) copy-start(s32[2,4,128]{2,1,0:T(4,128)} %param.12) | copy-start | bytes 12292
  18.0 16.4 %copy-start.5 = (s32[64]{0:T(128)S(1)}, s32[64]{0:T(128)}, u32[]{:S(2)}) copy-start(s32[64]{0:T(128)} %cells.1) | copy-start | bytes 772
  23.1 11.0 %collective-permute-start.4 = (bf16[2,1,2,128,256]{4,3,2,1,0:T(8,128)(2,1)}, bf16[2,1,2,128,256]{4,3,2,1,0:T(8,128)(2,1)S(1)}, u32[]{:S(2)}, u32[]{:S(2)}) collective-permute-start(bf16[2,1,2,128,256]{4,3,2,1,0:T(8,128)(2,1)} %pad_maximum_fusion), channel_id=1, source_target_pairs={{0,4},{4,8},{8,12},{12,16},{16,20},{20,24},{24,28},{28,0},{1,5},{5... | collective-permute-start | bytes 786440 | tf_op jit(solution)/shard_map/ppermute | solution.py:302
  23.9 10.4 %collective-permute-start.5 = (bf16[2,1,2,128,256]{4,3,2,1,0:T(8,128)(2,1)}, bf16[2,1,2,128,256]{4,3,2,1,0:T(8,128)(2,1)S(1)}, u32[]{:S(2)}, u32[]{:S(2)}) collective-permute-start(bf16[2,1,2,128,256]{4,3,2,1,0:T(8,128)(2,1)} %pad_maximum_fusion.1), channel_id=1, source_target_pairs={{4,0},{8,4},{12,8},{16,12},{20,16},{24,20},{28,24},{0,28},{5,1},{9... | collective-permute-start | bytes 786440 | tf_op jit(solution)/shard_map/ppermute | solution.py:302
  34.3 10.0 %copy-start.8 = (bf16[256,256]{1,0:T(8,128)(2,1)S(1)}, bf16[256,256]{1,0:T(8,128)(2,1)}, u32[]{:S(2)}) copy-start(bf16[256,256]{1,0:T(8,128)(2,1)} %constant.14.clone.swap_out) | copy-start | bytes 393220
  41.5 1.6 %copy-start.6 = (bf16[130,48,256]{2,1,0:T(8,128)(2,1)}, bf16[130,48,256]{2,1,0:T(8,128)(2,1)S(1)}, u32[]{:S(2)}) copy-start(bf16[130,48,256]{2,1,0:T(8,128)(2,1)S(1)} %get-tuple-element.8.packed) | copy-start | bytes 9584644
  44.4 1.9 %copy-start.7 = (bf16[130,48,256]{2,1,0:T(8,128)(2,1)S(1)}, bf16[130,48,256]{2,1,0:T(8,128)(2,1)}, u32[]{:S(2)}) copy-start(bf16[130,48,256]{2,1,0:T(8,128)(2,1)} %copy-done.6) | copy-start | bytes 9584644
  100.4 1.3 %copy-start.2 = (bf16[2560,256]{1,0:T(8,128)(2,1)S(1)}, bf16[2560,256]{1,0:T(8,128)(2,1)}, u32[]{:S(2)}) copy-start(bf16[2560,256]{1,0:T(8,128)(2,1)} %all-gather.3.cloned.1.call-done) | copy-start | bytes 3932164
Sparse Core Ops, SparseCore 0:
  43.2 57.1 all-gather.2

commit v4 on v2

--- a/solution.py
+++ b/solution.py
@@ -23,9 +23,10 @@
     high = [(f, planes + 1, x + 1) for f in range(2) for x in range(columns)]
     left = [(f, z + 1, 0) for f in range(2) for z in range(planes)]
     right = [(f, z + 1, columns + 1) for f in range(2) for z in range(planes)]
-    corner_left = [(f, z, 0) for f in range(2) for z in (0, planes + 1)]
-    corner_right = [(f, z, columns + 1) for f in range(2) for z in (0, planes + 1)]
-    return own + low + high + left + right + corner_left + corner_right
+    corners = [
+        (f, z, x) for x in (0, columns + 1) for z in (0, planes + 1) for f in range(2)
+    ]
+    return own + low + high + left + right + corners
 
 
 def tap_selector(planes, columns):
@@ -62,7 +63,7 @@
 
 
 def observe_kernel(
-    own, low, high, left, right, corner_left, corner_right, by_row, swap_in, read_column,
+    own, low, high, left, right, low_left, high_left, low_right, high_right, by_row, swap_in, read_column,
     sigma, values, cells, mask, packed, pay_out, pred
 ):
     lanes, members = own.shape[1], own.shape[2]
@@ -71,9 +72,9 @@
     packed[0] = jnp.zeros((count, members), jnp.bfloat16)
     packed[lanes + 1] = jnp.zeros((count, members), jnp.bfloat16)
 
-    def pack(step, carry):
-        at = pl.multiple_of(step * 16, 16)
-        groups = ((own,), (low, high), (left, right, corner_left, corner_right))
+    for step in range(lanes // 16):
+        at = step * 16
+        groups = ((own,), (low, high), (left, right, low_left, high_left, low_right, high_right))
         for g, refs in enumerate(groups):
             parts = [ref[:, pl.ds(at, 16), :] for ref in refs]
             block = parts[0] if len(parts) == 1 else jnp.concatenate(parts, axis=0)
@@ -83,15 +84,13 @@
             packed[pl.ds(at + 1, 16), 16 * g : 16 * g + 16, :] = (
                 moved.astype(jnp.bfloat16).reshape(16, 16, members)
             )
-        return carry
-
-    lax.fori_loop(0, lanes // 16, pack, 0)
+
     ones = ones_rows(members)
     read = jnp.broadcast_to(read_column[...], (read_column.shape[0], members))
 
     def some_cells(step, carry):
-        for k in range(4):
-            o = step * 4 + k
+        for k in range(16):
+            o = step * 16 + k
             cell = cells[o]
             row, y = cell // lanes, cell % lanes
             taps = jnp.concatenate(
@@ -103,7 +102,7 @@
             pred[pl.ds(o, 1), :] = found.astype(jnp.bfloat16).astype(jnp.float32)
         return carry
 
-    lax.fori_loop(0, observed // 4, some_cells, 0)
+    lax.fori_loop(0, observed // 16, some_cells, 0)
 
     root_count = math.sqrt(members - 1)
     predicted = pred[...]
@@ -121,17 +120,19 @@
     pay_out[observed : observed + PAY_ROWS, :] = tail.astype(jnp.bfloat16)
 
 
-def saturate_kernel(start, packed, weights, swap_out, mask, read_half, sat_out, sat_rows):
-    rows, span, members = sat_out.shape
+def saturate_kernel(
+    start, packed, weights, swap_out, mask, read_half, anomaly_out, mean_out, sat_rows
+):
+    rows, span, members = anomaly_out.shape
     count = packed.shape[1]
     channels = read_half.shape[0]
     ones = ones_rows(members)
     lane_index = lax.broadcasted_iota(jnp.int32, mask.shape, 1)
 
-    def two_rows(step, carry):
+    def some_rows(step, carry):
         found = []
-        for k in range(2):
-            y = start + step * 2 + k
+        for k in range(8):
+            y = start + step * 8 + k
             taps = jnp.concatenate(
                 [packed[pl.ds(y, 3)].reshape(3 * count, members), ones], axis=0
             )
@@ -142,13 +143,26 @@
                 total = total + read_half[c] * (part * (1.0 + jnp.tanh(part)))
             here = jnp.sum(jnp.where(lane_index == y, mask[...], 0.0), axis=1, keepdims=True)
             found.append(here * (0.5 + 0.5 * jnp.tanh(total)))
-        at = pl.multiple_of(step * 2 * rows, 2 * rows)
-        sat_rows[pl.ds(at, 2 * rows), :] = jnp.concatenate(found, axis=0).astype(jnp.bfloat16)
+        at = pl.multiple_of(step * 8 * rows, 8 * rows)
+        sat_rows[pl.ds(at, 8 * rows), :] = jnp.concatenate(found, axis=0).astype(jnp.bfloat16)
         return carry
 
-    lax.fori_loop(0, span // 2, two_rows, 0)
+    lax.fori_loop(0, span // 8, some_rows, 0)
     moved = jnp.dot(swap_out[...], sat_rows[...], preferred_element_type=jnp.float32)
-    sat_out[...] = moved.astype(jnp.bfloat16).reshape(rows, span, members)
+    mean = jnp.mean(moved, axis=1, keepdims=True)
+    anomaly_out[...] = (moved - mean).astype(jnp.bfloat16).reshape(rows, span, members)
+    mean_out[...] = mean.reshape(rows, span, 1)
+
+
+def moments_kernel(fields, anomaly_out, mean_out):
+    def step(n, carry):
+        state = fields[pl.ds(2 * n, 2)].astype(jnp.float32)
+        mean = jnp.mean(state, axis=2, keepdims=True)
+        anomaly_out[pl.ds(2 * n, 2)] = (state - mean).astype(jnp.bfloat16)
+        mean_out[pl.ds(2 * n, 2)] = mean
+        return carry
+
+    lax.fori_loop(0, fields.shape[0] // 2, step, 0)
 
 
 def transposed_dot(a, b, precision):
@@ -230,8 +244,8 @@
         pay, refs = refs[0], refs[1:]
     else:
         gram, coeff_in, refs = refs[0], refs[1], refs[2:]
-    fields, sats, (out, joint, mixing) = refs[0], refs[1:-3], refs[-3:]
-    members = fields.shape[2]
+    moments, (out, joint, mixing) = refs[:-3], refs[-3:]
+    members = out.shape[2]
     sub = lax.broadcasted_iota(jnp.int32, (members, members), 0)
     lane = lax.broadcasted_iota(jnp.int32, (members, members), 1)
     identity = jnp.where(sub == lane, 1.0, 0.0)
@@ -270,27 +284,27 @@
     weight = jnp.dot(half, inverse, preferred_element_type=jnp.float32, precision=HIGHEST)
     mixing[...] = jnp.transpose(inverse + weight[0:1, :]).astype(jnp.bfloat16)
 
-    def blend(state):
-        state = state.astype(jnp.float32)
-        mean = jnp.mean(state, axis=1, keepdims=True)
-        anomalies = (state - mean).astype(jnp.bfloat16)
-        moved = jnp.dot(anomalies, mixing[...], preferred_element_type=jnp.float32)
-        return (mean + moved).astype(jnp.bfloat16)
-
-    field_rows, lanes = fields.shape[0], fields.shape[1]
+    def blend(anomalies, mean):
+        outer, inner = anomalies.shape[0], anomalies.shape[1]
+        moved = jnp.dot(
+            anomalies.reshape(outer * inner, members), mixing[...], preferred_element_type=jnp.float32
+        )
+        return (mean + moved.reshape(outer, inner, members)).astype(jnp.bfloat16)
+
+    anomalies, mean = moments[:2]
+    field_rows = anomalies.shape[0]
 
     def step(n, carry):
-        at = pl.multiple_of(2 * n, 2)
-        block = fields[pl.ds(at, 2)].reshape(2 * lanes, members)
-        out[pl.ds(at, 2)] = blend(block).reshape(2, lanes, members)
+        for k in range(2):
+            at = 4 * n + 2 * k
+            out[pl.ds(at, 2)] = blend(anomalies[pl.ds(at, 2)], mean[pl.ds(at, 2)])
         return carry
 
-    lax.fori_loop(0, field_rows // 2, step, 0)
-    for n, sat in enumerate(sats):
-        rows, span = sat.shape[0], sat.shape[1]
-        out[field_rows:, n * span : (n + 1) * span, :] = blend(
-            sat[...].reshape(rows * span, members)
-        ).reshape(rows, span, members)
+    lax.fori_loop(0, field_rows // 4, step, 0)
+    for n in range(1, len(moments) // 2):
+        anomalies, mean = moments[2 * n : 2 * n + 2]
+        span = anomalies.shape[1]
+        out[field_rows:, (n - 1) * span : n * span, :] = blend(anomalies[...], mean[...])
 
 
 def shift(value, axis, by, closed):
@@ -300,6 +314,17 @@
     else:
         pairs = [((i + 1) % count, i) for i in range(count if closed else count - 1)]
     return lax.ppermute(value, axis, pairs)
+
+
+def shift_both(value, core_by, face_by):
+    core_count, face_count = lax.axis_size("cores"), lax.axis_size("face")
+    pairs = [
+        (i * face_count + j, ((i + core_by) % core_count) * face_count + j + face_by)
+        for i in range(core_count)
+        for j in range(face_count)
+        if 0 <= j + face_by < face_count
+    ]
+    return lax.ppermute(value, ("cores", "face"), pairs)
 
 
 def gather_rows(block, steps, packed, saturate):
@@ -333,6 +358,13 @@
     return pl.BlockSpec(memory_space=pltpu.SMEM)
 
 
+def moments_shape(outer, inner, members):
+    return (
+        jax.ShapeDtypeStruct((outer, inner, members), jnp.bfloat16),
+        jax.ShapeDtypeStruct((outer, inner, 1), jnp.float32),
+    )
+
+
 def shards(
     fields, pore_mask, conv_kernel, conv_bias, read_weight, obs_cells, obs_values, obs_sigma
 ):
@@ -343,14 +375,12 @@
 
     low = shift(fields[:, -1:], "cores", 1, True)
     high = shift(fields[:, :1], "cores", -1, True)
+    low_left = shift_both(fields[:, -1:, -1:], 1, 1)
+    high_left = shift_both(fields[:, :1, -1:], -1, 1)
+    low_right = shift_both(fields[:, -1:, :1], 1, -1)
+    high_right = shift_both(fields[:, :1, :1], -1, -1)
     left = shift(fields[:, :, -1:], "face", 1, False)
     right = shift(fields[:, :, :1], "face", -1, False)
-    corner_left = shift(
-        jnp.concatenate([low[:, :, -1:], high[:, :, -1:]], axis=1), "face", 1, False
-    )
-    corner_right = shift(
-        jnp.concatenate([low[:, :, :1], high[:, :, :1]], axis=1), "face", -1, False
-    )
 
     selector = tap_selector(planes, columns)
     count = selector.shape[2] // 3
@@ -380,23 +410,23 @@
             jax.ShapeDtypeStruct((lanes + 2, count, members), jnp.bfloat16),
             jax.ShapeDtypeStruct((observed + PAY_ROWS, members), jnp.bfloat16),
         ),
-        in_specs=[vmem()] * 12 + [smem()] * 2,
+        in_specs=[vmem()] * 14 + [smem()] * 2,
         out_specs=(vmem(), vmem()),
         scratch_shapes=[pltpu.VMEM((observed, members), jnp.float32)],
         compiler_params=params,
         name="observe",
     )(
-        flat(fields), flat(low), flat(high), flat(left), flat(right), flat(corner_left),
-        flat(corner_right), by_row, swap_in, read_half[:, None],
+        flat(fields), flat(low), flat(high), flat(left), flat(right), flat(low_left),
+        flat(high_left), flat(low_right), flat(high_right), by_row, swap_in, read_half[:, None],
         obs_sigma[:, None], obs_values[:, None], obs_cells, mask,
     )
 
     def saturate(n, packed):
         return pl.pallas_call(
             functools.partial(saturate_kernel, n * span),
-            out_shape=jax.ShapeDtypeStruct((rows, span, members), jnp.bfloat16),
+            out_shape=moments_shape(rows, span, members),
             in_specs=[vmem()] * 4 + [smem()],
-            out_specs=vmem(),
+            out_specs=(vmem(), vmem()),
             scratch_shapes=[pltpu.VMEM((rows * span, members), jnp.bfloat16)],
             compiler_params=params,
             cost_estimate=pl.CostEstimate(
@@ -407,6 +437,14 @@
             name="saturate",
         )(packed, weights, swap_out, mask_float, read_half)
 
+    field_moments = pl.pallas_call(
+        moments_kernel,
+        out_shape=moments_shape(2 * rows, lanes, members),
+        in_specs=[vmem()],
+        out_specs=(vmem(), vmem()),
+        compiler_params=params,
+        name="moments",
+    )(flat(fields))
     core_count, face_count = lax.axis_size("cores"), lax.axis_size("face")
     devices = core_count * face_count
     gathered = devices <= GATHER_DEVICES and devices & (devices - 1) == 0
@@ -426,7 +464,7 @@
     out = pl.pallas_call(
         functools.partial(update_kernel, gathered),
         out_shape=jax.ShapeDtypeStruct((3 * rows, lanes, members), jnp.bfloat16),
-        in_specs=[vmem()] * (len(terms) + 1 + PIECES),
+        in_specs=[vmem()] * (len(terms) + 2 + 2 * PIECES),
         out_specs=vmem(),
         scratch_shapes=[
             pltpu.VMEM((members, 2 * members), jnp.float32),
@@ -434,7 +472,7 @@
         ],
         compiler_params=params,
         name="update",
-    )(*terms, flat(fields), *pieces)
+    )(*terms, *field_moments, *(part for piece in pieces for part in piece))
     return out.reshape(3, planes, columns, lanes, members)
 
 

time: 87.6 us -> 78.6 us (0.90)
  Pallas kernels: 43.1 us -> 32.5 us
  starting transfers between devices: 19.1 us -> 28 us
  waiting for transfers between devices: 16.3 us -> 12.1 us
  other arithmetic: 2.87 us -> 0.45 us
    ppermute x0 -> x4, starting transfers between devices: none -> 13.9 us  [shift_both(): return lax.ppermute(value, ('cores', 'face'), pairs)]
    ppermute x6 -> x4, waiting for transfers between devices: 10.8 us -> 0.01 us  [shift(): return lax.ppermute(value, axis, pairs)]
    pallas_call x4 -> x5, Pallas kernels: 20.4 us -> 14 us  [the longest x4 13.1 us: saturate(): pl.pallas_call(functools.partial(saturate_kernel, n * span), out_shape=mo...]
    ppermute x6 -> x4, starting transfers between devices: 13.6 us -> 7.65 us  [shift(): return lax.ppermute(value, axis, pairs)]
    ppermute x0 -> x4, waiting for transfers between devices: none -> 5.17 us  [shift_both(): return lax.ppermute(value, ('cores', 'face'), pairs)]
    pallas_call x1, Pallas kernels: 6.51 us -> 3.38 us  [shards(): pl.pallas_call(observe_kernel, out_shape=(jax.ShapeDtypeStruct((lanes + 2...]
    unnamed x22 -> x23, local copies, waits for them, and re-layouts: 0.06 us -> 1.97 us
    ppermute x5, waiting for transfers between devices: 5.47 us -> 6.96 us  [gather_rows(): other = lax.ppermute(block, axis, [(i, i ^ bit) for i in range(count)])]
  transfers between devices with their start and end apart: 11 -> 13, of which waited for: 6 -> 4; matrix products, arithmetic and copies ran while one was open for 7% -> 4% of each run, Pallas kernels for 23% -> 18%
where the time goes in v4:
time: 78.6 us; the launch traced here: 78.4 us
  Pallas kernels  32.5 us (41%)
  starting transfers between devices  28 us (36%)
  waiting for transfers between devices  12.1 us (15%)
  local copies, waits for them, and re-layouts  4.78 us (6%)
    pallas_call x1, Pallas kernels, shards(): pl.pallas_call(functools.partial(update_kernel, gathered), out_shape=jax....  15.1 us
    ppermute x4, starting transfers between devices, shift_both(): return lax.ppermute(value, ('cores', 'face'), pairs)  13.9 us
    pallas_call x4, Pallas kernels, saturate(): pl.pallas_call(functools.partial(saturate_kernel, n * span), out_shape=mo...  13.1 us
    ppermute x4, starting transfers between devices, shift(): return lax.ppermute(value, axis, pairs)  7.65 us
    ppermute x5, waiting for transfers between devices, gather_rows(): other = lax.ppermute(block, axis, [(i, i ^ bit) for i in range(count)])  6.96 us
    ppermute x5, starting transfers between devices, gather_rows(): other = lax.ppermute(block, axis, [(i, i ^ bit) for i in range(count)])  6.46 us
    ppermute x4, waiting for transfers between devices, shift_both(): return lax.ppermute(value, ('cores', 'face'), pairs)  5.17 us
    pallas_call x1, Pallas kernels, shards(): pl.pallas_call(observe_kernel, out_shape=(jax.ShapeDtypeStruct((lanes + 2...  3.38 us
  transfers between devices with their start and end apart: 13, of which 4 were waited for; matrix products, arithmetic and copies ran while one was open for 4% of the time, Pallas kernels for 18%

profile of v4, /device:TPU:0, one launch (start us, length us, event | category | flops | bytes accessed | tf_op | source)
XLA Modules:
  0.0 78.4 jit_solution(8765141471017552040)
XLA Ops:
  0.0 1.9 %slice_bitcast_fusion = (bf16[2,1,1,128,256]{4,3,0,2,1:T(8,128)(2,1)S(1)}, bf16[2,1,1,128,256]{4,3,0,2,1:T(8,128)(2,1)S(1)}, bf16[2,1,1,128,256]{4,3,0,2,1:T(8,128)(2,1)}, bf16[2,1,1,128,256]{4,3,0,2,1:T(8,128)(2,1)}) fusion(bf16[2,2,4,128,256]{4,3,2,1,0:T(8,128)(2,1)} %param.11), kind=kLoop, calls=%fused_computation.9 | loop fusion | bytes 1048576
  1.9 1.3 %collective-permute-start.7 = (bf16[2,1,1,128,256]{4,3,0,2,1:T(8,128)(2,1)S(1)}, bf16[2,1,1,128,256]{4,3,0,2,1:T(8,128)(2,1)S(1)}, u32[]{:S(2)}, u32[]{:S(2)}) collective-permute-start(bf16[2,1,1,128,256]{4,3,0,2,1:T(8,128)(2,1)S(1)} %get-tuple-element.69), channel_id=1, source_target_pairs={{1,28},{2,29},{3,30},{5,0},{6,1},{7,2},{9,4},{10,5},{11,6},{13,8},... | collective-permute-start | bytes 393224 | tf_op jit(solution)/shard_map/ppermute | solution.py:327
  3.2 1.3 %collective-permute-start.6 = (bf16[2,1,1,128,256]{4,3,0,2,1:T(8,128)(2,1)S(1)}, bf16[2,1,1,128,256]{4,3,0,2,1:T(8,128)(2,1)S(1)}, u32[]{:S(2)}, u32[]{:S(2)}) collective-permute-start(bf16[2,1,1,128,256]{4,3,0,2,1:T(8,128)(2,1)S(1)} %get-tuple-element.70), channel_id=1, source_target_pairs={{1,4},{2,5},{3,6},{5,8},{6,9},{7,10},{9,12},{10,13},{11,14},{13,16... | collective-permute-start | bytes 393224 | tf_op jit(solution)/shard_map/ppermute | solution.py:327
  4.5 8.4 %collective-permute-start.5 = (bf16[2,1,1,128,256]{4,3,0,2,1:T(8,128)(2,1)}, bf16[2,1,1,128,256]{4,3,0,2,1:T(8,128)(2,1)S(1)}, u32[]{:S(2)}, u32[]{:S(2)}) collective-permute-start(bf16[2,1,1,128,256]{4,3,0,2,1:T(8,128)(2,1)} %get-tuple-element.71), channel_id=1, source_target_pairs={{0,29},{1,30},{2,31},{4,1},{5,2},{6,3},{8,5},{9,6},{10,7},{12,9},{... | collective-permute-start | bytes 393224 | tf_op jit(solution)/shard_map/ppermute | solution.py:327
  12.9 1.1 %fusion.6 = (bf16[2,1,4,128,256]{4,3,2,1,0:T(8,128)(2,1)}, bf16[2,1,4,128,256]{4,3,2,1,0:T(8,128)(2,1)}) fusion(bf16[2,2,4,128,256]{4,3,2,1,0:T(8,128)(2,1)S(1)} %copy-done.1), kind=kLoop, calls=%fused_computation.25 | loop fusion | bytes 2097152 | tf_op jit(solution)/shard_map/slice | solution.py:377
  14.0 0.2 collective-permute-start.1
  14.2 0.4 collective-permute-start
  14.6 0.8 %fusion.5 = (bf16[2,2,1,128,256]{4,3,2,1,0:T(8,128)(2,1)}, bf16[2,2,1,128,256]{4,3,2,1,0:T(8,128)(2,1)}) fusion(bf16[2,2,4,128,256]{4,3,2,1,0:T(8,128)(2,1)S(1)} %copy-done.1), kind=kLoop, calls=%fused_computation.24 | loop fusion | bytes 1048576 | tf_op jit(solution)/shard_map/slice | solution.py:383
  15.4 0.1 copy.25
  15.6 0.1 fusion.1
  15.7 0.2 mul.24
  16.1 1.3 %collective-permute-start.3 = (bf16[2,2,1,128,256]{4,3,2,1,0:T(8,128)(2,1)}, bf16[2,2,1,128,256]{4,3,2,1,0:T(8,128)(2,1)S(1)}, u32[]{:S(2)}, u32[]{:S(2)}) collective-permute-start(bf16[2,2,1,128,256]{4,3,2,1,0:T(8,128)(2,1)} %get-tuple-element.73), channel_id=1, source_target_pairs={{1,0},{2,1},{3,2},{5,4},{6,5},{7,6},{9,8},{10,9},{11,10},{13,12},{... | collective-permute-start | bytes 786440 | tf_op jit(solution)/shard_map/ppermute | solution.py:316
  17.4 5.8 %collective-permute-start.2 = (bf16[2,2,1,128,256]{4,3,2,1,0:T(8,128)(2,1)}, bf16[2,2,1,128,256]{4,3,2,1,0:T(8,128)(2,1)S(1)}, u32[]{:S(2)}, u32[]{:S(2)}) collective-permute-start(bf16[2,2,1,128,256]{4,3,2,1,0:T(8,128)(2,1)} %get-tuple-element.74), channel_id=1, source_target_pairs={{0,1},{1,2},{2,3},{4,5},{5,6},{6,7},{8,9},{9,10},{10,11},{12,13},{... | collective-permute-start | bytes 786440 | tf_op jit(solution)/shard_map/ppermute | solution.py:316
  23.3 0.2 mul.21
  23.6 0.1 copy.29.values
  23.7 0.1 copy.28.sigma
  23.8 3.0 %collective-permute-start.4 = (bf16[2,1,1,128,256]{4,3,0,2,1:T(8,128)(2,1)}, bf16[2,1,1,128,256]{4,3,0,2,1:T(8,128)(2,1)S(1)}, u32[]{:S(2)}, u32[]{:S(2)}) collective-permute-start(bf16[2,1,1,128,256]{4,3,0,2,1:T(8,128)(2,1)} %get-tuple-element.72), channel_id=1, source_target_pairs={{0,5},{1,6},{2,7},{4,9},{5,10},{6,11},{8,13},{9,14},{10,15},{12,17... | collective-permute-start | bytes 393224 | tf_op jit(solution)/shard_map/ppermute | solution.py:327
  26.9 5.2 %collective-permute-done.4 = bf16[2,1,1,128,256]{4,3,0,2,1:T(8,128)(2,1)S(1)} collective-permute-done((bf16[2,1,1,128,256]{4,3,0,2,1:T(8,128)(2,1)}, bf16[2,1,1,128,256]{4,3,0,2,1:T(8,128)(2,1)S(1)}, u32[]{:S(2)}, u32[]{:S(2)}) %collective-permute-start.4) | collective-permute-done | bytes 131104 | tf_op jit(solution)/shard_map/ppermute | solution.py:327
  32.1 3.4 %observe.1 = (bf16[130,48,256]{2,1,0:T(8,128)(2,1)S(1)}, bf16[80,256]{1,0:T(8,128)(2,1)S(1)}) custom-call(bf16[16,128,256]{2,1,0:T(8,128)(2,1)S(1)} %bitcast.38, bf16[8,128,256]{2,1,0:T(8,128)(2,1)S(1)} %bitcast.41, bf16[8,128,256]{2,1,0:T(8,128)(2,1)S(1)} %bitcast.40, bf16[4,128,256]{2,1,0:T(8,128)(2,1)S(1)} %bitcast.43, bf16[4,128,256]{2,1,0:T(8,128)(2,1)S(1)} %bitcast.42, ...), custom_call_target="tpu_custom_call" | custom-call | tf_op jit(solution)/shard_map/observe/pallas_call | solution.py:407
  35.5 4.4 %collective-permute-start.8 = (bf16[1,80,256]{2,1,0:T(8,128)(2,1)S(1)}, bf16[1,80,256]{2,1,0:T(8,128)(2,1)S(1)}, u32[]{:S(2)}, u32[]{:S(2)}) collective-permute-start(bf16[1,80,256]{2,1,0:T(8,128)(2,1)S(1)} %bitcast.48), channel_id=1, source_target_pairs={{0,2},{1,3},{2,0},{3,1},{4,6},{5,7},{6,4},{7,5},{8,10},{9,11},{10,... | collective-permute-start | bytes 122888 | tf_op jit(solution)/shard_map/ppermute | solution.py:336
  39.9 3.3 %saturate.4 = (bf16[8,32,256]{2,1,0:T(8,128)(2,1)S(1)}, f32[8,32,1]{2,1,0:T(8,128)S(1)}) custom-call(bf16[130,48,256]{2,1,0:T(8,128)(2,1)S(1)} %get-tuple-element.55.packed, bf16[256,160]{1,0:T(8,128)(2,1)S(1)} %maximum_maximum_fusion.weights, bf16[256,256]{1,0:T(8,128)(2,1)S(1)} %copy-done.5, f32[8,128]{1,0:T(8,128)S(1)} %convert_element_type.5.mask, ...), custom_call_target="tpu_custom_call" | custom-call | flops 1073741824 | bytes 4194304 | tf_op jit(solution)/shard_map/saturate/pallas_call | solution.py:425
  43.2 1.3 %collective-permute-start.9 = (bf16[2,80,256]{2,1,0:T(8,128)(2,1)S(1)}, bf16[2,80,256]{2,1,0:T(8,128)(2,1)S(1)}, u32[]{:S(2)}, u32[]{:S(2)}) collective-permute-start(bf16[2,80,256]{2,1,0:T(8,128)(2,1)S(1)} %pad_maximum_fusion.4), channel_id=1, source_target_pairs={{0,1},{1,0},{2,3},{3,2},{4,5},{5,4},{6,7},{7,6},{8,9},{9,8},{10,11... | collective-permute-start | bytes 245768 | tf_op jit(solution)/shard_map/ppermute | solution.py:336
  44.5 3.3 %saturate.5 = (bf16[8,32,256]{2,1,0:T(8,128)(2,1)S(1)}, f32[8,32,1]{2,1,0:T(8,128)S(1)}) custom-call(bf16[130,48,256]{2,1,0:T(8,128)(2,1)S(1)} %get-tuple-element.55.packed, bf16[256,160]{1,0:T(8,128)(2,1)S(1)} %maximum_maximum_fusion.weights, bf16[256,256]{1,0:T(8,128)(2,1)S(1)} %copy-done.5, f32[8,128]{1,0:T(8,128)S(1)} %convert_element_type.5.mask, ...), custom_call_target="tpu_custom_call" | custom-call | flops 1073741824 | bytes 4194304 | tf_op jit(solution)/shard_map/saturate/pallas_call | solution.py:425
  47.9 3.3 %saturate.6 = (bf16[8,32,256]{2,1,0:T(8,128)(2,1)S(1)}, f32[8,32,1]{2,1,0:T(8,128)S(1)}) custom-call(bf16[130,48,256]{2,1,0:T(8,128)(2,1)S(1)} %get-tuple-element.55.packed, bf16[256,160]{1,0:T(8,128)(2,1)S(1)} %maximum_maximum_fusion.weights, bf16[256,256]{1,0:T(8,128)(2,1)S(1)} %copy-done.5, f32[8,128]{1,0:T(8,128)S(1)} %convert_element_type.5.mask, ...), custom_call_target="tpu_custom_call" | custom-call | flops 1073741824 | bytes 4194304 | tf_op jit(solution)/shard_map/saturate/pallas_call | solution.py:425
  51.2 2.0 %collective-permute-done.10 = bf16[4,80,256]{2,1,0:T(8,128)(2,1)S(1)} collective-permute-done((bf16[4,80,256]{2,1,0:T(8,128)(2,1)S(1)}, bf16[4,80,256]{2,1,0:T(8,128)(2,1)S(1)}, u32[]{:S(2)}, u32[]{:S(2)}) %collective-permute-start.10) | collective-permute-done | bytes 163872 | tf_op jit(solution)/shard_map/ppermute | solution.py:336
  53.3 0.6 collective-permute-start.11
  53.9 3.3 %saturate.7 = (bf16[8,32,256]{2,1,0:T(8,128)(2,1)S(1)}, f32[8,32,1]{2,1,0:T(8,128)S(1)}) custom-call(bf16[130,48,256]{2,1,0:T(8,128)(2,1)S(1)} %get-tuple-element.55.packed, bf16[256,160]{1,0:T(8,128)(2,1)S(1)} %maximum_maximum_fusion.weights, bf16[256,256]{1,0:T(8,128)(2,1)S(1)} %copy-done.5, f32[8,128]{1,0:T(8,128)S(1)} %convert_element_type.5.mask, ...), custom_call_target="tpu_custom_call" | custom-call | flops 1073741824 | bytes 4194304 | tf_op jit(solution)/shard_map/saturate/pallas_call | solution.py:425
  57.1 3.8 %collective-permute-done.11 = bf16[8,80,256]{2,1,0:T(8,128)(2,1)S(1)} collective-permute-done((bf16[8,80,256]{2,1,0:T(8,128)(2,1)S(1)}, bf16[8,80,256]{2,1,0:T(8,128)(2,1)S(1)}, u32[]{:S(2)}, u32[]{:S(2)}) %collective-permute-start.11) | collective-permute-done | bytes 327712 | tf_op jit(solution)/shard_map/ppermute | solution.py:336
  61.0 0.9 %moments.1 = (bf16[16,128,256]{2,1,0:T(8,128)(2,1)S(1)}, f32[16,128,1]{2,1,0:T(8,128)S(1)}) custom-call(bf16[16,128,256]{2,1,0:T(8,128)(2,1)S(1)} %bitcast.39), custom_call_target="tpu_custom_call" | custom-call | tf_op jit(solution)/shard_map/moments/pallas_call | solution.py:440
  62.0 1.2 %collective-permute-done.12 = bf16[16,80,256]{2,1,0:T(8,128)(2,1)S(1)} collective-permute-done((bf16[16,80,256]{2,1,0:T(8,128)(2,1)S(1)}, bf16[16,80,256]{2,1,0:T(8,128)(2,1)S(1)}, u32[]{:S(2)}, u32[]{:S(2)}) %collective-permute-start.12) | collective-permute-done | bytes 655392 | tf_op jit(solution)/shard_map/ppermute | solution.py:336
  63.1 0.1 pad_maximum_fusion.refs_0_
  63.2 15.1 %update.1 = bf16[24,128,256]{2,1,0:T(8,128)(2,1)} custom-call(bf16[32,80,256]{2,1,0:T(8,128)(2,1)S(1)} %pad_maximum_fusion.refs_0_, bf16[16,128,256]{2,1,0:T(8,128)(2,1)S(1)} %get-tuple-element.59.refs_1_, f32[16,128,1]{2,1,0:T(8,128)S(1)} %get-tuple-element.60.refs_2_, bf16[8,32,256]{2,1,0:T(8,128)(2,1)S(1)} %get-tuple-element.61.refs_3_, ...), custom_call_target="tpu_custom_call" | custom-call | tf_op jit(solution)/shard_map/update/pallas_call | solution.py:464
  (49 shorter events, 0.8 us)
Async XLA Ops:
  0.0 15.5 %copy-start = (bf16[54,32]{0,1:T(8,128)(2,1)S(1)}, bf16[54,32]{0,1:T(8,128)(2,1)}, u32[]{:S(2)}) copy-start(bf16[54,32]{0,1:T(8,128)(2,1)} %param.13) | copy-start | bytes 10372
  0.0 12.9 %copy-start.1 = (bf16[2,2,4,128,256]{4,3,2,1,0:T(8,128)(2,1)S(1)}, bf16[2,2,4,128,256]{4,3,2,1,0:T(8,128)(2,1)}, u32[]{:S(2)}) copy-start(bf16[2,2,4,128,256]{4,3,2,1,0:T(8,128)(2,1)} %param.11) | copy-start | bytes 3145732
  1.9 14.2 %collective-permute-start.7 = (bf16[2,1,1,128,256]{4,3,0,2,1:T(8,128)(2,1)S(1)}, bf16[2,1,1,128,256]{4,3,0,2,1:T(8,128)(2,1)S(1)}, u32[]{:S(2)}, u32[]{:S(2)}) collective-permute-start(bf16[2,1,1,128,256]{4,3,0,2,1:T(8,128)(2,1)S(1)} %get-tuple-element.69), channel_id=1, source_target_pairs={{1,28},{2,29},{3,30},{5,0},{6,1},{7,2},{9,4},{10,5},{11,6},{13,8},... | collective-permute-start | bytes 393224 | tf_op jit(solution)/shard_map/ppermute | solution.py:327
  3.2 14.2 %collective-permute-start.6 = (bf16[2,1,1,128,256]{4,3,0,2,1:T(8,128)(2,1)S(1)}, bf16[2,1,1,128,256]{4,3,0,2,1:T(8,128)(2,1)S(1)}, u32[]{:S(2)}, u32[]{:S(2)}) collective-permute-start(bf16[2,1,1,128,256]{4,3,0,2,1:T(8,128)(2,1)S(1)} %get-tuple-element.70), channel_id=1, source_target_pairs={{1,4},{2,5},{3,6},{5,8},{6,9},{7,10},{9,12},{10,13},{11,14},{13,16... | collective-permute-start | bytes 393224 | tf_op jit(solution)/shard_map/ppermute | solution.py:327
  4.5 10.9 %copy-start.9 = (f32[32]{0:T(128)S(1)}, f32[32]{0:T(128)}, u32[]{:S(2)}) copy-start(f32[32]{0:T(128)} %param.14) | copy-start | bytes 388
  4.5 11.0 %copy-start.6 = (bf16[54,1152]{1,0:T(8,128)(2,1)S(1)}, bf16[54,1152]{1,0:T(8,128)(2,1)}, u32[]{:S(2)}) copy-start(bf16[54,1152]{1,0:T(8,128)(2,1)} %constant.12.clone) | copy-start | bytes 373252
  4.5 19.3 %collective-permute-start.5 = (bf16[2,1,1,128,256]{4,3,0,2,1:T(8,128)(2,1)}, bf16[2,1,1,128,256]{4,3,0,2,1:T(8,128)(2,1)S(1)}, u32[]{:S(2)}, u32[]{:S(2)}) collective-permute-start(bf16[2,1,1,128,256]{4,3,0,2,1:T(8,128)(2,1)} %get-tuple-element.71), channel_id=1, source_target_pairs={{0,29},{1,30},{2,31},{4,1},{5,2},{6,3},{8,5},{9,6},{10,7},{12,9},{... | collective-permute-start | bytes 393224 | tf_op jit(solution)/shard_map/ppermute | solution.py:327
  14.0 9.3 %copy-start.10 = (f32[32]{0:T(128)S(1)}, f32[32]{0:T(128)}, u32[]{:S(2)}) copy-start(f32[32]{0:T(128)} %param.15) | copy-start | bytes 388
  14.0 9.5 %copy-start.3 = (s32[2,4,128]{2,1,0:T(4,128)S(1)}, s32[2,4,128]{2,1,0:T(4,128)}, u32[]{:S(2)}) copy-start(s32[2,4,128]{2,1,0:T(4,128)} %param.12) | copy-start | bytes 12292
  14.0 9.6 %copy-start.7 = (f32[64]{0:T(128)S(1)}, f32[64]{0:T(128)}, u32[]{:S(2)}) copy-start(f32[64]{0:T(128)} %param.17) | copy-start | bytes 772
  14.0 9.7 %copy-start.8 = (f32[64]{0:T(128)S(1)}, f32[64]{0:T(128)}, u32[]{:S(2)}) copy-start(f32[64]{0:T(128)} %param.18) | copy-start | bytes 772
  14.0 18.1 %collective-permute-start.1 = (bf16[2,1,4,128,256]{4,3,2,1,0:T(8,128)(2,1)}, bf16[2,1,4,128,256]{4,3,2,1,0:T(8,128)(2,1)S(1)}, u32[]{:S(2)}, u32[]{:S(2)}) collective-permute-start(bf16[2,1,4,128,256]{4,3,2,1,0:T(8,128)(2,1)} %get-tuple-element.75), channel_id=1, source_target_pairs={{4,0},{8,4},{12,8},{16,12},{20,16},{24,20},{28,24},{0,28},{5,1},{9... | collective-permute-start | bytes 1572872 | tf_op jit(solution)/shard_map/ppermute | solution.py:316
  14.2 17.9 %copy-start.2 = (bf16[256,256]{1,0:T(8,128)(2,1)S(1)}, bf16[256,256]{1,0:T(8,128)(2,1)}, u32[]{:S(2)}) copy-start(bf16[256,256]{1,0:T(8,128)(2,1)} %constant.13.clone.swap_in) | copy-start | bytes 393220
  14.2 17.9 %copy-start.4 = (s32[64]{0:T(128)S(1)}, s32[64]{0:T(128)}, u32[]{:S(2)}) copy-start(s32[64]{0:T(128)} %cells.1) | copy-start | bytes 772
  14.2 17.9 %collective-permute-start = (bf16[2,1,4,128,256]{4,3,2,1,0:T(8,128)(2,1)}, bf16[2,1,4,128,256]{4,3,2,1,0:T(8,128)(2,1)S(1)}, u32[]{:S(2)}, u32[]{:S(2)}) collective-permute-start(bf16[2,1,4,128,256]{4,3,2,1,0:T(8,128)(2,1)} %get-tuple-element.76), channel_id=1, source_target_pairs={{0,4},{4,8},{8,12},{12,16},{16,20},{20,24},{24,28},{28,0},{1,5},{5... | collective-permute-start | bytes 1572872 | tf_op jit(solution)/shard_map/ppermute | solution.py:316
  16.1 15.9 %collective-permute-start.3 = (bf16[2,2,1,128,256]{4,3,2,1,0:T(8,128)(2,1)}, bf16[2,2,1,128,256]{4,3,2,1,0:T(8,128)(2,1)S(1)}, u32[]{:S(2)}, u32[]{:S(2)}) collective-permute-start(bf16[2,2,1,128,256]{4,3,2,1,0:T(8,128)(2,1)} %get-tuple-element.73), channel_id=1, source_target_pairs={{1,0},{2,1},{3,2},{5,4},{6,5},{7,6},{9,8},{10,9},{11,10},{13,12},{... | collective-permute-start | bytes 786440 | tf_op jit(solution)/shard_map/ppermute | solution.py:316
  17.4 14.6 %collective-permute-start.2 = (bf16[2,2,1,128,256]{4,3,2,1,0:T(8,128)(2,1)}, bf16[2,2,1,128,256]{4,3,2,1,0:T(8,128)(2,1)S(1)}, u32[]{:S(2)}, u32[]{:S(2)}) collective-permute-start(bf16[2,2,1,128,256]{4,3,2,1,0:T(8,128)(2,1)} %get-tuple-element.74), channel_id=1, source_target_pairs={{0,1},{1,2},{2,3},{4,5},{5,6},{6,7},{8,9},{9,10},{10,11},{12,13},{... | collective-permute-start | bytes 786440 | tf_op jit(solution)/shard_map/ppermute | solution.py:316
  23.8 8.2 %collective-permute-start.4 = (bf16[2,1,1,128,256]{4,3,0,2,1:T(8,128)(2,1)}, bf16[2,1,1,128,256]{4,3,0,2,1:T(8,128)(2,1)S(1)}, u32[]{:S(2)}, u32[]{:S(2)}) collective-permute-start(bf16[2,1,1,128,256]{4,3,0,2,1:T(8,128)(2,1)} %get-tuple-element.72), channel_id=1, source_target_pairs={{0,5},{1,6},{2,7},{4,9},{5,10},{6,11},{8,13},{9,14},{10,15},{12,17... | collective-permute-start | bytes 393224 | tf_op jit(solution)/shard_map/ppermute | solution.py:327
  32.1 7.8 %copy-start.5 = (bf16[256,256]{1,0:T(8,128)(2,1)S(1)}, bf16[256,256]{1,0:T(8,128)(2,1)}, u32[]{:S(2)}) copy-start(bf16[256,256]{1,0:T(8,128)(2,1)} %constant.14.clone.swap_out) | copy-start | bytes 393220
  35.5 7.7 %collective-permute-start.8 = (bf16[1,80,256]{2,1,0:T(8,128)(2,1)S(1)}, bf16[1,80,256]{2,1,0:T(8,128)(2,1)S(1)}, u32[]{:S(2)}, u32[]{:S(2)}) collective-permute-start(bf16[1,80,256]{2,1,0:T(8,128)(2,1)S(1)} %bitcast.48), channel_id=1, source_target_pairs={{0,2},{1,3},{2,0},{3,1},{4,6},{5,7},{6,4},{7,5},{8,10},{9,11},{10,... | collective-permute-start | bytes 122888 | tf_op jit(solution)/shard_map/ppermute | solution.py:336
  43.2 4.6 %collective-permute-start.9 = (bf16[2,80,256]{2,1,0:T(8,128)(2,1)S(1)}, bf16[2,80,256]{2,1,0:T(8,128)(2,1)S(1)}, u32[]{:S(2)}, u32[]{:S(2)}) collective-permute-start(bf16[2,80,256]{2,1,0:T(8,128)(2,1)S(1)} %pad_maximum_fusion.4), channel_id=1, source_target_pairs={{0,1},{1,0},{2,3},{3,2},{4,5},{5,4},{6,7},{7,6},{8,9},{9,8},{10,11... | collective-permute-start | bytes 245768 | tf_op jit(solution)/shard_map/ppermute | solution.py:336
  47.9 5.4 %collective-permute-start.10 = (bf16[4,80,256]{2,1,0:T(8,128)(2,1)S(1)}, bf16[4,80,256]{2,1,0:T(8,128)(2,1)S(1)}, u32[]{:S(2)}, u32[]{:S(2)}) collective-permute-start(bf16[4,80,256]{2,1,0:T(8,128)(2,1)S(1)} %pad_maximum_fusion.3), channel_id=1, source_target_pairs={{0,8},{4,12},{8,0},{12,4},{16,24},{20,28},{24,16},{28,20},{1,9},{5... | collective-permute-start | bytes 491528 | tf_op jit(solution)/shard_map/ppermute | solution.py:336
  53.3 7.6 %collective-permute-start.11 = (bf16[8,80,256]{2,1,0:T(8,128)(2,1)S(1)}, bf16[8,80,256]{2,1,0:T(8,128)(2,1)S(1)}, u32[]{:S(2)}, u32[]{:S(2)}) collective-permute-start(bf16[8,80,256]{2,1,0:T(8,128)(2,1)S(1)} %pad_maximum_fusion.2), channel_id=1, source_target_pairs={{0,16},{4,20},{8,24},{12,28},{16,0},{20,4},{24,8},{28,12},{1,17},{... | collective-permute-start | bytes 983048 | tf_op jit(solution)/shard_map/ppermute | solution.py:336
  61.0 2.2 %collective-permute-start.12 = (bf16[16,80,256]{2,1,0:T(8,128)(2,1)S(1)}, bf16[16,80,256]{2,1,0:T(8,128)(2,1)S(1)}, u32[]{:S(2)}, u32[]{:S(2)}) collective-permute-start(bf16[16,80,256]{2,1,0:T(8,128)(2,1)S(1)} %pad_maximum_fusion.1), channel_id=1, source_target_pairs={{0,4},{4,0},{8,12},{12,8},{16,20},{20,16},{24,28},{28,24},{1,5},{5... | collective-permute-start | bytes 1966088 | tf_op jit(solution)/shard_map/ppermute | solution.py:336

commit v5 on v4

--- a/solution.py
+++ b/solution.py
@@ -13,7 +13,7 @@
 PAY_ROWS = 16
 GATHER_DEVICES = 64
 BLOCK = 64
-PIECES = 4
+SPANS = (16, 32, 32, 48)
 VMEM_BYTES = 32 * 1024 * 1024
 
 
@@ -24,7 +24,7 @@
     left = [(f, z + 1, 0) for f in range(2) for z in range(planes)]
     right = [(f, z + 1, columns + 1) for f in range(2) for z in range(planes)]
     corners = [
-        (f, z, x) for x in (0, columns + 1) for z in (0, planes + 1) for f in range(2)
+        (f, z, x) for z in (0, planes + 1) for x in (0, columns + 1) for f in range(2)
     ]
     return own + low + high + left + right + corners
 
@@ -62,9 +62,13 @@
     return jnp.where(row_index < 3, 1.0, 0.0).astype(jnp.bfloat16)
 
 
+def ordered(odd, far, near):
+    return jnp.where(odd == 0, far, near), jnp.where(odd == 0, near, far)
+
+
 def observe_kernel(
-    own, low, high, left, right, low_left, high_left, low_right, high_right, by_row, swap_in, read_column,
-    sigma, values, cells, mask, packed, pay_out, pred
+    own, far, near, left, right, far_left, far_right, near_corner, by_row, swap_in, read_column,
+    sigma, values, cells, mask, odd, packed, pay_out, pred
 ):
     lanes, members = own.shape[1], own.shape[2]
     count = packed.shape[1]
@@ -74,10 +78,18 @@
 
     for step in range(lanes // 16):
         at = step * 16
-        groups = ((own,), (low, high), (left, right, low_left, high_left, low_right, high_right))
-        for g, refs in enumerate(groups):
-            parts = [ref[:, pl.ds(at, 16), :] for ref in refs]
-            block = parts[0] if len(parts) == 1 else jnp.concatenate(parts, axis=0)
+        part = lambda ref: ref[:, pl.ds(at, 16), :]
+        far_block, near_block = part(far), part(near)
+        far_sides = jnp.concatenate([part(far_left), part(far_right)], axis=0)
+        near_sides = part(near_corner)
+        blocks = (
+            part(own),
+            jnp.concatenate(ordered(odd[0], far_block, near_block), axis=0),
+            jnp.concatenate(
+                [part(left), part(right), *ordered(odd[0], far_sides, near_sides)], axis=0
+            ),
+        )
+        for g, block in enumerate(blocks):
             moved = jnp.dot(
                 swap_in[...], block.reshape(256, members), preferred_element_type=jnp.float32
             )
@@ -148,10 +160,13 @@
         return carry
 
     lax.fori_loop(0, span // 8, some_rows, 0)
-    moved = jnp.dot(swap_out[...], sat_rows[...], preferred_element_type=jnp.float32)
-    mean = jnp.mean(moved, axis=1, keepdims=True)
-    anomaly_out[...] = (moved - mean).astype(jnp.bfloat16).reshape(rows, span, members)
-    mean_out[...] = mean.reshape(rows, span, 1)
+    for n in range(span // 16):
+        block = sat_rows[n * 16 * rows : (n + 1) * 16 * rows, :]
+        moved = jnp.dot(swap_out[...], block, preferred_element_type=jnp.float32)
+        mean = jnp.mean(moved, axis=1, keepdims=True)
+        anomalies = (moved - mean).astype(jnp.bfloat16)
+        anomaly_out[:, n * 16 : n * 16 + 16, :] = anomalies.reshape(rows, 16, members)
+        mean_out[:, n * 16 : n * 16 + 16, :] = mean.reshape(rows, 16, 1)
 
 
 def moments_kernel(fields, anomaly_out, mean_out):
@@ -177,11 +192,6 @@
 
 def spread_lane(part, q):
     return jnp.broadcast_to(part[:, q : q + 1], part.shape)
-
-
-def inverse_root(value):
-    guess = lax.rsqrt(value)
-    return guess * (1.5 - (0.5 * value) * (guess * guess))
 
 
 def inverse_factor_block(block):
@@ -205,7 +215,7 @@
             beside = [spread_lane(parts[j + 1], 8 * j + q) for q in range(8)]
         factor, scale = {}, []
         for q in range(8):
-            root = inverse_root(entry[q, q])
+            root = lax.rsqrt(entry[q, q])
             scale.append(root)
             line[q] = line[q] * root
             for p in range(q + 1, 8):
@@ -301,10 +311,12 @@
         return carry
 
     lax.fori_loop(0, field_rows // 4, step, 0)
+    at = 0
     for n in range(1, len(moments) // 2):
         anomalies, mean = moments[2 * n : 2 * n + 2]
         span = anomalies.shape[1]
-        out[field_rows:, (n - 1) * span : n * span, :] = blend(anomalies[...], mean[...])
+        out[field_rows:, at : at + span, :] = blend(anomalies[...], mean[...])
+        at += span
 
 
 def shift(value, axis, by, closed):
@@ -316,31 +328,29 @@
     return lax.ppermute(value, axis, pairs)
 
 
-def shift_both(value, core_by, face_by):
-    core_count, face_count = lax.axis_size("cores"), lax.axis_size("face")
-    pairs = [
-        (i * face_count + j, ((i + core_by) % core_count) * face_count + j + face_by)
-        for i in range(core_count)
-        for j in range(face_count)
-        if 0 <= j + face_by < face_count
-    ]
-    return lax.ppermute(value, ("cores", "face"), pairs)
+def swap_cores(value, inside):
+    count = lax.axis_size("cores")
+    pairs = []
+    for i in range(count):
+        step = 1 if (i % 2 == 0) == inside else -1
+        pairs.append((i, (i + step) % count))
+    return lax.ppermute(value, "cores", pairs)
 
 
 def gather_rows(block, steps, packed, saturate):
     pieces = []
     for n, (axis, bit) in enumerate(steps):
         count = lax.axis_size(axis)
-        if n < PIECES:
+        if n < len(SPANS):
             block, packed = lax.optimization_barrier((block, packed))
         other = lax.ppermute(block, axis, [(i, i ^ bit) for i in range(count)])
-        if n < PIECES:
+        if n < len(SPANS):
             piece = saturate(n, packed)
         block = jnp.concatenate([block, other], axis=0)
-        if n < PIECES:
+        if n < len(SPANS):
             block, piece = lax.optimization_barrier((block, piece))
             pieces.append(piece)
-    return block, pieces + [saturate(n, packed) for n in range(len(pieces), PIECES)]
+    return block, pieces + [saturate(n, packed) for n in range(len(pieces), len(SPANS))]
 
 
 def bits_of(axis, count):
@@ -373,14 +383,19 @@
     rows = planes * columns
     observed = obs_cells.shape[0]
 
-    low = shift(fields[:, -1:], "cores", 1, True)
-    high = shift(fields[:, :1], "cores", -1, True)
-    low_left = shift_both(fields[:, -1:, -1:], 1, 1)
-    high_left = shift_both(fields[:, :1, -1:], -1, 1)
-    low_right = shift_both(fields[:, -1:, :1], 1, -1)
-    high_right = shift_both(fields[:, :1, :1], -1, -1)
-    left = shift(fields[:, :, -1:], "face", 1, False)
-    right = shift(fields[:, :, :1], "face", -1, False)
+    odd = lax.axis_index("cores") % 2
+    near_plane = (1 - odd) * (planes - 1)
+    far = lax.dynamic_slice_in_dim(fields, odd * (planes - 1), 1, axis=1)
+    near = lax.dynamic_slice_in_dim(fields, near_plane, 1, axis=1)
+    far, near, tied = lax.optimization_barrier((far, near, fields))
+    far = swap_cores(far, False)
+    near = swap_cores(near, True)
+    left = shift(tied[:, :, -1:], "face", 1, False)
+    right = shift(tied[:, :, :1], "face", -1, False)
+    far_left = shift(far[:, :, -1:], "face", 1, False)
+    far_right = shift(far[:, :, :1], "face", -1, False)
+    near_sides = [lax.dynamic_slice_in_dim(side, near_plane, 1, axis=1) for side in (left, right)]
+    near_corner = swap_cores(jnp.concatenate(near_sides, axis=0), True)
 
     selector = tap_selector(planes, columns)
     count = selector.shape[2] // 3
@@ -397,12 +412,12 @@
     by_row = jnp.transpose(weights, (1, 0, 2))
     weights = weights.reshape(channels * rows, 3 * count + 16)
     flat = lambda a: a.reshape(-1, lanes, members)
-    span = lanes // PIECES
+    starts = [sum(SPANS[:n]) for n in range(len(SPANS))]
     mask = pore_mask.reshape(rows, lanes)
     mask_float = mask.astype(jnp.float32)
     read_half = 0.5 * read_weight
     swap_in = jnp.asarray(swap_matrix(16, 16), jnp.bfloat16)
-    swap_out = jnp.asarray(swap_matrix(span, rows), jnp.bfloat16)
+    swap_out = jnp.asarray(swap_matrix(16, rows), jnp.bfloat16)
     params = pltpu.CompilerParams(vmem_limit_bytes=VMEM_BYTES)
     packed, pay = pl.pallas_call(
         observe_kernel,
@@ -410,20 +425,21 @@
             jax.ShapeDtypeStruct((lanes + 2, count, members), jnp.bfloat16),
             jax.ShapeDtypeStruct((observed + PAY_ROWS, members), jnp.bfloat16),
         ),
-        in_specs=[vmem()] * 14 + [smem()] * 2,
+        in_specs=[vmem()] * 13 + [smem()] * 3,
         out_specs=(vmem(), vmem()),
         scratch_shapes=[pltpu.VMEM((observed, members), jnp.float32)],
         compiler_params=params,
         name="observe",
     )(
-        flat(fields), flat(low), flat(high), flat(left), flat(right), flat(low_left),
-        flat(high_left), flat(low_right), flat(high_right), by_row, swap_in, read_half[:, None],
-        obs_sigma[:, None], obs_values[:, None], obs_cells, mask,
+        flat(fields), flat(far), flat(near), flat(left), flat(right), flat(far_left),
+        flat(far_right), flat(near_corner), by_row, swap_in, read_half[:, None],
+        obs_sigma[:, None], obs_values[:, None], obs_cells, mask, odd.astype(jnp.int32)[None],
     )
 
     def saturate(n, packed):
+        span = SPANS[n]
         return pl.pallas_call(
-            functools.partial(saturate_kernel, n * span),
+            functools.partial(saturate_kernel, starts[n]),
             out_shape=moments_shape(rows, span, members),
             in_specs=[vmem()] * 4 + [smem()],
             out_specs=(vmem(), vmem()),
@@ -460,11 +476,11 @@
         )
         coeff = jnp.sum(pay[observed:].astype(jnp.float32), axis=0, keepdims=True)
         terms = lax.psum((gram, coeff), ("cores", "face"))
-        pieces = [saturate(n, packed) for n in range(PIECES)]
+        pieces = [saturate(n, packed) for n in range(len(SPANS))]
     out = pl.pallas_call(
         functools.partial(update_kernel, gathered),
         out_shape=jax.ShapeDtypeStruct((3 * rows, lanes, members), jnp.bfloat16),
-        in_specs=[vmem()] * (len(terms) + 2 + 2 * PIECES),
+        in_specs=[vmem()] * (len(terms) + 2 + 2 * len(SPANS)),
         out_specs=vmem(),
         scratch_shapes=[
             pltpu.VMEM((members, 2 * members), jnp.float32),

time: 78.6 us -> 77.7 us (0.989)
  starting transfers between devices: 28 us -> 23 us
  waiting for transfers between devices: 12.1 us -> 16 us
  other arithmetic: 0.45 us -> 1.32 us
    ppermute x4 -> x3, starting transfers between devices: 13.9 us -> 2.18 us  [swap_cores(): return lax.ppermute(value, 'cores', pairs)]
    ppermute x4, starting transfers between devices: 7.65 us -> 13.2 us  [shift(): return lax.ppermute(value, axis, pairs)]
    ppermute x4 -> x3, waiting for transfers between devices: 5.17 us -> 8.74 us  [swap_cores(): return lax.ppermute(value, 'cores', pairs)]
    ppermute x4, waiting for transfers between devices: 0.01 us -> 3.24 us  [shift(): return lax.ppermute(value, axis, pairs)]
    ppermute x5, waiting for transfers between devices: 6.96 us -> 3.98 us  [gather_rows(): other = lax.ppermute(block, axis, [(i, i ^ bit) for i in range(count)])]
    dynamic_slice x0 -> x3, local copies, waits for them, and re-layouts: none -> 2.18 us  [the longest x1 2.15 us: shards(): near = lax.dynamic_slice_in_dim(fields, near_plane, 1, axis=1)]
    unnamed x23 -> x22, local copies, waits for them, and re-layouts: 1.97 us -> 0.05 us
    ppermute x5, starting transfers between devices: 6.46 us -> 7.63 us  [gather_rows(): other = lax.ppermute(block, axis, [(i, i ^ bit) for i in range(count)])]
  transfers between devices with their start and end apart: 13 -> 12, of which waited for: 4 -> 7; matrix products, arithmetic and copies ran while one was open for 4% -> 4% of each run, Pallas kernels for 18% -> 18%
where the time goes in v5:
time: 77.7 us; the launch traced here: 77.4 us
  Pallas kernels  31.9 us (41%)
  starting transfers between devices  23 us (30%)
  waiting for transfers between devices  16 us (21%)
  local copies, waits for them, and re-layouts  4.73 us (6%)
  other arithmetic  1.32 us (2%)
    pallas_call x1, Pallas kernels, shards(): pl.pallas_call(functools.partial(update_kernel, gathered), out_shape=jax....  14.6 us
    ppermute x4, starting transfers between devices, shift(): return lax.ppermute(value, axis, pairs)  13.2 us
    pallas_call x4, Pallas kernels, saturate(): pl.pallas_call(functools.partial(saturate_kernel, starts[n]), out_shape=m...  13 us
    ppermute x3, waiting for transfers between devices, swap_cores(): return lax.ppermute(value, 'cores', pairs)  8.74 us
    ppermute x5, starting transfers between devices, gather_rows(): other = lax.ppermute(block, axis, [(i, i ^ bit) for i in range(count)])  7.63 us
    ppermute x5, waiting for transfers between devices, gather_rows(): other = lax.ppermute(block, axis, [(i, i ^ bit) for i in range(count)])  3.98 us
    pallas_call x1, Pallas kernels, shards(): pl.pallas_call(observe_kernel, out_shape=(jax.ShapeDtypeStruct((lanes + 2...  3.4 us
    ppermute x4, waiting for transfers between devices, shift(): return lax.ppermute(value, axis, pairs)  3.24 us
  transfers between devices with their start and end apart: 12, of which 7 were waited for; matrix products, arithmetic and copies ran while one was open for 4% of the time, Pallas kernels for 18%

profile of v5, /device:TPU:0, one launch (start us, length us, event | category | flops | bytes accessed | tf_op | source)
XLA Modules:
  0.0 77.4 jit_solution(7743421137847641335)
XLA Ops:
  0.0 2.1 %constant_dynamic-slice_fusion.2 = (bf16[2,1,4,128,256]{4,3,2,1,0:T(8,128)(2,1)}, bf16[2,1,4,128,256]{4,3,2,1,0:T(8,128)(2,1)S(1)}) fusion(bf16[2,2,4,128,256]{4,3,2,1,0:T(8,128)(2,1)} %param.11, s32[]{:T(128)S(6)} %select_n.17, s32[]{:T(128)S(6)} %select_n.16), kind=kLoop, calls=%fused_computation.15 | loop fusion | bytes 2097160 | tf_op jit(solution)/shard_map/dynamic_slice | solution.py:389
  2.2 0.8 %fusion.5 = (bf16[2,2,1,128,256]{4,3,0,2,1:T(8,128)(2,1)}, bf16[2,2,1,128,256]{4,3,0,2,1:T(8,128)(2,1)}) fusion(bf16[2,2,4,128,256]{4,3,2,1,0:T(8,128)(2,1)S(1)} %copy-done.1), kind=kLoop, calls=%fused_computation.25 | loop fusion | bytes 1048576 | tf_op jit(solution)/shard_map/slice | solution.py:394
  3.1 1.3 %collective-permute-start.3 = (bf16[2,2,1,128,256]{4,3,0,2,1:T(8,128)(2,1)}, bf16[2,2,1,128,256]{4,3,0,2,1:T(8,128)(2,1)S(1)}, u32[]{:S(2)}, u32[]{:S(2)}) collective-permute-start(bf16[2,2,1,128,256]{4,3,0,2,1:T(8,128)(2,1)} %get-tuple-element.75), channel_id=1, source_target_pairs={{1,0},{2,1},{3,2},{5,4},{6,5},{7,6},{9,8},{10,9},{11,10},{13,12},{... | collective-permute-start | bytes 786440 | tf_op jit(solution)/shard_map/ppermute | solution.py:328
  4.4 5.6 %collective-permute-start.2 = (bf16[2,2,1,128,256]{4,3,0,2,1:T(8,128)(2,1)}, bf16[2,2,1,128,256]{4,3,0,2,1:T(8,128)(2,1)S(1)}, u32[]{:S(2)}, u32[]{:S(2)}) collective-permute-start(bf16[2,2,1,128,256]{4,3,0,2,1:T(8,128)(2,1)} %get-tuple-element.76), channel_id=1, source_target_pairs={{0,1},{1,2},{2,3},{4,5},{5,6},{6,7},{8,9},{9,10},{10,11},{12,13},{... | collective-permute-start | bytes 786440 | tf_op jit(solution)/shard_map/ppermute | solution.py:328
  9.9 1.8 %collective-permute-start = (bf16[2,1,4,128,256]{4,3,0,2,1:T(8,128)(2,1)S(1)}, bf16[2,1,4,128,256]{4,3,0,2,1:T(8,128)(2,1)S(1)}, u32[]{:S(2)}, u32[]{:S(2)}) collective-permute-start(bf16[2,1,4,128,256]{4,3,0,2,1:T(8,128)(2,1)S(1)} %copy.32), channel_id=1, source_target_pairs={{0,28},{4,8},{8,4},{12,16},{16,12},{20,24},{24,20},{28,0},{1,29},{... | collective-permute-start | bytes 1572872 | tf_op jit(solution)/shard_map/ppermute | solution.py:337
  11.8 0.3 collective-permute-start.1
  12.2 0.6 broadcast_bitcast_fusion
  12.8 0.1 fusion.1
  13.0 0.2 mul.24
  13.2 0.2 mul.21
  13.8 0.9 %maximum_maximum_fusion.weights = bf16[256,160]{1,0:T(8,128)(2,1)S(1)} fusion(bf16[256,3]{1,0:T(8,128)(2,1)} %broadcast_bitcast_fusion, bf16[256,144]{1,0:T(8,128)(2,1)S(1)} %mul.24, bf16[160]{0:T(256)(128)(2,1)S(1)} %pad.15.clone), kind=kLoop, calls=%fused_computation.9 | loop fusion | flops 245760 | bytes 157504 | tf_op jit(solution)/shard_map/concatenate | solution.py:409
  14.8 1.0 %collective-permute-done.2 = bf16[2,2,1,128,256]{4,3,0,2,1:T(8,128)(2,1)S(1)} collective-permute-done((bf16[2,2,1,128,256]{4,3,0,2,1:T(8,128)(2,1)}, bf16[2,2,1,128,256]{4,3,0,2,1:T(8,128)(2,1)S(1)}, u32[]{:S(2)}, u32[]{:S(2)}) %collective-permute-start.2) | collective-permute-done | bytes 262176 | tf_op jit(solution)/shard_map/ppermute | solution.py:328
  15.9 8.7 %collective-permute-done = bf16[2,1,4,128,256]{4,3,0,2,1:T(8,128)(2,1)S(1)} collective-permute-done((bf16[2,1,4,128,256]{4,3,0,2,1:T(8,128)(2,1)S(1)}, bf16[2,1,4,128,256]{4,3,0,2,1:T(8,128)(2,1)S(1)}, u32[]{:S(2)}, u32[]{:S(2)}) %collective-permute-start) | collective-permute-done | bytes 524320 | tf_op jit(solution)/shard_map/ppermute | solution.py:337
  24.7 1.4 %collective-permute-start.5 = (bf16[2,1,1,128,256]{4,3,0,2,1:T(8,128)(2,1)S(1)}, bf16[2,1,1,128,256]{4,3,0,2,1:T(8,128)(2,1)S(1)}, u32[]{:S(2)}, u32[]{:S(2)}) collective-permute-start(bf16[2,1,1,128,256]{4,3,0,2,1:T(8,128)(2,1)S(1)} %get-tuple-element.79), channel_id=1, source_target_pairs={{1,0},{2,1},{3,2},{5,4},{6,5},{7,6},{9,8},{10,9},{11,10},{13,12},{... | collective-permute-start | bytes 393224 | tf_op jit(solution)/shard_map/ppermute | solution.py:328
  26.1 4.9 %collective-permute-start.4 = (bf16[2,1,1,128,256]{4,3,0,2,1:T(8,128)(2,1)S(1)}, bf16[2,1,1,128,256]{4,3,0,2,1:T(8,128)(2,1)S(1)}, u32[]{:S(2)}, u32[]{:S(2)}) collective-permute-start(bf16[2,1,1,128,256]{4,3,0,2,1:T(8,128)(2,1)S(1)} %get-tuple-element.80), channel_id=1, source_target_pairs={{0,1},{1,2},{2,3},{4,5},{5,6},{6,7},{8,9},{9,10},{10,11},{12,13},{... | collective-permute-start | bytes 393224 | tf_op jit(solution)/shard_map/ppermute | solution.py:328
  31.3 0.8 collective-permute-done.5
  32.1 1.5 %collective-permute-done.4 = bf16[2,1,1,128,256]{4,3,0,2,1:T(8,128)(2,1)S(1)} collective-permute-done((bf16[2,1,1,128,256]{4,3,0,2,1:T(8,128)(2,1)S(1)}, bf16[2,1,1,128,256]{4,3,0,2,1:T(8,128)(2,1)S(1)}, u32[]{:S(2)}, u32[]{:S(2)}) %collective-permute-start.4) | collective-permute-done | bytes 131104 | tf_op jit(solution)/shard_map/ppermute | solution.py:328
  33.6 3.4 %observe.1 = (bf16[130,48,256]{2,1,0:T(8,128)(2,1)S(1)}, bf16[80,256]{1,0:T(8,128)(2,1)S(1)}) custom-call(bf16[16,128,256]{2,1,0:T(8,128)(2,1)S(1)} %bitcast.30, bf16[8,128,256]{2,1,0:T(8,128)(2,1)S(1)} %bitcast.32, bf16[8,128,256]{2,1,0:T(8,128)(2,1)S(1)} %bitcast.35, bf16[4,128,256]{2,1,0:T(8,128)(2,1)S(1)} %bitcast.34, bf16[4,128,256]{2,1,0:T(8,128)(2,1)S(1)} %bitcast.33, ...), custom_call_target="tpu_custom_call" | custom-call | tf_op jit(solution)/shard_map/observe/pallas_call | solution.py:422
  37.0 4.0 %collective-permute-start.7 = (bf16[1,80,256]{2,1,0:T(8,128)(2,1)S(1)}, bf16[1,80,256]{2,1,0:T(8,128)(2,1)S(1)}, u32[]{:S(2)}, u32[]{:S(2)}) collective-permute-start(bf16[1,80,256]{2,1,0:T(8,128)(2,1)S(1)} %bitcast.39), channel_id=1, source_target_pairs={{0,2},{1,3},{2,0},{3,1},{4,6},{5,7},{6,4},{7,5},{8,10},{9,11},{10,... | collective-permute-start | bytes 122888 | tf_op jit(solution)/shard_map/ppermute | solution.py:346
  40.9 2.0 %saturate.4 = (bf16[8,16,256]{2,1,0:T(8,128)(2,1)S(1)}, f32[8,16,1]{2,1,0:T(8,128)S(1)}) custom-call(bf16[130,48,256]{2,1,0:T(8,128)(2,1)S(1)} %get-tuple-element.61.packed, bf16[256,160]{1,0:T(8,128)(2,1)S(1)} %maximum_maximum_fusion.weights, bf16[128,128]{1,0:T(8,128)(2,1)S(1)} %copy-done.3, f32[8,128]{1,0:T(8,128)S(1)} %convert_element_type.5.mask, ...), custom_call_target="tpu_custom_call" | custom-call | flops 536870912 | bytes 4194304 | tf_op jit(solution)/shard_map/saturate/pallas_call | solution.py:441
  43.0 1.7 %collective-permute-start.8 = (bf16[2,80,256]{2,1,0:T(8,128)(2,1)S(1)}, bf16[2,80,256]{2,1,0:T(8,128)(2,1)S(1)}, u32[]{:S(2)}, u32[]{:S(2)}) collective-permute-start(bf16[2,80,256]{2,1,0:T(8,128)(2,1)S(1)} %pad_maximum_fusion.5), channel_id=1, source_target_pairs={{0,1},{1,0},{2,3},{3,2},{4,5},{5,4},{6,7},{7,6},{8,9},{9,8},{10,11... | collective-permute-start | bytes 245768 | tf_op jit(solution)/shard_map/ppermute | solution.py:346
  44.6 3.3 %saturate.5 = (bf16[8,32,256]{2,1,0:T(8,128)(2,1)S(1)}, f32[8,32,1]{2,1,0:T(8,128)S(1)}) custom-call(bf16[130,48,256]{2,1,0:T(8,128)(2,1)S(1)} %get-tuple-element.61.packed, bf16[256,160]{1,0:T(8,128)(2,1)S(1)} %maximum_maximum_fusion.weights, bf16[128,128]{1,0:T(8,128)(2,1)S(1)} %copy-done.3, f32[8,128]{1,0:T(8,128)S(1)} %convert_element_type.5.mask, ...), custom_call_target="tpu_custom_call" | custom-call | flops 1073741824 | bytes 4194304 | tf_op jit(solution)/shard_map/saturate/pallas_call | solution.py:441
  47.9 0.8 %collective-permute-start.9 = (bf16[4,80,256]{2,1,0:T(8,128)(2,1)S(1)}, bf16[4,80,256]{2,1,0:T(8,128)(2,1)S(1)}, u32[]{:S(2)}, u32[]{:S(2)}) collective-permute-start(bf16[4,80,256]{2,1,0:T(8,128)(2,1)S(1)} %pad_maximum_fusion.4), channel_id=1, source_target_pairs={{0,8},{4,12},{8,0},{12,4},{16,24},{20,28},{24,16},{28,20},{1,9},{5... | collective-permute-start | bytes 491528 | tf_op jit(solution)/shard_map/ppermute | solution.py:346
  48.7 3.3 %saturate.6 = (bf16[8,32,256]{2,1,0:T(8,128)(2,1)S(1)}, f32[8,32,1]{2,1,0:T(8,128)S(1)}) custom-call(bf16[130,48,256]{2,1,0:T(8,128)(2,1)S(1)} %get-tuple-element.61.packed, bf16[256,160]{1,0:T(8,128)(2,1)S(1)} %maximum_maximum_fusion.weights, bf16[128,128]{1,0:T(8,128)(2,1)S(1)} %copy-done.3, f32[8,128]{1,0:T(8,128)S(1)} %convert_element_type.5.mask, ...), custom_call_target="tpu_custom_call" | custom-call | flops 1073741824 | bytes 4194304 | tf_op jit(solution)/shard_map/saturate/pallas_call | solution.py:441
  52.0 1.3 %collective-permute-done.9 = bf16[4,80,256]{2,1,0:T(8,128)(2,1)S(1)} collective-permute-done((bf16[4,80,256]{2,1,0:T(8,128)(2,1)S(1)}, bf16[4,80,256]{2,1,0:T(8,128)(2,1)S(1)}, u32[]{:S(2)}, u32[]{:S(2)}) %collective-permute-start.9) | collective-permute-done | bytes 163872 | tf_op jit(solution)/shard_map/ppermute | solution.py:346
  53.3 1.1 %collective-permute-start.10 = (bf16[8,80,256]{2,1,0:T(8,128)(2,1)S(1)}, bf16[8,80,256]{2,1,0:T(8,128)(2,1)S(1)}, u32[]{:S(2)}, u32[]{:S(2)}) collective-permute-start(bf16[8,80,256]{2,1,0:T(8,128)(2,1)S(1)} %pad_maximum_fusion.2), channel_id=1, source_target_pairs={{0,16},{4,20},{8,24},{12,28},{16,0},{20,4},{24,8},{28,12},{1,17},{... | collective-permute-start | bytes 983048 | tf_op jit(solution)/shard_map/ppermute | solution.py:346
  54.4 4.5 %saturate.7 = (bf16[8,48,256]{2,1,0:T(8,128)(2,1)S(1)}, f32[8,48,1]{2,1,0:T(8,128)S(1)}) custom-call(bf16[130,48,256]{2,1,0:T(8,128)(2,1)S(1)} %get-tuple-element.61.packed, bf16[256,160]{1,0:T(8,128)(2,1)S(1)} %maximum_maximum_fusion.weights, bf16[128,128]{1,0:T(8,128)(2,1)S(1)} %copy-done.3, f32[8,128]{1,0:T(8,128)S(1)} %convert_element_type.5.mask, ...), custom_call_target="tpu_custom_call" | custom-call | flops 1610612736 | bytes 4194304 | tf_op jit(solution)/shard_map/saturate/pallas_call | solution.py:441
  59.0 1.5 %collective-permute-done.10 = bf16[8,80,256]{2,1,0:T(8,128)(2,1)S(1)} collective-permute-done((bf16[8,80,256]{2,1,0:T(8,128)(2,1)S(1)}, bf16[8,80,256]{2,1,0:T(8,128)(2,1)S(1)}, u32[]{:S(2)}, u32[]{:S(2)}) %collective-permute-start.10) | collective-permute-done | bytes 327712 | tf_op jit(solution)/shard_map/ppermute | solution.py:346
  60.6 0.9 %moments.1 = (bf16[16,128,256]{2,1,0:T(8,128)(2,1)S(1)}, f32[16,128,1]{2,1,0:T(8,128)S(1)}) custom-call(bf16[16,128,256]{2,1,0:T(8,128)(2,1)S(1)} %bitcast.31), custom_call_target="tpu_custom_call" | custom-call | tf_op jit(solution)/shard_map/moments/pallas_call | solution.py:456
  61.5 1.2 %collective-permute-done.11 = bf16[16,80,256]{2,1,0:T(8,128)(2,1)S(1)} collective-permute-done((bf16[16,80,256]{2,1,0:T(8,128)(2,1)S(1)}, bf16[16,80,256]{2,1,0:T(8,128)(2,1)S(1)}, u32[]{:S(2)}, u32[]{:S(2)}) %collective-permute-start.11) | collective-permute-done | bytes 655392 | tf_op jit(solution)/shard_map/ppermute | solution.py:346
  62.7 0.1 pad_maximum_fusion.refs_0_
  62.8 14.6 %update.1 = bf16[24,128,256]{2,1,0:T(8,128)(2,1)} custom-call(bf16[32,80,256]{2,1,0:T(8,128)(2,1)S(1)} %pad_maximum_fusion.refs_0_, bf16[16,128,256]{2,1,0:T(8,128)(2,1)S(1)} %get-tuple-element.65.refs_1_, f32[16,128,1]{2,1,0:T(8,128)S(1)} %get-tuple-element.66.refs_2_, bf16[8,16,256]{2,1,0:T(8,128)(2,1)S(1)} %get-tuple-element.67.refs_3_, ...), custom_call_target="tpu_custom_call" | custom-call | tf_op jit(solution)/shard_map/update/pallas_call | solution.py:480
  (54 shorter events, 1.1 us)
Async XLA Ops:
  0.0 12.8 %copy-start = (bf16[54,32]{0,1:T(8,128)(2,1)S(1)}, bf16[54,32]{0,1:T(8,128)(2,1)}, u32[]{:S(2)}) copy-start(bf16[54,32]{0,1:T(8,128)(2,1)} %param.13) | copy-start | bytes 10372
  0.0 2.2 %copy-start.1 = (bf16[2,2,4,128,256]{4,3,2,1,0:T(8,128)(2,1)S(1)}, bf16[2,2,4,128,256]{4,3,2,1,0:T(8,128)(2,1)}, u32[]{:S(2)}) copy-start(bf16[2,2,4,128,256]{4,3,2,1,0:T(8,128)(2,1)} %param.11) | copy-start | bytes 3145732
  2.2 9.9 %copy-start.9 = (f32[32]{0:T(128)S(1)}, f32[32]{0:T(128)}, u32[]{:S(2)}) copy-start(f32[32]{0:T(128)} %param.14) | copy-start | bytes 388
  2.2 10.7 %copy-start.6 = (bf16[54,1152]{1,0:T(8,128)(2,1)S(1)}, bf16[54,1152]{1,0:T(8,128)(2,1)}, u32[]{:S(2)}) copy-start(bf16[54,1152]{1,0:T(8,128)(2,1)} %constant.35.clone) | copy-start | bytes 373252
  2.2 10.8 %copy-start.10 = (f32[32]{0:T(128)S(1)}, f32[32]{0:T(128)}, u32[]{:S(2)}) copy-start(f32[32]{0:T(128)} %param.15) | copy-start | bytes 388
  2.2 11.3 %copy-start.4 = (s32[2,4,128]{2,1,0:T(4,128)S(1)}, s32[2,4,128]{2,1,0:T(4,128)}, u32[]{:S(2)}) copy-start(s32[2,4,128]{2,1,0:T(4,128)} %param.12) | copy-start | bytes 12292
  2.2 11.4 %copy-start.7 = (f32[64]{0:T(128)S(1)}, f32[64]{0:T(128)}, u32[]{:S(2)}) copy-start(f32[64]{0:T(128)} %param.17) | copy-start | bytes 772
  2.2 11.4 %copy-start.8 = (f32[64]{0:T(128)S(1)}, f32[64]{0:T(128)}, u32[]{:S(2)}) copy-start(f32[64]{0:T(128)} %param.18) | copy-start | bytes 772
  3.1 11.7 %collective-permute-start.3 = (bf16[2,2,1,128,256]{4,3,0,2,1:T(8,128)(2,1)}, bf16[2,2,1,128,256]{4,3,0,2,1:T(8,128)(2,1)S(1)}, u32[]{:S(2)}, u32[]{:S(2)}) collective-permute-start(bf16[2,2,1,128,256]{4,3,0,2,1:T(8,128)(2,1)} %get-tuple-element.75), channel_id=1, source_target_pairs={{1,0},{2,1},{3,2},{5,4},{6,5},{7,6},{9,8},{10,9},{11,10},{13,12},{... | collective-permute-start | bytes 786440 | tf_op jit(solution)/shard_map/ppermute | solution.py:328
  4.4 11.4 %collective-permute-start.2 = (bf16[2,2,1,128,256]{4,3,0,2,1:T(8,128)(2,1)}, bf16[2,2,1,128,256]{4,3,0,2,1:T(8,128)(2,1)S(1)}, u32[]{:S(2)}, u32[]{:S(2)}) collective-permute-start(bf16[2,2,1,128,256]{4,3,0,2,1:T(8,128)(2,1)} %get-tuple-element.76), channel_id=1, source_target_pairs={{0,1},{1,2},{2,3},{4,5},{5,6},{6,7},{8,9},{9,10},{10,11},{12,13},{... | collective-permute-start | bytes 786440 | tf_op jit(solution)/shard_map/ppermute | solution.py:328
  9.9 14.7 %collective-permute-start = (bf16[2,1,4,128,256]{4,3,0,2,1:T(8,128)(2,1)S(1)}, bf16[2,1,4,128,256]{4,3,0,2,1:T(8,128)(2,1)S(1)}, u32[]{:S(2)}, u32[]{:S(2)}) collective-permute-start(bf16[2,1,4,128,256]{4,3,0,2,1:T(8,128)(2,1)S(1)} %copy.32), channel_id=1, source_target_pairs={{0,28},{4,8},{8,4},{12,16},{16,12},{20,24},{24,20},{28,0},{1,29},{... | collective-permute-start | bytes 1572872 | tf_op jit(solution)/shard_map/ppermute | solution.py:337
  11.8 19.5 %collective-permute-start.1 = (bf16[2,1,4,128,256]{4,3,2,1,0:T(8,128)(2,1)}, bf16[2,1,4,128,256]{4,3,2,1,0:T(8,128)(2,1)S(1)}, u32[]{:S(2)}, u32[]{:S(2)}) collective-permute-start(bf16[2,1,4,128,256]{4,3,2,1,0:T(8,128)(2,1)} %get-tuple-element.41), channel_id=1, source_target_pairs={{0,4},{4,0},{8,12},{12,8},{16,20},{20,16},{24,28},{28,24},{1,5},{5... | collective-permute-start | bytes 1572872 | tf_op jit(solution)/shard_map/ppermute | solution.py:337
  15.8 15.4 %collective-permute-start.6 = (bf16[4,1,1,128,256]{4,3,0,2,1:T(8,128)(2,1)S(1)}, bf16[4,1,1,128,256]{4,3,0,2,1:T(8,128)(2,1)S(1)}, u32[]{:S(2)}, u32[]{:S(2)}) collective-permute-start(bf16[4,1,1,128,256]{4,3,0,2,1:T(8,128)(2,1)S(1)} %pad_maximum_fusion.3), channel_id=1, source_target_pairs={{0,4},{4,0},{8,12},{12,8},{16,20},{20,16},{24,28},{28,24},{1,5},{5... | collective-permute-start | bytes 786440 | tf_op jit(solution)/shard_map/ppermute | solution.py:337
  24.7 8.9 %copy-start.2 = (bf16[256,256]{1,0:T(8,128)(2,1)S(1)}, bf16[256,256]{1,0:T(8,128)(2,1)}, u32[]{:S(2)}) copy-start(bf16[256,256]{1,0:T(8,128)(2,1)} %constant.36.clone.swap_in) | copy-start | bytes 393220
  24.7 8.9 %copy-start.5 = (s32[64]{0:T(128)S(1)}, s32[64]{0:T(128)}, u32[]{:S(2)}) copy-start(s32[64]{0:T(128)} %cells.1) | copy-start | bytes 772
  24.7 7.4 %collective-permute-start.5 = (bf16[2,1,1,128,256]{4,3,0,2,1:T(8,128)(2,1)S(1)}, bf16[2,1,1,128,256]{4,3,0,2,1:T(8,128)(2,1)S(1)}, u32[]{:S(2)}, u32[]{:S(2)}) collective-permute-start(bf16[2,1,1,128,256]{4,3,0,2,1:T(8,128)(2,1)S(1)} %get-tuple-element.79), channel_id=1, source_target_pairs={{1,0},{2,1},{3,2},{5,4},{6,5},{7,6},{9,8},{10,9},{11,10},{13,12},{... | collective-permute-start | bytes 393224 | tf_op jit(solution)/shard_map/ppermute | solution.py:328
  26.1 7.4 %collective-permute-start.4 = (bf16[2,1,1,128,256]{4,3,0,2,1:T(8,128)(2,1)S(1)}, bf16[2,1,1,128,256]{4,3,0,2,1:T(8,128)(2,1)S(1)}, u32[]{:S(2)}, u32[]{:S(2)}) collective-permute-start(bf16[2,1,1,128,256]{4,3,0,2,1:T(8,128)(2,1)S(1)} %get-tuple-element.80), channel_id=1, source_target_pairs={{0,1},{1,2},{2,3},{4,5},{5,6},{6,7},{8,9},{9,10},{10,11},{12,13},{... | collective-permute-start | bytes 393224 | tf_op jit(solution)/shard_map/ppermute | solution.py:328
  33.6 7.4 %copy-start.3 = (bf16[128,128]{1,0:T(8,128)(2,1)S(1)}, bf16[128,128]{1,0:T(8,128)(2,1)}, u32[]{:S(2)}) copy-start(bf16[128,128]{1,0:T(8,128)(2,1)} %constant.37.clone.swap_out) | copy-start | bytes 98308
  37.0 6.0 %collective-permute-start.7 = (bf16[1,80,256]{2,1,0:T(8,128)(2,1)S(1)}, bf16[1,80,256]{2,1,0:T(8,128)(2,1)S(1)}, u32[]{:S(2)}, u32[]{:S(2)}) collective-permute-start(bf16[1,80,256]{2,1,0:T(8,128)(2,1)S(1)} %bitcast.39), channel_id=1, source_target_pairs={{0,2},{1,3},{2,0},{3,1},{4,6},{5,7},{6,4},{7,5},{8,10},{9,11},{10,... | collective-permute-start | bytes 122888 | tf_op jit(solution)/shard_map/ppermute | solution.py:346
  43.0 4.9 %collective-permute-start.8 = (bf16[2,80,256]{2,1,0:T(8,128)(2,1)S(1)}, bf16[2,80,256]{2,1,0:T(8,128)(2,1)S(1)}, u32[]{:S(2)}, u32[]{:S(2)}) collective-permute-start(bf16[2,80,256]{2,1,0:T(8,128)(2,1)S(1)} %pad_maximum_fusion.5), channel_id=1, source_target_pairs={{0,1},{1,0},{2,3},{3,2},{4,5},{5,4},{6,7},{7,6},{8,9},{9,8},{10,11... | collective-permute-start | bytes 245768 | tf_op jit(solution)/shard_map/ppermute | solution.py:346
  47.9 5.4 %collective-permute-start.9 = (bf16[4,80,256]{2,1,0:T(8,128)(2,1)S(1)}, bf16[4,80,256]{2,1,0:T(8,128)(2,1)S(1)}, u32[]{:S(2)}, u32[]{:S(2)}) collective-permute-start(bf16[4,80,256]{2,1,0:T(8,128)(2,1)S(1)} %pad_maximum_fusion.4), channel_id=1, source_target_pairs={{0,8},{4,12},{8,0},{12,4},{16,24},{20,28},{24,16},{28,20},{1,9},{5... | collective-permute-start | bytes 491528 | tf_op jit(solution)/shard_map/ppermute | solution.py:346
  53.3 7.1 %collective-permute-start.10 = (bf16[8,80,256]{2,1,0:T(8,128)(2,1)S(1)}, bf16[8,80,256]{2,1,0:T(8,128)(2,1)S(1)}, u32[]{:S(2)}, u32[]{:S(2)}) collective-permute-start(bf16[8,80,256]{2,1,0:T(8,128)(2,1)S(1)} %pad_maximum_fusion.2), channel_id=1, source_target_pairs={{0,16},{4,20},{8,24},{12,28},{16,0},{20,4},{24,8},{28,12},{1,17},{... | collective-permute-start | bytes 983048 | tf_op jit(solution)/shard_map/ppermute | solution.py:346
  60.5 2.2 %collective-permute-start.11 = (bf16[16,80,256]{2,1,0:T(8,128)(2,1)S(1)}, bf16[16,80,256]{2,1,0:T(8,128)(2,1)S(1)}, u32[]{:S(2)}, u32[]{:S(2)}) collective-permute-start(bf16[16,80,256]{2,1,0:T(8,128)(2,1)S(1)} %pad_maximum_fusion.1), channel_id=1, source_target_pairs={{0,4},{4,0},{8,12},{12,8},{16,20},{20,16},{24,28},{28,24},{1,5},{5... | collective-permute-start | bytes 1966088 | tf_op jit(solution)/shard_map/ppermute | solution.py:346

commit v6 on v5

--- a/solution.py
+++ b/solution.py
@@ -273,26 +273,32 @@
     else:
         total = identity + gram[...]
         coeff = coeff_in[...]
-    joint[:, 0:members] = total
-    joint[:, members:] = identity
+    joint[...] = total
     for k in range(members // BLOCK):
         at = k * BLOCK
-        inverse = inverse_factor_block(joint[at : at + BLOCK, at : at + BLOCK])
-        rows = jnp.dot(
-            inverse, joint[at : at + BLOCK, :], precision=HIGHEST, preferred_element_type=jnp.float32
+        below = at + BLOCK
+        wide_sub, wide_lane = sub[0:BLOCK, :], lane[0:BLOCK, :]
+        inside = jnp.logical_and(wide_lane >= at, wide_lane < below)
+        row = joint[at:below, :]
+        inverse = inverse_factor_block(row[:, at:below])
+        unit = jnp.where(wide_lane == wide_sub + at, 1.0, 0.0)
+        row = jnp.dot(
+            inverse,
+            jnp.where(inside, unit, row),
+            precision=HIGHEST,
+            preferred_element_type=jnp.float32,
         )
-        joint[at : at + BLOCK, :] = rows
-        if at + BLOCK < members:
-            joint[at + BLOCK :, :] = joint[at + BLOCK :, :] - transposed_dot(
-                rows[:, at + BLOCK : members], rows, HIGHEST
-            )
-    inverse = joint[:, members:]
-    wide = jnp.broadcast_to(coeff, (8, members))
-    half = lax.dot_general(
-        wide, inverse, (((1,), (1,)), ((), ())), preferred_element_type=jnp.float32, precision=HIGHEST
-    )
-    weight = jnp.dot(half, inverse, preferred_element_type=jnp.float32, precision=HIGHEST)
-    mixing[...] = jnp.transpose(inverse + weight[0:1, :]).astype(jnp.bfloat16)
+        joint[at:below, :] = row
+        if below < members:
+            ahead = jnp.where(wide_lane >= below, row, 0.0)
+            change = transposed_dot(ahead, row, HIGHEST)
+            rest_lane = lane[below:, :]
+            inside = jnp.logical_and(rest_lane >= at, rest_lane < below)
+            joint[below:, :] = jnp.where(inside, 0.0, joint[below:, :]) - change[below:, :]
+    inverse = jnp.where(lane <= sub, joint[...], 0.0)
+    half = jnp.sum(inverse * coeff, axis=1, keepdims=True)
+    weight = jnp.sum(inverse * half, axis=0, keepdims=True)
+    mixing[...] = jnp.transpose((inverse + weight).astype(jnp.bfloat16))
 
     def blend(anomalies, mean):
         outer, inner = anomalies.shape[0], anomalies.shape[1]
@@ -328,13 +334,25 @@
     return lax.ppermute(value, axis, pairs)
 
 
+def core_pairs(inside):
+    count = lax.axis_size("cores")
+    steps = [1 if (i % 2 == 0) == inside else -1 for i in range(count)]
+    return [(i, (i + step) % count) for i, step in enumerate(steps)]
+
+
 def swap_cores(value, inside):
-    count = lax.axis_size("cores")
-    pairs = []
-    for i in range(count):
-        step = 1 if (i % 2 == 0) == inside else -1
-        pairs.append((i, (i + step) % count))
-    return lax.ppermute(value, "cores", pairs)
+    return lax.ppermute(value, "cores", core_pairs(inside))
+
+
+def swap_far_corner(value, face_by):
+    face_count = lax.axis_size("face")
+    pairs = [
+        (i * face_count + j, other * face_count + j + face_by)
+        for i, other in core_pairs(False)
+        for j in range(face_count)
+        if 0 <= j + face_by < face_count
+    ]
+    return lax.ppermute(value, ("cores", "face"), pairs)
 
 
 def gather_rows(block, steps, packed, saturate):
@@ -387,13 +405,13 @@
     near_plane = (1 - odd) * (planes - 1)
     far = lax.dynamic_slice_in_dim(fields, odd * (planes - 1), 1, axis=1)
     near = lax.dynamic_slice_in_dim(fields, near_plane, 1, axis=1)
-    far, near, tied = lax.optimization_barrier((far, near, fields))
+    far, near = lax.optimization_barrier((far, near))
+    far_left = swap_far_corner(far[:, :, -1:], 1)
+    far_right = swap_far_corner(far[:, :, :1], -1)
     far = swap_cores(far, False)
-    near = swap_cores(near, True)
+    near, tied = lax.optimization_barrier((swap_cores(near, True), fields))
     left = shift(tied[:, :, -1:], "face", 1, False)
     right = shift(tied[:, :, :1], "face", -1, False)
-    far_left = shift(far[:, :, -1:], "face", 1, False)
-    far_right = shift(far[:, :, :1], "face", -1, False)
     near_sides = [lax.dynamic_slice_in_dim(side, near_plane, 1, axis=1) for side in (left, right)]
     near_corner = swap_cores(jnp.concatenate(near_sides, axis=0), True)
 
@@ -419,6 +437,15 @@
     swap_in = jnp.asarray(swap_matrix(16, 16), jnp.bfloat16)
     swap_out = jnp.asarray(swap_matrix(16, rows), jnp.bfloat16)
     params = pltpu.CompilerParams(vmem_limit_bytes=VMEM_BYTES)
+    field_moments = pl.pallas_call(
+        moments_kernel,
+        out_shape=moments_shape(2 * rows, lanes, members),
+        in_specs=[vmem()],
+        out_specs=(vmem(), vmem()),
+        compiler_params=params,
+        name="moments",
+    )(flat(fields))
+    by_row, field_moments = lax.optimization_barrier((by_row, tuple(field_moments)))
     packed, pay = pl.pallas_call(
         observe_kernel,
         out_shape=(
@@ -453,14 +480,6 @@
             name="saturate",
         )(packed, weights, swap_out, mask_float, read_half)
 
-    field_moments = pl.pallas_call(
-        moments_kernel,
-        out_shape=moments_shape(2 * rows, lanes, members),
-        in_specs=[vmem()],
-        out_specs=(vmem(), vmem()),
-        compiler_params=params,
-        name="moments",
-    )(flat(fields))
     core_count, face_count = lax.axis_size("cores"), lax.axis_size("face")
     devices = core_count * face_count
     gathered = devices <= GATHER_DEVICES and devices & (devices - 1) == 0
@@ -483,7 +502,7 @@
         in_specs=[vmem()] * (len(terms) + 2 + 2 * len(SPANS)),
         out_specs=vmem(),
         scratch_shapes=[
-            pltpu.VMEM((members, 2 * members), jnp.float32),
+            pltpu.VMEM((members, members), jnp.float32),
             pltpu.VMEM((members, members), jnp.bfloat16),
         ],
         compiler_params=params,

time: 77.7 us -> 80.3 us (1.033)
  local copies, waits for them, and re-layouts: 4.73 us -> 11.7 us
  waiting for transfers between devices: 16 us -> 10.5 us
  other arithmetic: 1.32 us -> 2.7 us
    ppermute x3 -> x5, waiting for transfers between devices: 8.74 us -> 0.01 us  [the longest x3 0.01 us: swap_cores(): return lax.ppermute(value, 'cores', core_pairs(inside))]
    ppermute x3 -> x5, starting transfers between devices: 2.18 us -> 8.94 us  [the longest x2 4.93 us: swap_far_corner(): return lax.ppermute(value, ('cores', 'face'), pairs)]
    ppermute x4 -> x2, starting transfers between devices: 13.2 us -> 8.48 us  [shift(): return lax.ppermute(value, axis, pairs)]
    ppermute x5, waiting for transfers between devices: 3.98 us -> 7.22 us  [gather_rows(): other = lax.ppermute(block, axis, [(i, i ^ bit) for i in range(count)])]
    ppermute x5, starting transfers between devices: 7.63 us -> 5.15 us  [gather_rows(): other = lax.ppermute(block, axis, [(i, i ^ bit) for i in range(count)])]
    slice x1, local copies, waits for them, and re-layouts: 0.02 us -> 1.69 us  [shards(): far_right = swap_far_corner(far[:, :, :1], -1)]
    broadcast_in_dim x1, local copies, waits for them, and re-layouts: 0.1 us -> 1.36 us  [shards(): obs_values[:, None]]
    broadcast_in_dim x1, local copies, waits for them, and re-layouts: 0.1 us -> 1.34 us  [shards(): obs_sigma[:, None]]
  transfers between devices with their start and end apart: 12 -> 12, of which waited for: 7 -> 6; matrix products, arithmetic and copies ran while one was open for 4% -> 14% of each run, Pallas kernels for 18% -> 18%
where the time goes in v6:
time: 80.3 us; the launch traced here: 79.9 us
  Pallas kernels  31.9 us (40%)
  starting transfers between devices  22.6 us (28%)
  local copies, waits for them, and re-layouts  11.7 us (15%)
  waiting for transfers between devices  10.5 us (13%)
  other arithmetic  2.7 us (3%)
    pallas_call x1, Pallas kernels, shards(): pl.pallas_call(functools.partial(update_kernel, gathered), out_shape=jax....  14.2 us
    pallas_call x4, Pallas kernels, saturate(): pl.pallas_call(functools.partial(saturate_kernel, starts[n]), out_shape=m...  13.2 us
    ppermute x2, starting transfers between devices, shift(): return lax.ppermute(value, axis, pairs)  8.48 us
    ppermute x5, waiting for transfers between devices, gather_rows(): other = lax.ppermute(block, axis, [(i, i ^ bit) for i in range(count)])  7.22 us
    ppermute x5, starting transfers between devices, gather_rows(): other = lax.ppermute(block, axis, [(i, i ^ bit) for i in range(count)])  5.15 us
    ppermute x2, starting transfers between devices, swap_far_corner(): return lax.ppermute(value, ('cores', 'face'), pairs)  4.93 us
    ppermute x3, starting transfers between devices, swap_cores(): return lax.ppermute(value, 'cores', core_pairs(inside))  4.01 us
    pallas_call x1, Pallas kernels, shards(): pl.pallas_call(observe_kernel, out_shape=(jax.ShapeDtypeStruct((lanes + 2...  3.61 us
  transfers between devices with their start and end apart: 12, of which 6 were waited for; matrix products, arithmetic and copies ran while one was open for 14% of the time, Pallas kernels for 18%

profile of v6, /device:TPU:0, one launch (start us, length us, event | category | flops | bytes accessed | tf_op | source)
XLA Modules:
  0.0 79.9 jit_solution(16607710731559572395)
XLA Ops:
  0.0 1.3 %constant_dynamic-slice_fusion.2 = (bf16[2,1,4,128,256]{4,3,2,1,0:T(8,128)(2,1)S(1)}, bf16[2,1,4,128,256]{4,3,2,1,0:T(8,128)(2,1)S(1)}) fusion(bf16[2,2,4,128,256]{4,3,2,1,0:T(8,128)(2,1)} %param.11, s32[]{:T(128)S(6)} %select_n.17, s32[]{:T(128)S(6)} %select_n.16), kind=kLoop, calls=%fused_computation.15 | loop fusion | bytes 2097160 | tf_op jit(solution)/shard_map/dynamic_slice | solution.py:407
  1.3 0.8 %copy.32 = bf16[2,1,4,128,256]{4,3,0,2,1:T(8,128)(2,1)} copy(bf16[2,1,4,128,256]{4,3,2,1,0:T(8,128)(2,1)S(1)} %get-tuple-element.86) | data formatting | bytes 1048576 | tf_op jit(solution)/shard_map/optimization_barrier | solution.py:408
  2.6 3.6 %collective-permute-start = (bf16[2,1,4,128,256]{4,3,0,2,1:T(8,128)(2,1)}, bf16[2,1,4,128,256]{4,3,0,2,1:T(8,128)(2,1)}, u32[]{:S(2)}, u32[]{:S(2)}) collective-permute-start(bf16[2,1,4,128,256]{4,3,0,2,1:T(8,128)(2,1)} %copy.32), channel_id=1, source_target_pairs={{0,28},{4,8},{8,4},{12,16},{16,12},{20,24},{24,20},{28,0},{1,29},{... | collective-permute-start | bytes 1572872 | tf_op jit(solution)/shard_map/ppermute | solution.py:344
  6.2 1.7 %fusion.6 = (bf16[2,1,1,128,256]{4,3,0,2,1:T(8,128)(2,1)}, bf16[2,1,1,128,256]{4,3,0,2,1:T(8,128)(2,1)}) fusion(bf16[2,1,4,128,256]{4,3,0,2,1:T(8,128)(2,1)} %copy.32), kind=kLoop, calls=%fused_computation.26 | loop fusion | bytes 524288 | tf_op jit(solution)/shard_map/slice | solution.py:410
  7.9 3.7 %collective-permute-start.4 = (bf16[2,1,1,128,256]{4,3,0,2,1:T(8,128)(2,1)}, bf16[2,1,1,128,256]{4,3,0,2,1:T(8,128)(2,1)}, u32[]{:S(2)}, u32[]{:S(2)}) collective-permute-start(bf16[2,1,1,128,256]{4,3,0,2,1:T(8,128)(2,1)} %get-tuple-element.88), channel_id=1, source_target_pairs={{0,29},{1,30},{2,31},{4,9},{5,10},{6,11},{8,5},{9,6},{10,7},{12,17... | collective-permute-start | bytes 393224 | tf_op jit(solution)/shard_map/ppermute | solution.py:355
  11.5 1.3 %collective-permute-start.5 = (bf16[2,1,1,128,256]{4,3,0,2,1:T(8,128)(2,1)}, bf16[2,1,1,128,256]{4,3,0,2,1:T(8,128)(2,1)}, u32[]{:S(2)}, u32[]{:S(2)}) collective-permute-start(bf16[2,1,1,128,256]{4,3,0,2,1:T(8,128)(2,1)} %get-tuple-element.87), channel_id=1, source_target_pairs={{1,28},{2,29},{3,30},{5,8},{6,9},{7,10},{9,4},{10,5},{11,6},{13,16... | collective-permute-start | bytes 393224 | tf_op jit(solution)/shard_map/ppermute | solution.py:355
  13.5 1.3 %collective-permute-start.3 = (bf16[2,2,1,128,256]{4,3,0,2,1:T(8,128)(2,1)S(1)}, bf16[2,2,1,128,256]{4,3,0,2,1:T(8,128)(2,1)S(1)}, u32[]{:S(2)}, u32[]{:S(2)}) collective-permute-start(bf16[2,2,1,128,256]{4,3,0,2,1:T(8,128)(2,1)S(1)} %get-tuple-element.83), channel_id=1, source_target_pairs={{1,0},{2,1},{3,2},{5,4},{6,5},{7,6},{9,8},{10,9},{11,10},{13,12},{... | collective-permute-start | bytes 786440 | tf_op jit(solution)/shard_map/ppermute | solution.py:334
  14.9 7.2 %collective-permute-start.2 = (bf16[2,2,1,128,256]{4,3,0,2,1:T(8,128)(2,1)S(1)}, bf16[2,2,1,128,256]{4,3,0,2,1:T(8,128)(2,1)S(1)}, u32[]{:S(2)}, u32[]{:S(2)}) collective-permute-start(bf16[2,2,1,128,256]{4,3,0,2,1:T(8,128)(2,1)S(1)} %get-tuple-element.84), channel_id=1, source_target_pairs={{0,1},{1,2},{2,3},{4,5},{5,6},{6,7},{8,9},{9,10},{10,11},{12,13},{... | collective-permute-start | bytes 786440 | tf_op jit(solution)/shard_map/ppermute | solution.py:334
  22.1 0.6 broadcast_bitcast_fusion
  22.8 3.3 %collective-permute-done.3 = bf16[2,2,1,128,256]{4,3,0,2,1:T(8,128)(2,1)S(1)} collective-permute-done((bf16[2,2,1,128,256]{4,3,0,2,1:T(8,128)(2,1)S(1)}, bf16[2,2,1,128,256]{4,3,0,2,1:T(8,128)(2,1)S(1)}, u32[]{:S(2)}, u32[]{:S(2)}) %collective-permute-start.3) | collective-permute-done | bytes 262176 | tf_op jit(solution)/shard_map/ppermute | solution.py:334
  26.1 0.7 copy-done.12
  26.8 0.7 pad_maximum_fusion.3
  28.1 0.9 %mul.24 = bf16[256,144]{1,0:T(8,128)(2,1)} reshape(bf16[32,1152]{1,0:T(8,128)(2,1)S(1)} %fusion.1) | data formatting | bytes 147456 | tf_op jit(solution)/shard_map/mul | solution.py:428
  28.9 0.9 %moments.1 = (bf16[16,128,256]{2,1,0:T(8,128)(2,1)S(1)}, f32[16,128,1]{2,1,0:T(8,128)S(1)}) custom-call(bf16[16,128,256]{2,1,0:T(8,128)(2,1)S(1)} %bitcast.30), custom_call_target="tpu_custom_call" | custom-call | tf_op jit(solution)/shard_map/moments/pallas_call | solution.py:440
  29.9 1.3 %copy.28.read_column = f32[32,1]{1,0:T(8,128)} copy(f32[32,1]{0,1:T(1,128)} %get-tuple-element.90) | data formatting | bytes 256 | tf_op jit(solution)/shard_map/broadcast_in_dim | solution.py:462
  31.2 1.3 %copy.29.sigma = f32[64,1]{1,0:T(8,128)} copy(f32[64,1]{0,1:T(1,128)} %bitcast.41) | data formatting | bytes 512 | tf_op jit(solution)/shard_map/broadcast_in_dim | solution.py:463
  32.5 1.4 %copy.30.values = f32[64,1]{1,0:T(8,128)} copy(f32[64,1]{0,1:T(1,128)} %bitcast.42) | data formatting | bytes 512 | tf_op jit(solution)/shard_map/broadcast_in_dim | solution.py:463
  33.9 1.1 %maximum_maximum_fusion.weights = bf16[256,160]{1,0:T(8,128)(2,1)S(1)} fusion(bf16[256,3]{1,0:T(8,128)(2,1)} %broadcast_bitcast_fusion, bf16[256,144]{1,0:T(8,128)(2,1)} %mul.24, bf16[160]{0:T(256)(128)(2,1)} %copy-done.17), kind=kLoop, calls=%fused_computation.9 | loop fusion | flops 245760 | bytes 157504 | tf_op jit(solution)/shard_map/concatenate | solution.py:427
  35.0 1.1 %copy.21 = bf16[2,1,4,128,256]{4,3,2,0,1:T(8,128)(2,1)S(1)} copy(bf16[2,1,4,128,256]{4,3,0,2,1:T(8,128)(2,1)} %collective-permute-done) | data formatting | bytes 1048576 | tf_op jit(solution)/shard_map/ppermute | solution.py:344
  36.3 3.6 %observe.1 = (bf16[130,48,256]{2,1,0:T(8,128)(2,1)S(1)}, bf16[80,256]{1,0:T(8,128)(2,1)S(1)}) custom-call(bf16[16,128,256]{2,1,0:T(8,128)(2,1)S(1)} %bitcast.31, bf16[8,128,256]{2,1,0:T(8,128)(2,1)S(1)} %bitcast.32, bf16[8,128,256]{2,1,0:T(8,128)(2,1)S(1)} %bitcast.35, bf16[4,128,256]{2,1,0:T(8,128)(2,1)S(1)} %bitcast.33, bf16[4,128,256]{2,1,0:T(8,128)(2,1)S(1)} %bitcast.34, ...), custom_call_target="tpu_custom_call" | custom-call | tf_op jit(solution)/shard_map/observe/pallas_call | solution.py:449
  39.9 3.3 %collective-permute-start.7 = (bf16[1,80,256]{2,1,0:T(8,128)(2,1)S(1)}, bf16[1,80,256]{2,1,0:T(8,128)(2,1)S(1)}, u32[]{:S(2)}, u32[]{:S(2)}) collective-permute-start(bf16[1,80,256]{2,1,0:T(8,128)(2,1)S(1)} %bitcast.37), channel_id=1, source_target_pairs={{0,2},{1,3},{2,0},{3,1},{4,6},{5,7},{6,4},{7,5},{8,10},{9,11},{10,... | collective-permute-start | bytes 122888 | tf_op jit(solution)/shard_map/ppermute | solution.py:364
  43.2 2.0 %saturate.4 = (bf16[8,16,256]{2,1,0:T(8,128)(2,1)S(1)}, f32[8,16,1]{2,1,0:T(8,128)S(1)}) custom-call(bf16[130,48,256]{2,1,0:T(8,128)(2,1)S(1)} %get-tuple-element.69.packed, bf16[256,160]{1,0:T(8,128)(2,1)S(1)} %maximum_maximum_fusion.weights, bf16[128,128]{1,0:T(8,128)(2,1)S(1)} %copy-done.8, f32[8,128]{1,0:T(8,128)S(1)} %convert_element_type.5.mask, ...), custom_call_target="tpu_custom_call" | custom-call | flops 536870912 | bytes 4194304 | tf_op jit(solution)/shard_map/saturate/pallas_call | solution.py:468
  45.2 1.1 %collective-permute-done.7 = bf16[1,80,256]{2,1,0:T(8,128)(2,1)S(1)} collective-permute-done((bf16[1,80,256]{2,1,0:T(8,128)(2,1)S(1)}, bf16[1,80,256]{2,1,0:T(8,128)(2,1)S(1)}, u32[]{:S(2)}, u32[]{:S(2)}) %collective-permute-start.7) | collective-permute-done | bytes 40992 | tf_op jit(solution)/shard_map/ppermute | solution.py:364
  46.8 3.3 %saturate.5 = (bf16[8,32,256]{2,1,0:T(8,128)(2,1)S(1)}, f32[8,32,1]{2,1,0:T(8,128)S(1)}) custom-call(bf16[130,48,256]{2,1,0:T(8,128)(2,1)S(1)} %get-tuple-element.69.packed, bf16[256,160]{1,0:T(8,128)(2,1)S(1)} %maximum_maximum_fusion.weights, bf16[128,128]{1,0:T(8,128)(2,1)S(1)} %copy-done.8, f32[8,128]{1,0:T(8,128)S(1)} %convert_element_type.5.mask, ...), custom_call_target="tpu_custom_call" | custom-call | flops 1073741824 | bytes 4194304 | tf_op jit(solution)/shard_map/saturate/pallas_call | solution.py:468
  50.0 0.8 collective-permute-done.8
  51.4 3.3 %saturate.6 = (bf16[8,32,256]{2,1,0:T(8,128)(2,1)S(1)}, f32[8,32,1]{2,1,0:T(8,128)S(1)}) custom-call(bf16[130,48,256]{2,1,0:T(8,128)(2,1)S(1)} %get-tuple-element.69.packed, bf16[256,160]{1,0:T(8,128)(2,1)S(1)} %maximum_maximum_fusion.weights, bf16[128,128]{1,0:T(8,128)(2,1)S(1)} %copy-done.8, f32[8,128]{1,0:T(8,128)S(1)} %convert_element_type.5.mask, ...), custom_call_target="tpu_custom_call" | custom-call | flops 1073741824 | bytes 4194304 | tf_op jit(solution)/shard_map/saturate/pallas_call | solution.py:468
  54.7 1.5 %collective-permute-done.9 = bf16[4,80,256]{2,1,0:T(8,128)(2,1)S(1)} collective-permute-done((bf16[4,80,256]{2,1,0:T(8,128)(2,1)S(1)}, bf16[4,80,256]{2,1,0:T(8,128)(2,1)S(1)}, u32[]{:S(2)}, u32[]{:S(2)}) %collective-permute-start.9) | collective-permute-done | bytes 163872 | tf_op jit(solution)/shard_map/ppermute | solution.py:364
  56.2 0.7 collective-permute-start.10
  57.0 4.7 %saturate.7 = (bf16[8,48,256]{2,1,0:T(8,128)(2,1)S(1)}, f32[8,48,1]{2,1,0:T(8,128)S(1)}) custom-call(bf16[130,48,256]{2,1,0:T(8,128)(2,1)S(1)} %get-tuple-element.69.packed, bf16[256,160]{1,0:T(8,128)(2,1)S(1)} %maximum_maximum_fusion.weights, bf16[128,128]{1,0:T(8,128)(2,1)S(1)} %copy-done.8, f32[8,128]{1,0:T(8,128)S(1)} %convert_element_type.5.mask, ...), custom_call_target="tpu_custom_call" | custom-call | flops 1610612736 | bytes 4194304 | tf_op jit(solution)/shard_map/saturate/pallas_call | solution.py:468
  61.7 1.8 %collective-permute-done.10 = bf16[8,80,256]{2,1,0:T(8,128)(2,1)S(1)} collective-permute-done((bf16[8,80,256]{2,1,0:T(8,128)(2,1)S(1)}, bf16[8,80,256]{2,1,0:T(8,128)(2,1)S(1)}, u32[]{:S(2)}, u32[]{:S(2)}) %collective-permute-start.10) | collective-permute-done | bytes 327712 | tf_op jit(solution)/shard_map/ppermute | solution.py:364
  63.6 2.1 %collective-permute-done.11 = bf16[16,80,256]{2,1,0:T(8,128)(2,1)S(1)} collective-permute-done((bf16[16,80,256]{2,1,0:T(8,128)(2,1)S(1)}, bf16[16,80,256]{2,1,0:T(8,128)(2,1)S(1)}, u32[]{:S(2)}, u32[]{:S(2)}) %collective-permute-start.11) | collective-permute-done | bytes 655392 | tf_op jit(solution)/shard_map/ppermute | solution.py:364
  65.8 14.2 %update.1 = bf16[24,128,256]{2,1,0:T(8,128)(2,1)} custom-call(bf16[32,80,256]{2,1,0:T(8,128)(2,1)S(1)} %pad_maximum_fusion.refs_0_, bf16[16,128,256]{2,1,0:T(8,128)(2,1)S(1)} %get-tuple-element.73.refs_1_, f32[16,128,1]{2,1,0:T(8,128)S(1)} %get-tuple-element.74.refs_2_, bf16[8,16,256]{2,1,0:T(8,128)(2,1)S(1)} %get-tuple-element.75.refs_3_, ...), custom_call_target="tpu_custom_call" | custom-call | tf_op jit(solution)/shard_map/update/pallas_call | solution.py:499
  (72 shorter events, 3.3 us)
Async XLA Ops:
  0.0 12.9 %copy-start = (bf16[54,32]{0,1:T(8,128)(2,1)S(1)}, bf16[54,32]{0,1:T(8,128)(2,1)}, u32[]{:S(2)}) copy-start(bf16[54,32]{0,1:T(8,128)(2,1)} %param.13) | copy-start | bytes 10372
  1.3 11.5 %copy-start.18 = (f32[32]{0:T(128)S(1)}, f32[32]{0:T(128)}, u32[]{:S(2)}) copy-start(f32[32]{0:T(128)} %param.14) | copy-start | bytes 388
  1.3 11.6 %copy-start.16 = (bf16[54,1152]{1,0:T(8,128)(2,1)S(1)}, bf16[54,1152]{1,0:T(8,128)(2,1)}, u32[]{:S(2)}) copy-start(bf16[54,1152]{1,0:T(8,128)(2,1)} %constant.35.clone) | copy-start | bytes 373252
  1.3 12.1 %copy-start.1 = (bf16[2,2,4,128,256]{4,3,2,1,0:T(8,128)(2,1)S(1)}, bf16[2,2,4,128,256]{4,3,2,1,0:T(8,128)(2,1)}, u32[]{:S(2)}) copy-start(bf16[2,2,4,128,256]{4,3,2,1,0:T(8,128)(2,1)} %param.11) | copy-start | bytes 3145732
  2.2 11.3 %collective-permute-start.1 = (bf16[2,1,4,128,256]{4,3,2,1,0:T(8,128)(2,1)S(1)}, bf16[2,1,4,128,256]{4,3,2,1,0:T(8,128)(2,1)S(1)}, u32[]{:S(2)}, u32[]{:S(2)}) collective-permute-start(bf16[2,1,4,128,256]{4,3,2,1,0:T(8,128)(2,1)S(1)} %get-tuple-element.45), channel_id=1, source_target_pairs={{0,4},{4,0},{8,12},{12,8},{16,20},{20,16},{24,28},{28,24},{1,5},{5... | collective-permute-start | bytes 1572872 | tf_op jit(solution)/shard_map/ppermute | solution.py:344
  2.6 32.4 %collective-permute-start = (bf16[2,1,4,128,256]{4,3,0,2,1:T(8,128)(2,1)}, bf16[2,1,4,128,256]{4,3,0,2,1:T(8,128)(2,1)}, u32[]{:S(2)}, u32[]{:S(2)}) collective-permute-start(bf16[2,1,4,128,256]{4,3,0,2,1:T(8,128)(2,1)} %copy.32), channel_id=1, source_target_pairs={{0,28},{4,8},{8,4},{12,16},{16,12},{20,24},{24,20},{28,0},{1,29},{... | collective-permute-start | bytes 1572872 | tf_op jit(solution)/shard_map/ppermute | solution.py:344
  7.9 28.3 %collective-permute-start.4 = (bf16[2,1,1,128,256]{4,3,0,2,1:T(8,128)(2,1)}, bf16[2,1,1,128,256]{4,3,0,2,1:T(8,128)(2,1)}, u32[]{:S(2)}, u32[]{:S(2)}) collective-permute-start(bf16[2,1,1,128,256]{4,3,0,2,1:T(8,128)(2,1)} %get-tuple-element.88), channel_id=1, source_target_pairs={{0,29},{1,30},{2,31},{4,9},{5,10},{6,11},{8,5},{9,6},{10,7},{12,17... | collective-permute-start | bytes 393224 | tf_op jit(solution)/shard_map/ppermute | solution.py:355
  11.5 24.7 %collective-permute-start.5 = (bf16[2,1,1,128,256]{4,3,0,2,1:T(8,128)(2,1)}, bf16[2,1,1,128,256]{4,3,0,2,1:T(8,128)(2,1)}, u32[]{:S(2)}, u32[]{:S(2)}) collective-permute-start(bf16[2,1,1,128,256]{4,3,0,2,1:T(8,128)(2,1)} %get-tuple-element.87), channel_id=1, source_target_pairs={{1,28},{2,29},{3,30},{5,8},{6,9},{7,10},{9,4},{10,5},{11,6},{13,16... | collective-permute-start | bytes 393224 | tf_op jit(solution)/shard_map/ppermute | solution.py:355
  13.3 14.2 %copy-start.19 = (f32[32]{0:T(128)S(1)}, f32[32]{0:T(128)}, u32[]{:S(2)}) copy-start(f32[32]{0:T(128)} %param.15) | copy-start | bytes 388
  13.4 15.5 %copy-start.17 = (bf16[160]{0:T(256)(128)(2,1)}, bf16[160]{0:T(256)(128)(2,1)S(1)}, u32[]{:S(2)}) copy-start(bf16[160]{0:T(256)(128)(2,1)S(1)} %pad.15.clone) | copy-start | bytes 964
  13.5 15.5 %copy-start.2 = (bf16[2,1,4,128,256]{4,3,2,1,0:T(8,128)(2,1)}, bf16[2,1,4,128,256]{4,3,2,1,0:T(8,128)(2,1)S(1)}, u32[]{:S(2)}) copy-start(bf16[2,1,4,128,256]{4,3,2,1,0:T(8,128)(2,1)S(1)} %collective-permute-done.1) | copy-start | bytes 1572868
  13.5 12.6 %collective-permute-start.3 = (bf16[2,2,1,128,256]{4,3,0,2,1:T(8,128)(2,1)S(1)}, bf16[2,2,1,128,256]{4,3,0,2,1:T(8,128)(2,1)S(1)}, u32[]{:S(2)}, u32[]{:S(2)}) collective-permute-start(bf16[2,2,1,128,256]{4,3,0,2,1:T(8,128)(2,1)S(1)} %get-tuple-element.83), channel_id=1, source_target_pairs={{1,0},{2,1},{3,2},{5,4},{6,5},{7,6},{9,8},{10,9},{11,10},{13,12},{... | collective-permute-start | bytes 786440 | tf_op jit(solution)/shard_map/ppermute | solution.py:334
  14.9 19.0 %copy-start.9 = (s32[2,4,128]{2,1,0:T(4,128)S(1)}, s32[2,4,128]{2,1,0:T(4,128)}, u32[]{:S(2)}) copy-start(s32[2,4,128]{2,1,0:T(4,128)} %param.12) | copy-start | bytes 12292
  14.9 11.2 %collective-permute-start.2 = (bf16[2,2,1,128,256]{4,3,0,2,1:T(8,128)(2,1)S(1)}, bf16[2,2,1,128,256]{4,3,0,2,1:T(8,128)(2,1)S(1)}, u32[]{:S(2)}, u32[]{:S(2)}) collective-permute-start(bf16[2,2,1,128,256]{4,3,0,2,1:T(8,128)(2,1)S(1)} %get-tuple-element.84), channel_id=1, source_target_pairs={{0,1},{1,2},{2,3},{4,5},{5,6},{6,7},{8,9},{9,10},{10,11},{12,13},{... | collective-permute-start | bytes 786440 | tf_op jit(solution)/shard_map/ppermute | solution.py:334
  26.1 0.7 copy-start.12
  26.1 2.9 %copy-start.14 = (bf16[2,2,1,128,256]{4,3,0,2,1:T(8,128)(2,1)}, bf16[2,2,1,128,256]{4,3,0,2,1:T(8,128)(2,1)S(1)}, u32[]{:S(2)}) copy-start(bf16[2,2,1,128,256]{4,3,0,2,1:T(8,128)(2,1)S(1)} %collective-permute-done.2) | copy-start | bytes 786436
  27.5 8.7 %collective-permute-start.6 = (bf16[4,1,1,128,256]{4,3,0,2,1:T(8,128)(2,1)}, bf16[4,1,1,128,256]{4,3,0,2,1:T(8,128)(2,1)S(1)}, u32[]{:S(2)}, u32[]{:S(2)}) collective-permute-start(bf16[4,1,1,128,256]{4,3,0,2,1:T(8,128)(2,1)} %pad_maximum_fusion.3), channel_id=1, source_target_pairs={{0,4},{4,0},{8,12},{12,8},{16,20},{20,16},{24,28},{28,24},{1,5},{5... | collective-permute-start | bytes 786440 | tf_op jit(solution)/shard_map/ppermute | solution.py:344
  29.9 6.4 %copy-start.10 = (s32[64]{0:T(128)S(1)}, s32[64]{0:T(128)}, u32[]{:S(2)}) copy-start(s32[64]{0:T(128)} %cells.1) | copy-start | bytes 772
  33.9 2.2 %copy-start.15 = (bf16[2,2,1,128,256]{4,3,0,2,1:T(8,128)(2,1)S(1)}, bf16[2,2,1,128,256]{4,3,0,2,1:T(8,128)(2,1)}, u32[]{:S(2)}) copy-start(bf16[2,2,1,128,256]{4,3,0,2,1:T(8,128)(2,1)} %copy-done.14) | copy-start | bytes 786436
  33.9 2.3 %copy-start.13 = (bf16[2,2,1,128,256]{4,3,0,2,1:T(8,128)(2,1)S(1)}, bf16[2,2,1,128,256]{4,3,0,2,1:T(8,128)(2,1)}, u32[]{:S(2)}) copy-start(bf16[2,2,1,128,256]{4,3,0,2,1:T(8,128)(2,1)} %copy-done.12) | copy-start | bytes 786436
  33.9 2.4 %copy-start.3 = (bf16[2,1,4,128,256]{4,3,2,1,0:T(8,128)(2,1)S(1)}, bf16[2,1,4,128,256]{4,3,2,1,0:T(8,128)(2,1)}, u32[]{:S(2)}) copy-start(bf16[2,1,4,128,256]{4,3,2,1,0:T(8,128)(2,1)} %copy-done.2) | copy-start | bytes 1572868
  33.9 2.4 %copy-start.4 = (f32[64,1]{1,0:T(8,128)S(1)}, f32[64,1]{1,0:T(8,128)}, u32[]{:S(2)}) copy-start(f32[64,1]{1,0:T(8,128)} %copy.29.sigma) | copy-start | bytes 772
  33.9 2.4 %copy-start.5 = (f32[64,1]{1,0:T(8,128)S(1)}, f32[64,1]{1,0:T(8,128)}, u32[]{:S(2)}) copy-start(f32[64,1]{1,0:T(8,128)} %copy.30.values) | copy-start | bytes 772
  33.9 2.4 %copy-start.6 = (bf16[256,256]{1,0:T(8,128)(2,1)S(1)}, bf16[256,256]{1,0:T(8,128)(2,1)}, u32[]{:S(2)}) copy-start(bf16[256,256]{1,0:T(8,128)(2,1)} %constant.36.clone.swap_in) | copy-start | bytes 393220
  33.9 2.4 %copy-start.7 = (f32[32,1]{1,0:T(8,128)S(1)}, f32[32,1]{1,0:T(8,128)}, u32[]{:S(2)}) copy-start(f32[32,1]{1,0:T(8,128)} %copy.28.read_column) | copy-start | bytes 388
  36.3 6.9 %copy-start.8 = (bf16[128,128]{1,0:T(8,128)(2,1)S(1)}, bf16[128,128]{1,0:T(8,128)(2,1)}, u32[]{:S(2)}) copy-start(bf16[128,128]{1,0:T(8,128)(2,1)} %constant.37.clone.swap_out) | copy-start | bytes 98308
  36.3 6.9 %copy-start.11 = (f32[32]{0:T(128)S(1)}, f32[32]{0:T(128)}, u32[]{:S(2)}) copy-start(f32[32]{0:T(128)} %get-tuple-element.89.read_half) | copy-start | bytes 388
  39.9 6.4 %collective-permute-start.7 = (bf16[1,80,256]{2,1,0:T(8,128)(2,1)S(1)}, bf16[1,80,256]{2,1,0:T(8,128)(2,1)S(1)}, u32[]{:S(2)}, u32[]{:S(2)}) collective-permute-start(bf16[1,80,256]{2,1,0:T(8,128)(2,1)S(1)} %bitcast.37), channel_id=1, source_target_pairs={{0,2},{1,3},{2,0},{3,1},{4,6},{5,7},{6,4},{7,5},{8,10},{9,11},{10,... | collective-permute-start | bytes 122888 | tf_op jit(solution)/shard_map/ppermute | solution.py:364
  46.3 4.5 %collective-permute-start.8 = (bf16[2,80,256]{2,1,0:T(8,128)(2,1)S(1)}, bf16[2,80,256]{2,1,0:T(8,128)(2,1)S(1)}, u32[]{:S(2)}, u32[]{:S(2)}) collective-permute-start(bf16[2,80,256]{2,1,0:T(8,128)(2,1)S(1)} %pad_maximum_fusion.5), channel_id=1, source_target_pairs={{0,1},{1,0},{2,3},{3,2},{4,5},{5,4},{6,7},{7,6},{8,9},{9,8},{10,11... | collective-permute-start | bytes 245768 | tf_op jit(solution)/shard_map/ppermute | solution.py:364
  50.8 5.4 %collective-permute-start.9 = (bf16[4,80,256]{2,1,0:T(8,128)(2,1)S(1)}, bf16[4,80,256]{2,1,0:T(8,128)(2,1)S(1)}, u32[]{:S(2)}, u32[]{:S(2)}) collective-permute-start(bf16[4,80,256]{2,1,0:T(8,128)(2,1)S(1)} %pad_maximum_fusion.4), channel_id=1, source_target_pairs={{0,8},{4,12},{8,0},{12,4},{16,24},{20,28},{24,16},{28,20},{1,9},{5... | collective-permute-start | bytes 491528 | tf_op jit(solution)/shard_map/ppermute | solution.py:364
  56.2 7.2 %collective-permute-start.10 = (bf16[8,80,256]{2,1,0:T(8,128)(2,1)S(1)}, bf16[8,80,256]{2,1,0:T(8,128)(2,1)S(1)}, u32[]{:S(2)}, u32[]{:S(2)}) collective-permute-start(bf16[8,80,256]{2,1,0:T(8,128)(2,1)S(1)} %pad_maximum_fusion.2), channel_id=1, source_target_pairs={{0,16},{4,20},{8,24},{12,28},{16,0},{20,4},{24,8},{28,12},{1,17},{... | collective-permute-start | bytes 983048 | tf_op jit(solution)/shard_map/ppermute | solution.py:364
  63.5 2.2 %collective-permute-start.11 = (bf16[16,80,256]{2,1,0:T(8,128)(2,1)S(1)}, bf16[16,80,256]{2,1,0:T(8,128)(2,1)S(1)}, u32[]{:S(2)}, u32[]{:S(2)}) collective-permute-start(bf16[16,80,256]{2,1,0:T(8,128)(2,1)S(1)} %pad_maximum_fusion.1), channel_id=1, source_target_pairs={{0,4},{4,0},{8,12},{12,8},{16,20},{20,16},{24,28},{28,24},{1,5},{5... | collective-permute-start | bytes 1966088 | tf_op jit(solution)/shard_map/ppermute | solution.py:364
